TPU v7x, 256 devices: a whole 4x4x8 slice. The times are simulated.
256 devices in a mesh: gx: 4 (over x), gy: 8 (over z), vert: 8 (over y, core).
Axes of the slice: x: 4, y: 4, z: 8, core: 2. Of those that a mesh axis runs over, the one named last changes fastest.
Arguments:
- snapshot: float32 [16, 32, 1024, 1024], P('vert', None, 'gx', 'gy'), may hold values from -6 to 6
- basis_first: float32 [1024, 128], replicated, may hold values from -6 to 6
- basis_second: float32 [1024, 128], P('gy'), may hold values from -0.1875 to 0.1875
- basis_third: float32 [16, 32, 128], P('vert'), may hold values from -0.25 to 0.25
Outputs:
- basis_update: float32 [1024, 128], P('gx')
All inputs are finite; a program needn't handle non-finite values.
Results may differ from a plain program's by a relative error of at most 0.00005.
Values sent between devices are 32-bit elements; how exact they have to be, the bound alone decides.
No kernel may reach another device: no remote copies, remote signals or barrier semaphores. Data moves between devices by JAX's collectives and lax.ppermute only.
A program may use at most 64 MiB of HBM per device.

v0:
```python
import jax
import jax.numpy as jnp
from jax import lax
from jax.sharding import PartitionSpec as P


def local(snapshot, basis_first, basis_second, basis_third):
    depth = snapshot.shape[0] * snapshot.shape[1]
    width_x = snapshot.shape[2]
    width_y = snapshot.shape[3]
    rank = basis_second.shape[1]
    matrix_rows = snapshot.reshape(depth * width_x, width_y)
    third_mode = basis_third.reshape(depth, rank)
    groups = lax.axis_size("gy") * lax.axis_size("vert")
    highest = lax.Precision.HIGHEST
    partial_all = lax.dot_general(
        basis_second,
        matrix_rows,
        (((0,), (1,)), ((), ())),
        precision=highest,
        preferred_element_type=jnp.float32,
    )
    partial_cube = partial_all.reshape(rank, depth, width_x)
    both_modes = jnp.einsum("rkx,kc->rcx", partial_cube, third_mode, precision=highest)
    columns = lax.psum_scatter(
        both_modes.reshape(rank * rank // groups * lax.axis_size(("gy", "vert")), width_x),
        ("gy", "vert"),
        scatter_dimension=0,
        tiled=True,
    )
    gram_rows = lax.dot_general(
        columns,
        lax.all_gather(columns, "gx", axis=1, tiled=True),
        (((0,), (0,)), ((), ())),
        precision=highest,
        preferred_element_type=jnp.float32,
    )
    gram_rows = lax.psum(gram_rows, ("gy", "vert"))
    updated = jnp.dot(gram_rows, basis_first, precision=highest, preferred_element_type=jnp.float32)
    return updated / float(rank * rank)


def solution(mesh):
    placed = (P("vert", None, "gx", "gy"), P(), P("gy", None), P("vert", None, None))
    return jax.shard_map(
        local, mesh=mesh, in_specs=placed, out_specs=P("gx", None), check_vma=False
    )
```

profile of v0, /device:TPU:1, one launch (start us, length us, event | category | flops | bytes accessed | tf_op | source)
XLA Modules:
  0.0 457.6 jit_solution(14481938930686143439)
XLA Ops:
  6.5 0.0 copy-start
  6.5 0.0 reduce-scatter.2.cloned.1.call-start
  6.5 0.0 copy-start.1
  6.5 10.6 %fusion.2 = f32[128,64,256]{2,0,1:T(8,128)S(1)} fusion(f32[64,256,128]{2,1,0:T(8,128)} %bitcast.17, f32[128,128]{1,0:T(8,128)} %param.6), kind=kOutput, calls=%fused_computation.3 | convolution fusion | flops 3221225472 | bytes 16842752 | tf_op jit(solution)/shard_map/dot_general | solution.py:16
  17.2 0.0 copy-done.1
  17.2 23.6 %fusion = f32[128,256,128]{1,2,0:T(8,128)} fusion(f32[64,128,1]{1,0,2:T(8,128)S(1)} %bitcast.18, f32[128,64,256]{2,0,1:T(8,128)S(1)} %fusion.2), kind=kOutput, calls=%fused_computation | convolution fusion | flops 3221225472 | bytes 25198592 | tf_op jit(solution)/shard_map/rkx,kc->rcx/dot_general | solution.py:24
  40.8 0.0 reduce-scatter.2.cloned.1.call-update
  40.8 0.0 all-gather.2.cloned.1.call-start
  40.8 189.1 %reduce-scatter.2.cloned.1.call-done = f32[256,256]{1,0:T(8,128)} async-done(((f32[16384,256]{1,0:T(8,128)}), f32[256,256]{1,0:T(8,128)}) %reduce-scatter.2.cloned.1.call-update) | async-done | bytes 262160 | tf_op jit(solution)/shard_map/reduce_scatter | solution.py:25
  229.9 0.0 all-gather.2.cloned.1.call-update
  229.9 0.0 all-reduce.2.cloned.1.call-start
  230.0 29.9 %all-gather.2.cloned.1.call-done = f32[256,1024]{1,0:T(8,128)} async-done(((f32[256,256]{1,0:T(8,128)}), f32[256,1024]{1,0:T(8,128)}) %all-gather.2.cloned.1.call-update) | async-done | bytes 1048592 | tf_op jit(solution)/shard_map/all_gather | solution.py:33
  259.9 3.3 fusion.4
  263.2 0.0 all-reduce.2.cloned.1.call-update
  263.2 185.0 %all-reduce.2.cloned.1.call-done = f32[256,1024]{1,0:T(8,128)} async-done(((f32[256,1024]{1,0:T(8,128)}), f32[256,1024]{1,0:T(8,128)}) %all-reduce.2.cloned.1.call-update) | async-done | bytes 1048592 | tf_op jit(solution)/shard_map/psum | solution.py:38
  448.2 0.0 copy-done
  448.2 2.9 convolution_multiply_fusion
Async XLA Ops:
  6.5 441.7 %copy-start = (f32[1024,128]{1,0:T(8,128)S(1)}, f32[1024,128]{1,0:T(8,128)}, u32[]{:S(2)}) copy-start(f32[1024,128]{1,0:T(8,128)} %param.5) | copy-start | bytes 1572868
  6.5 223.4 %reduce-scatter.2.cloned.1.call-start = ((), (), s32[]{:S(2)}) async-start(), calls=%async_computation.1 | async-start | bytes 17039360 | tf_op jit(solution)/shard_map/reduce_scatter | solution.py:25
  6.5 10.6 %copy-start.1 = (f32[2,32,128]{2,1,0:T(8,128)S(1)}, f32[2,32,128]{2,1,0:T(8,128)}, u32[]{:S(2)}) copy-start(f32[2,32,128]{2,1,0:T(8,128)} %param.7) | copy-start | bytes 98308
  40.8 219.1 %all-gather.2.cloned.1.call-start = ((), (), s32[]{:S(2)}) async-start(), calls=%async_computation.2 | async-start | bytes 1310720 | tf_op jit(solution)/shard_map/all_gather | solution.py:33
  229.9 218.3 %all-reduce.2.cloned.1.call-start = ((), (), s32[]{:S(2)}) async-start(), calls=%async_computation.3 | async-start | bytes 2097152 | tf_op jit(solution)/shard_map/psum | solution.py:38
Sparse Core Ops, SparseCore 0:
  40.9 188.9 reduce-scatter.1
  231.7 28.0 all-gather.1
  263.3 184.8 all-reduce.1
where the time goes:
time: 458 us
  waiting for transfers between devices  404 us (88%)
  matrix products  40.4 us (9%)
  between operations  13.1 us (3%)
    reduce_scatter x1, waiting for transfers between devices, local(): lax.psum_scatter(both_modes.reshape(rank * rank // groups * lax.axis_size...  189 us
    psum x1, waiting for transfers between devices, local(): gram_rows = lax.psum(gram_rows, ('gy', 'vert'))  185 us
    all_gather x1, waiting for transfers between devices, local(): lax.all_gather(columns, 'gx', axis=1, tiled=True)  29.9 us
    dot_general x1, matrix products, local(): jnp.einsum('rkx,kc->rcx', partial_cube, third_mode, precision=highest)  23.6 us
    dot_general x1, matrix products, local(): lax.dot_general(basis_second, matrix_rows, (((0,), (1,)), ((), ())), prec...  10.6 us
  transfers between devices with their start and end apart: 3, of which 3 were waited for; matrix products, arithmetic and copies ran while one was open for 0% of the time, Pallas kernels for 0%

commit v1 on v0

v1 whole, which is shorter than its diff:
```python
import functools

import jax
import jax.numpy as jnp
from jax import lax
from jax.experimental import pallas as pl
from jax.experimental.pallas import tpu as pltpu
from jax.sharding import PartitionSpec as P

HIGHEST = lax.Precision.HIGHEST
NT = (((1,), (1,)), ((), ()))
NN = (((1,), (0,)), ((), ()))
VMEM_LIMIT = 24 * 2**20
STEP = 8


def split(value):
    high = value.astype(jnp.bfloat16)
    return high, (value - high.astype(jnp.float32)).astype(jnp.bfloat16)


def product(high, both, value, dims):
    rows = high.shape[0]
    v_high, v_low = split(value)
    main = lax.dot_general(both, v_high, dims, preferred_element_type=jnp.float32)
    rest = lax.dot_general(high, v_low, dims, preferred_element_type=jnp.float32)
    return main[:rows] + (main[rows:] + rest)


def mode_kernel(second_ref, field_ref, out_ref):
    high, low = split(second_ref[...])
    both = jnp.concatenate([high, low], 0)
    for j in range(field_ref.shape[0]):
        out_ref[:, j, :] = product(high, both, field_ref[j], NT)


def mode_third_kernel(steps, second_ref, field_ref, third_ref, out_ref):
    @pl.when(pl.program_id(0) < steps)
    def _():
        mode_kernel(second_ref, field_ref, out_ref)

    @pl.when(pl.program_id(0) == steps)
    def _():
        rank = third_ref.shape[1]
        groups = third_ref.shape[0] // STEP
        for r in range(out_ref.shape[0]):
            g = r % groups
            out_ref[r, :, :rank] = third_ref[g * STEP : (g + 1) * STEP, :]


def mode_product(second, field, start, count, third=None):
    _, nx, ny = field.shape
    rows = second.shape[0]
    steps = count // STEP
    first = start // STEP
    kernel, extra, operands = mode_kernel, 0, (second, field)
    in_specs = [
        pl.BlockSpec((rows, ny), lambda i: (0, 0)),
        pl.BlockSpec((STEP, nx, ny), lambda i: (first + jnp.minimum(i, steps - 1), 0, 0)),
    ]
    if third is not None:
        kernel, extra, operands = functools.partial(mode_third_kernel, steps), 1, (second, field, third)
        in_specs.append(pl.BlockSpec(third.shape, lambda i: (0, 0)))
    return pl.pallas_call(
        kernel,
        grid=(steps + extra,),
        in_specs=in_specs,
        out_specs=pl.BlockSpec((rows, STEP, nx), lambda i: (0, i, 0)),
        out_shape=jax.ShapeDtypeStruct((rows, count + extra * STEP, nx), jnp.float32),
        compiler_params=pltpu.CompilerParams(vmem_limit_bytes=VMEM_LIMIT),
        cost_estimate=pl.CostEstimate(
            flops=6 * count * nx * ny * rows,
            bytes_accessed=4 * count * nx * (ny + rows),
            transcendentals=0,
        ),
    )(*operands)


def depth_kernel(third_ref, part_ref, out_ref):
    high, low = split(third_ref[...])
    both = jnp.concatenate([high, low], 0)
    n, _, depth, nx = part_ref.shape
    out_ref[0] = product(high, both, part_ref[...].reshape(n * depth, nx), NN)


def depth_product(third, part, depth):
    n, groups, _, nx = part.shape
    rank = third.shape[0]
    return pl.pallas_call(
        depth_kernel,
        grid=(groups,),
        in_specs=[
            pl.BlockSpec((rank, n * depth), lambda i: (0, 0)),
            pl.BlockSpec((n, 1, depth, nx), lambda i: (0, i, 0, 0)),
        ],
        out_specs=pl.BlockSpec((1, rank, nx), lambda i: (i, 0, 0)),
        out_shape=jax.ShapeDtypeStruct((groups, rank, nx), jnp.float32),
        compiler_params=pltpu.CompilerParams(vmem_limit_bytes=VMEM_LIMIT),
        cost_estimate=pl.CostEstimate(
            flops=6 * part.size * rank,
            bytes_accessed=4 * part.size,
            transcendentals=0,
        ),
    )(third, part)


def shifts(moves, axis):
    n = lax.axis_size(axis)
    values = lax.optimization_barrier([value for value, _ in moves])
    return [
        lax.ppermute(value, axis, [(i, (i + by) % n) for i in range(n)])
        for value, (_, by) in zip(values, moves)
    ]


def ring_sum(parts, axis):
    n = len(parts)
    half = n // 2
    mid = parts[half].shape[0] // 2
    up, down = shifts([(parts[half][:mid], 1), (parts[half][mid:], -1)], axis)
    for d in range(half - 1, 0, -1):
        if d == half - 1:
            up = jnp.concatenate([parts[d][:mid] + up, parts[d][mid:]], 0)
            down = jnp.concatenate([parts[n - d][:mid], parts[n - d][mid:] + down], 0)
        else:
            up = parts[d] + up
            down = parts[n - d] + down
        up, down = shifts([(up, 1), (down, -1)], axis)
    return parts[0] + up + down


def trade(value, axis):
    return lax.all_to_all(value, axis, 0, 0)


def spread(value, axis):
    n = lax.axis_size(axis)
    return trade(jnp.broadcast_to(value[None], (n,) + value.shape), axis)


def local(snapshot, basis_first, basis_second, basis_third):
    depth = snapshot.shape[0] * snapshot.shape[1]
    nx = snapshot.shape[2]
    ny = snapshot.shape[3]
    rank = basis_second.shape[1]
    gx = lax.axis_size("gx")
    gy = lax.axis_size("gy")
    vert = lax.axis_size("vert")
    share = rank // gy
    part_m = share // 2
    field = snapshot.reshape(depth, nx, ny)
    first = lax.dynamic_slice_in_dim(basis_first, lax.axis_index("gx") * nx, nx, 0)

    place = jnp.arange(rank // 2)
    ring = lax.axis_index("gy")
    order_m = (place // part_m + ring) % gy * share + place % part_m
    order_f = (place % gy + ring) % gy * share + part_m + place // gy

    def rows(order):
        turn = (order[:, None] == jnp.arange(rank)[None, :]).astype(jnp.float32)
        return lax.dot_general(turn, basis_second, NT, precision=HIGHEST)

    f = mode_product(rows(order_f), field, 0, depth, basis_third.reshape(depth, rank))
    f, rows_m = lax.optimization_barrier((f, rows(order_m)))
    f = trade(f.reshape(vert, gy, depth + STEP, nx), "vert")

    half = depth // 2
    m = []
    for start in (0, half):
        part = mode_product(rows_m, field, start, half).reshape(gy, part_m, half, nx)
        m.append(ring_sum([part[d] for d in range(gy)], "gy"))
    m, f = lax.optimization_barrier((jnp.concatenate(m, 1), f))
    m = trade(m, "vert")

    third = f[:, :, depth:, :rank].reshape(vert * depth, rank).T
    f = depth_product(third, f, depth)
    f = ring_sum([f[d] for d in range(gy)], "gy")
    f, m = lax.optimization_barrier((f, m))
    m = depth_product(third, m.reshape(vert, 1, depth, nx), depth)[0]

    columns = jnp.concatenate([f, m], 0)
    weights = jnp.dot(columns, first, precision=HIGHEST)
    others = shifts([(weights, d) for d in range(1, gx)], "gx")
    for other in others:
        weights = weights + other
    updated = lax.dot_general(columns, weights, (((0,), (0,)), ((), ())), precision=HIGHEST)

    updated = jnp.sum(trade(updated.reshape(vert, nx // vert, rank), "vert"), axis=0)
    updated = jnp.sum(spread(updated, "gy"), axis=0) / float(rank * rank)
    return spread(updated, "vert").reshape(nx, rank)


def solution(mesh):
    placed = (P("vert", None, "gx", "gy"), P(), P("gy", None), P("vert", None, None))
    return jax.shard_map(
        local, mesh=mesh, in_specs=placed, out_specs=P("gx", None), check_vma=False
    )
```

time: 458 us -> 157 us (0.34)
  waiting for transfers between devices: 404 us -> 36.4 us
  starting transfers between devices: 0.08 us -> 55.5 us
  matrix products: 40.4 us -> 3.18 us
  blocking collectives: 0 us -> 32.6 us
  Pallas kernels: 0 us -> 15.3 us
  between operations: 13.1 us -> 0.35 us
  local copies, waits for them, and re-layouts: 0.01 us -> 11.5 us
    reduce_scatter x1 -> x0, waiting for transfers between devices: 189 us -> none  [local(): lax.psum_scatter(both_modes.reshape(rank * rank // groups * lax.axis_size...]
    psum x1 -> x0, waiting for transfers between devices: 185 us -> none  [local(): gram_rows = lax.psum(gram_rows, ('gy', 'vert'))]
    ppermute x0 -> x27, starting transfers between devices: none -> 40.9 us  [shifts(): lax.ppermute(value, axis, [(i, (i + by) % n) for i in range(n)])]
    dot_general x4, matrix products: 40.4 us -> 3.18 us  [the longest x2 2.2 us: rows(): return lax.dot_general(turn, basis_second, NT, precision=HIGHEST)]
    all_to_all x0 -> x3, blocking collectives: none -> 32.6 us  [trade(): return lax.all_to_all(value, axis, 0, 0)]
    ppermute x0 -> x27, waiting for transfers between devices: none -> 30.3 us  [shifts(): lax.ppermute(value, axis, [(i, (i + by) % n) for i in range(n)])]
    all_gather x1 -> x0, waiting for transfers between devices: 29.9 us -> none  [local(): lax.all_gather(columns, 'gx', axis=1, tiled=True)]
    pallas_call x0 -> x5, Pallas kernels: none -> 15.3 us  [the longest x3 9.23 us: mode_product(): pl.pallas_call(kernel, grid=(steps + extra,), in_specs=in_specs, out_spec...]
  transfers between devices with their start and end apart: 3 -> 29, of which waited for: 3 -> 15; matrix products, arithmetic and copies ran while one was open for 0% -> 1% of each run, Pallas kernels for 0% -> 3%
where the time goes in v1:
time: 157 us; the launch traced here: 156 us
  starting transfers between devices  55.5 us (35%)
  waiting for transfers between devices  36.4 us (23%)
  blocking collectives  32.6 us (21%)
  Pallas kernels  15.3 us (10%)
  local copies, waits for them, and re-layouts  11.5 us (7%)
  matrix products  3.18 us (2%)
  other arithmetic  1.61 us (1%)
    ppermute x27, starting transfers between devices, shifts(): lax.ppermute(value, axis, [(i, (i + by) % n) for i in range(n)])  40.9 us
    all_to_all x3, blocking collectives, trade(): return lax.all_to_all(value, axis, 0, 0)  32.6 us
    ppermute x27, waiting for transfers between devices, shifts(): lax.ppermute(value, axis, [(i, (i + by) % n) for i in range(n)])  30.3 us
    all_to_all x2, starting transfers between devices, trade(): return lax.all_to_all(value, axis, 0, 0)  14.6 us
    unnamed x11, local copies, waits for them, and re-layouts  10.3 us
    pallas_call x3, Pallas kernels, mode_product(): pl.pallas_call(kernel, grid=(steps + extra,), in_specs=in_specs, out_spec...  9.23 us
    all_to_all x2, waiting for transfers between devices, trade(): return lax.all_to_all(value, axis, 0, 0)  6.12 us
    pallas_call x2, Pallas kernels, depth_product(): pl.pallas_call(depth_kernel, grid=(groups,), in_specs=[pl.BlockSpec((rank...  6.04 us
  transfers between devices with their start and end apart: 29, of which 15 were waited for; matrix products, arithmetic and copies ran while one was open for 1% of the time, Pallas kernels for 3%

profile of v1, /device:TPU:1, one launch (start us, length us, event | category | flops | bytes accessed | tf_op | source)
XLA Modules:
  0.0 156.3 jit_solution(2814842070284905923)
XLA Ops:
  2.2 3.4 %copy-done.1 = f32[2,32,256,128]{3,2,1,0:T(8,128)S(1)} copy-done((f32[2,32,256,128]{3,2,1,0:T(8,128)S(1)}, f32[2,32,256,128]{3,2,1,0:T(8,128)}, u32[]{:S(2)}) %copy-start.1) | copy-done | bytes 8388632
  6.4 4.6 %shard_map.46 = f32[64,72,256]{2,1,0:T(8,128)S(1)} custom-call(f32[64,128]{1,0:T(8,128)S(1)} %fusion.16.second_ref, f32[64,256,128]{2,1,0:T(8,128)S(1)} %bitcast.49, f32[64,128]{1,0:T(8,128)S(1)} %bitcast.58), custom_call_target="tpu_custom_call" | custom-call | flops 805306368 | bytes 12582912 | tf_op jit(solution)/shard_map/pallas_call | solution.py:64
  13.2 7.7 %all-to-all-start = ((f32[8,8,72,256]{3,2,1,0:T(8,128)}), f32[8,8,72,256]{3,2,1,0:T(8,128)}, u32[]{:S(2)}, u32[]{:S(2)}) async-start(f32[8,8,72,256]{3,2,1,0:T(8,128)} %bitcast.52), calls=%async_computation | async-start | bytes 9437184 | tf_op jit(solution)/shard_map/all_to_all | solution.py:133
  20.9 3.4 %copy-done.2 = f32[2,32,256,128]{3,2,1,0:T(8,128)S(1)} copy-done((f32[2,32,256,128]{3,2,1,0:T(8,128)S(1)}, f32[2,32,256,128]{3,2,1,0:T(8,128)}, u32[]{:S(2)}) %copy-start.2) | copy-done | bytes 8388632
  24.3 2.3 %shard_map.48 = f32[64,32,256]{2,1,0:T(8,128)S(1)} custom-call(f32[64,128]{1,0:T(8,128)S(1)} %fusion.17.second_ref, f32[64,256,128]{2,1,0:T(8,128)S(1)} %bitcast.50), custom_call_target="tpu_custom_call" | custom-call | flops 402653184 | bytes 6291456 | tf_op jit(solution)/shard_map/pallas_call | solution.py:64
  26.7 3.9 %collective-permute-start.9 = (f32[4,32,256]{2,1,0:T(8,128)S(1)}, f32[4,32,256]{2,1,0:T(8,128)S(1)}, u32[]{:S(2)}, u32[]{:S(2)}) collective-permute-start(f32[4,32,256]{2,1,0:T(8,128)S(1)} %get-tuple-element.48), channel_id=1, source_target_pairs={{0,56},{8,0},{16,8},{24,16},{32,24},{40,32},{48,40},{56,48},{1,57}... | collective-permute-start | bytes 393224 | tf_op jit(solution)/shard_map/ppermute | solution.py:111
  30.6 2.3 %shard_map.47 = f32[64,32,256]{2,1,0:T(8,128)S(1)} custom-call(f32[64,128]{1,0:T(8,128)S(1)} %fusion.17.second_ref, f32[64,256,128]{2,1,0:T(8,128)S(1)} %bitcast.51), custom_call_target="tpu_custom_call" | custom-call | flops 402653184 | bytes 6291456 | tf_op jit(solution)/shard_map/pallas_call | solution.py:64
  33.0 2.7 %collective-permute-start.1 = (f32[4,32,256]{2,1,0:T(8,128)S(1)}, f32[4,32,256]{2,1,0:T(8,128)S(1)}, u32[]{:S(2)}, u32[]{:S(2)}) collective-permute-start(f32[4,32,256]{2,1,0:T(8,128)S(1)} %get-tuple-element.40), channel_id=1, source_target_pairs={{0,56},{8,0},{16,8},{24,16},{32,24},{40,32},{48,40},{56,48},{1,57}... | collective-permute-start | bytes 393224 | tf_op jit(solution)/shard_map/ppermute | solution.py:111
  35.9 2.7 %collective-permute-start.11 = (f32[8,32,256]{2,1,0:T(8,128)S(1)}, f32[8,32,256]{2,1,0:T(8,128)S(1)}, u32[]{:S(2)}, u32[]{:S(2)}) collective-permute-start(f32[8,32,256]{2,1,0:T(8,128)S(1)} %pad_maximum_fusion.4), channel_id=1, source_target_pairs={{0,56},{8,0},{16,8},{24,16},{32,24},{40,32},{48,40},{56,48},{1,57}... | collective-permute-start | bytes 786440 | tf_op jit(solution)/shard_map/ppermute | solution.py:111
  39.1 2.7 %collective-permute-start.3 = (f32[8,32,256]{2,1,0:T(8,128)S(1)}, f32[8,32,256]{2,1,0:T(8,128)S(1)}, u32[]{:S(2)}, u32[]{:S(2)}) collective-permute-start(f32[8,32,256]{2,1,0:T(8,128)S(1)} %pad_maximum_fusion.2), channel_id=1, source_target_pairs={{0,56},{8,0},{16,8},{24,16},{32,24},{40,32},{48,40},{56,48},{1,57}... | collective-permute-start | bytes 786440 | tf_op jit(solution)/shard_map/ppermute | solution.py:111
  41.7 2.3 %collective-permute-done.10 = f32[8,32,256]{2,1,0:T(8,128)S(1)} collective-permute-done((f32[8,32,256]{2,1,0:T(8,128)S(1)}, f32[8,32,256]{2,1,0:T(8,128)S(1)}, u32[]{:S(2)}, u32[]{:S(2)}) %collective-permute-start.10) | collective-permute-done | bytes 262176 | tf_op jit(solution)/shard_map/ppermute | solution.py:111
  44.3 2.6 %collective-permute-start.13 = (f32[8,32,256]{2,1,0:T(8,128)S(1)}, f32[8,32,256]{2,1,0:T(8,128)S(1)}, u32[]{:S(2)}, u32[]{:S(2)}) collective-permute-start(f32[8,32,256]{2,1,0:T(8,128)S(1)} %get-tuple-element.52), channel_id=1, source_target_pairs={{0,56},{8,0},{16,8},{24,16},{32,24},{40,32},{48,40},{56,48},{1,57}... | collective-permute-start | bytes 786440 | tf_op jit(solution)/shard_map/ppermute | solution.py:111
  46.9 2.8 %collective-permute-done.2 = f32[8,32,256]{2,1,0:T(8,128)S(1)} collective-permute-done((f32[8,32,256]{2,1,0:T(8,128)S(1)}, f32[8,32,256]{2,1,0:T(8,128)S(1)}, u32[]{:S(2)}, u32[]{:S(2)}) %collective-permute-start.2) | collective-permute-done | bytes 262176 | tf_op jit(solution)/shard_map/ppermute | solution.py:111
  50.2 2.3 %collective-permute-start.5 = (f32[8,32,256]{2,1,0:T(8,128)S(1)}, f32[8,32,256]{2,1,0:T(8,128)S(1)}, u32[]{:S(2)}, u32[]{:S(2)}) collective-permute-start(f32[8,32,256]{2,1,0:T(8,128)S(1)} %get-tuple-element.44), channel_id=1, source_target_pairs={{0,56},{8,0},{16,8},{24,16},{32,24},{40,32},{48,40},{56,48},{1,57}... | collective-permute-start | bytes 786440 | tf_op jit(solution)/shard_map/ppermute | solution.py:111
  52.5 2.8 %collective-permute-done.12 = f32[8,32,256]{2,1,0:T(8,128)S(1)} collective-permute-done((f32[8,32,256]{2,1,0:T(8,128)S(1)}, f32[8,32,256]{2,1,0:T(8,128)S(1)}, u32[]{:S(2)}, u32[]{:S(2)}) %collective-permute-start.12) | collective-permute-done | bytes 262176 | tf_op jit(solution)/shard_map/ppermute | solution.py:111
  55.6 2.7 %collective-permute-start.15 = (f32[8,32,256]{2,1,0:T(8,128)S(1)}, f32[8,32,256]{2,1,0:T(8,128)S(1)}, u32[]{:S(2)}, u32[]{:S(2)}) collective-permute-start(f32[8,32,256]{2,1,0:T(8,128)S(1)} %get-tuple-element.54), channel_id=1, source_target_pairs={{0,56},{8,0},{16,8},{24,16},{32,24},{40,32},{48,40},{56,48},{1,57}... | collective-permute-start | bytes 786440 | tf_op jit(solution)/shard_map/ppermute | solution.py:111
  58.3 2.6 %collective-permute-done.4 = f32[8,32,256]{2,1,0:T(8,128)S(1)} collective-permute-done((f32[8,32,256]{2,1,0:T(8,128)S(1)}, f32[8,32,256]{2,1,0:T(8,128)S(1)}, u32[]{:S(2)}, u32[]{:S(2)}) %collective-permute-start.4) | collective-permute-done | bytes 262176 | tf_op jit(solution)/shard_map/ppermute | solution.py:111
  61.1 2.7 %collective-permute-start.7 = (f32[8,32,256]{2,1,0:T(8,128)S(1)}, f32[8,32,256]{2,1,0:T(8,128)S(1)}, u32[]{:S(2)}, u32[]{:S(2)}) collective-permute-start(f32[8,32,256]{2,1,0:T(8,128)S(1)} %get-tuple-element.46), channel_id=1, source_target_pairs={{0,56},{8,0},{16,8},{24,16},{32,24},{40,32},{48,40},{56,48},{1,57}... | collective-permute-start | bytes 786440 | tf_op jit(solution)/shard_map/ppermute | solution.py:111
  63.7 2.8 %collective-permute-done.14 = f32[8,32,256]{2,1,0:T(8,128)S(1)} collective-permute-done((f32[8,32,256]{2,1,0:T(8,128)S(1)}, f32[8,32,256]{2,1,0:T(8,128)S(1)}, u32[]{:S(2)}, u32[]{:S(2)}) %collective-permute-start.14) | collective-permute-done | bytes 262176 | tf_op jit(solution)/shard_map/ppermute | solution.py:111
  66.6 5.6 %collective-permute-done.6 = f32[8,32,256]{2,1,0:T(8,128)S(1)} collective-permute-done((f32[8,32,256]{2,1,0:T(8,128)S(1)}, f32[8,32,256]{2,1,0:T(8,128)S(1)}, u32[]{:S(2)}, u32[]{:S(2)}) %collective-permute-start.6) | collective-permute-done | bytes 262176 | tf_op jit(solution)/shard_map/ppermute | solution.py:111
  73.0 2.4 %all-to-all-done.part_ref = f32[8,8,72,256]{3,2,1,0:T(8,128)} async-done(((f32[8,8,72,256]{3,2,1,0:T(8,128)}), f32[8,8,72,256]{3,2,1,0:T(8,128)}, u32[]{:S(2)}, u32[]{:S(2)}) %all-to-all-start) | async-done | bytes 4718624 | tf_op jit(solution)/shard_map/all_to_all | solution.py:133
  76.6 5.8 %shard_map.49 = f32[8,128,256]{2,1,0:T(8,128)S(1)} custom-call(f32[128,512]{1,0:T(8,128)S(1)} %bitcast.53, f32[8,8,72,256]{3,2,1,0:T(8,128)} %all-to-all-done.part_ref), custom_call_target="tpu_custom_call" | custom-call | flops 905969664 | bytes 4718592 | tf_op jit(solution)/shard_map/pallas_call | solution.py:89
  82.4 3.9 %collective-permute-start.17 = (f32[64,256]{1,0:T(8,128)S(1)}, f32[64,256]{1,0:T(8,128)S(1)}, u32[]{:S(2)}, u32[]{:S(2)}) collective-permute-start(f32[64,256]{1,0:T(8,128)S(1)} %get-tuple-element.58), channel_id=1, source_target_pairs={{0,56},{8,0},{16,8},{24,16},{32,24},{40,32},{48,40},{56,48},{1,57}... | collective-permute-start | bytes 196616 | tf_op jit(solution)/shard_map/ppermute | solution.py:111
  88.1 2.8 %collective-permute-start.19 = (f32[128,256]{1,0:T(8,128)S(1)}, f32[128,256]{1,0:T(8,128)S(1)}, u32[]{:S(2)}, u32[]{:S(2)}) collective-permute-start(f32[128,256]{1,0:T(8,128)S(1)} %pad_maximum_fusion.9), channel_id=1, source_target_pairs={{0,56},{8,0},{16,8},{24,16},{32,24},{40,32},{48,40},{56,48},{1,57}... | collective-permute-start | bytes 393224 | tf_op jit(solution)/shard_map/ppermute | solution.py:111
  96.1 6.8 %all-to-all-start.1 = ((f32[8,64,256]{2,1,0:T(8,128)}), f32[8,64,256]{2,1,0:T(8,128)S(1)}, u32[]{:S(2)}, u32[]{:S(2)}) async-start(f32[8,64,256]{2,1,0:T(8,128)} %pad_maximum_fusion), calls=%async_computation.1 | async-start | bytes 1048576 | tf_op jit(solution)/shard_map/all_to_all | solution.py:133
  105.8 2.5 %collective-permute-done.22 = f32[128,256]{1,0:T(8,128)S(1)} collective-permute-done((f32[128,256]{1,0:T(8,128)S(1)}, f32[128,256]{1,0:T(8,128)S(1)}, u32[]{:S(2)}, u32[]{:S(2)}) %collective-permute-start.22) | collective-permute-done | bytes 131104 | tf_op jit(solution)/shard_map/ppermute | solution.py:111
  108.8 3.7 %all-to-all-done.1 = f32[8,64,256]{2,1,0:T(8,128)S(1)} async-done(((f32[8,64,256]{2,1,0:T(8,128)}), f32[8,64,256]{2,1,0:T(8,128)S(1)}, u32[]{:S(2)}, u32[]{:S(2)}) %all-to-all-start.1) | async-done | bytes 524320 | tf_op jit(solution)/shard_map/all_to_all | solution.py:133
  114.5 2.5 %collective-permute-start.25 = (f32[256,128]{1,0:T(8,128)S(1)}, f32[256,128]{1,0:T(8,128)S(1)}, u32[]{:S(2)}, u32[]{:S(2)}) collective-permute-start(f32[256,128]{1,0:T(8,128)S(1)} %fusion.3), channel_id=1, source_target_pairs={{0,128},{64,192},{128,0},{192,64},{1,129},{65,193},{129,1},{193,65... | collective-permute-start | bytes 393224 | tf_op jit(solution)/shard_map/ppermute | solution.py:111
  118.6 3.8 %collective-permute-done.25 = f32[256,128]{1,0:T(8,128)S(1)} collective-permute-done((f32[256,128]{1,0:T(8,128)S(1)}, f32[256,128]{1,0:T(8,128)S(1)}, u32[]{:S(2)}, u32[]{:S(2)}) %collective-permute-start.25) | collective-permute-done | bytes 131104 | tf_op jit(solution)/shard_map/ppermute | solution.py:111
  123.0 9.4 %all_to_all.25 = f32[8,32,128]{2,1,0:T(8,128)S(1)} all-to-all(f32[8,32,128]{2,1,0:T(8,128)S(1)} %bitcast.60), channel_id=1, replica_groups=mesh['gx'=4,'gy'=8,'vert'=8] {'vert'}, dimensions={0} | all-to-all | bytes 262144 | tf_op jit(solution)/shard_map/all_to_all | solution.py:133
  132.5 13.1 %all_to_all.26 = f32[8,32,128]{2,1,0:T(8,128)S(1)} all-to-all(f32[8,32,128]{2,1,0:T(8,128)S(1)} %broadcast_in_dim.4), channel_id=1, replica_groups=mesh['gx'=4,'gy'=8,'vert'=8] {'gy'}, dimensions={0} | all-to-all | bytes 262144 | tf_op jit(solution)/shard_map/all_to_all | solution.py:133
  145.6 10.0 %all_to_all.27 = f32[8,32,128]{2,1,0:T(8,128)S(1)} all-to-all(f32[8,32,128]{2,1,0:T(8,128)S(1)} %broadcast_in_dim.5), channel_id=1, replica_groups=mesh['gx'=4,'gy'=8,'vert'=8] {'vert'}, dimensions={0} | all-to-all | bytes 262144 | tf_op jit(solution)/shard_map/all_to_all | solution.py:133
  (79 shorter events, 24.7 us)
Async XLA Ops:
  0.0 112.8 %copy-start = (f32[1024,128]{1,0:T(8,128)S(1)}, f32[1024,128]{1,0:T(8,128)}, u32[]{:S(2)}) copy-start(f32[1024,128]{1,0:T(8,128)} %param.5) | copy-start | bytes 1572868
  2.2 3.4 %copy-start.1 = (f32[2,32,256,128]{3,2,1,0:T(8,128)S(1)}, f32[2,32,256,128]{3,2,1,0:T(8,128)}, u32[]{:S(2)}) copy-start(f32[2,32,256,128]{3,2,1,0:T(8,128)} %param.4) | copy-start | bytes 25165828
  13.2 62.3 %all-to-all-start = ((f32[8,8,72,256]{3,2,1,0:T(8,128)}), f32[8,8,72,256]{3,2,1,0:T(8,128)}, u32[]{:S(2)}, u32[]{:S(2)}) async-start(f32[8,8,72,256]{3,2,1,0:T(8,128)} %bitcast.52), calls=%async_computation | async-start | bytes 9437184 | tf_op jit(solution)/shard_map/all_to_all | solution.py:133
  20.9 3.4 %copy-start.2 = (f32[2,32,256,128]{3,2,1,0:T(8,128)S(1)}, f32[2,32,256,128]{3,2,1,0:T(8,128)}, u32[]{:S(2)}) copy-start(f32[2,32,256,128]{3,2,1,0:T(8,128)} %param.4) | copy-start | bytes 25165828
  26.6 9.1 %collective-permute-start.8 = (f32[4,32,256]{2,1,0:T(8,128)S(1)}, f32[4,32,256]{2,1,0:T(8,128)S(1)}, u32[]{:S(2)}, u32[]{:S(2)}) collective-permute-start(f32[4,32,256]{2,1,0:T(8,128)S(1)} %get-tuple-element.47), channel_id=1, source_target_pairs={{0,8},{8,16},{16,24},{24,32},{32,40},{40,48},{48,56},{56,0},{1,9},... | collective-permute-start | bytes 393224 | tf_op jit(solution)/shard_map/ppermute | solution.py:111
  26.7 9.0 %collective-permute-start.9 = (f32[4,32,256]{2,1,0:T(8,128)S(1)}, f32[4,32,256]{2,1,0:T(8,128)S(1)}, u32[]{:S(2)}, u32[]{:S(2)}) collective-permute-start(f32[4,32,256]{2,1,0:T(8,128)S(1)} %get-tuple-element.48), channel_id=1, source_target_pairs={{0,56},{8,0},{16,8},{24,16},{32,24},{40,32},{48,40},{56,48},{1,57}... | collective-permute-start | bytes 393224 | tf_op jit(solution)/shard_map/ppermute | solution.py:111
  32.9 5.9 %collective-permute-start = (f32[4,32,256]{2,1,0:T(8,128)S(1)}, f32[4,32,256]{2,1,0:T(8,128)S(1)}, u32[]{:S(2)}, u32[]{:S(2)}) collective-permute-start(f32[4,32,256]{2,1,0:T(8,128)S(1)} %get-tuple-element.39), channel_id=1, source_target_pairs={{0,8},{8,16},{16,24},{24,32},{32,40},{40,48},{48,56},{56,0},{1,9},... | collective-permute-start | bytes 393224 | tf_op jit(solution)/shard_map/ppermute | solution.py:111
  33.0 5.8 %collective-permute-start.1 = (f32[4,32,256]{2,1,0:T(8,128)S(1)}, f32[4,32,256]{2,1,0:T(8,128)S(1)}, u32[]{:S(2)}, u32[]{:S(2)}) collective-permute-start(f32[4,32,256]{2,1,0:T(8,128)S(1)} %get-tuple-element.40), channel_id=1, source_target_pairs={{0,56},{8,0},{16,8},{24,16},{32,24},{40,32},{48,40},{56,48},{1,57}... | collective-permute-start | bytes 393224 | tf_op jit(solution)/shard_map/ppermute | solution.py:111
  35.8 8.2 %collective-permute-start.10 = (f32[8,32,256]{2,1,0:T(8,128)S(1)}, f32[8,32,256]{2,1,0:T(8,128)S(1)}, u32[]{:S(2)}, u32[]{:S(2)}) collective-permute-start(f32[8,32,256]{2,1,0:T(8,128)S(1)} %pad_maximum_fusion.3), channel_id=1, source_target_pairs={{0,8},{8,16},{16,24},{24,32},{32,40},{40,48},{48,56},{56,0},{1,9},... | collective-permute-start | bytes 786440 | tf_op jit(solution)/shard_map/ppermute | solution.py:111
  35.9 8.1 %collective-permute-start.11 = (f32[8,32,256]{2,1,0:T(8,128)S(1)}, f32[8,32,256]{2,1,0:T(8,128)S(1)}, u32[]{:S(2)}, u32[]{:S(2)}) collective-permute-start(f32[8,32,256]{2,1,0:T(8,128)S(1)} %pad_maximum_fusion.4), channel_id=1, source_target_pairs={{0,56},{8,0},{16,8},{24,16},{32,24},{40,32},{48,40},{56,48},{1,57}... | collective-permute-start | bytes 786440 | tf_op jit(solution)/shard_map/ppermute | solution.py:111
  39.0 10.7 %collective-permute-start.2 = (f32[8,32,256]{2,1,0:T(8,128)S(1)}, f32[8,32,256]{2,1,0:T(8,128)S(1)}, u32[]{:S(2)}, u32[]{:S(2)}) collective-permute-start(f32[8,32,256]{2,1,0:T(8,128)S(1)} %pad_maximum_fusion.1), channel_id=1, source_target_pairs={{0,8},{8,16},{16,24},{24,32},{32,40},{40,48},{48,56},{56,0},{1,9},... | collective-permute-start | bytes 786440 | tf_op jit(solution)/shard_map/ppermute | solution.py:111
  39.1 10.6 %collective-permute-start.3 = (f32[8,32,256]{2,1,0:T(8,128)S(1)}, f32[8,32,256]{2,1,0:T(8,128)S(1)}, u32[]{:S(2)}, u32[]{:S(2)}) collective-permute-start(f32[8,32,256]{2,1,0:T(8,128)S(1)} %pad_maximum_fusion.2), channel_id=1, source_target_pairs={{0,56},{8,0},{16,8},{24,16},{32,24},{40,32},{48,40},{56,48},{1,57}... | collective-permute-start | bytes 786440 | tf_op jit(solution)/shard_map/ppermute | solution.py:111
  44.1 11.2 %collective-permute-start.12 = (f32[8,32,256]{2,1,0:T(8,128)S(1)}, f32[8,32,256]{2,1,0:T(8,128)S(1)}, u32[]{:S(2)}, u32[]{:S(2)}) collective-permute-start(f32[8,32,256]{2,1,0:T(8,128)S(1)} %get-tuple-element.51), channel_id=1, source_target_pairs={{0,8},{8,16},{16,24},{24,32},{32,40},{40,48},{48,56},{56,0},{1,9},... | collective-permute-start | bytes 786440 | tf_op jit(solution)/shard_map/ppermute | solution.py:111
  44.3 11.0 %collective-permute-start.13 = (f32[8,32,256]{2,1,0:T(8,128)S(1)}, f32[8,32,256]{2,1,0:T(8,128)S(1)}, u32[]{:S(2)}, u32[]{:S(2)}) collective-permute-start(f32[8,32,256]{2,1,0:T(8,128)S(1)} %get-tuple-element.52), channel_id=1, source_target_pairs={{0,56},{8,0},{16,8},{24,16},{32,24},{40,32},{48,40},{56,48},{1,57}... | collective-permute-start | bytes 786440 | tf_op jit(solution)/shard_map/ppermute | solution.py:111
  49.7 11.2 %collective-permute-start.4 = (f32[8,32,256]{2,1,0:T(8,128)S(1)}, f32[8,32,256]{2,1,0:T(8,128)S(1)}, u32[]{:S(2)}, u32[]{:S(2)}) collective-permute-start(f32[8,32,256]{2,1,0:T(8,128)S(1)} %get-tuple-element.43), channel_id=1, source_target_pairs={{0,8},{8,16},{16,24},{24,32},{32,40},{40,48},{48,56},{56,0},{1,9},... | collective-permute-start | bytes 786440 | tf_op jit(solution)/shard_map/ppermute | solution.py:111
  50.2 10.7 %collective-permute-start.5 = (f32[8,32,256]{2,1,0:T(8,128)S(1)}, f32[8,32,256]{2,1,0:T(8,128)S(1)}, u32[]{:S(2)}, u32[]{:S(2)}) collective-permute-start(f32[8,32,256]{2,1,0:T(8,128)S(1)} %get-tuple-element.44), channel_id=1, source_target_pairs={{0,56},{8,0},{16,8},{24,16},{32,24},{40,32},{48,40},{56,48},{1,57}... | collective-permute-start | bytes 786440 | tf_op jit(solution)/shard_map/ppermute | solution.py:111
  55.3 11.2 %collective-permute-start.14 = (f32[8,32,256]{2,1,0:T(8,128)S(1)}, f32[8,32,256]{2,1,0:T(8,128)S(1)}, u32[]{:S(2)}, u32[]{:S(2)}) collective-permute-start(f32[8,32,256]{2,1,0:T(8,128)S(1)} %get-tuple-element.53), channel_id=1, source_target_pairs={{0,8},{8,16},{16,24},{24,32},{32,40},{40,48},{48,56},{56,0},{1,9},... | collective-permute-start | bytes 786440 | tf_op jit(solution)/shard_map/ppermute | solution.py:111
  55.6 10.9 %collective-permute-start.15 = (f32[8,32,256]{2,1,0:T(8,128)S(1)}, f32[8,32,256]{2,1,0:T(8,128)S(1)}, u32[]{:S(2)}, u32[]{:S(2)}) collective-permute-start(f32[8,32,256]{2,1,0:T(8,128)S(1)} %get-tuple-element.54), channel_id=1, source_target_pairs={{0,56},{8,0},{16,8},{24,16},{32,24},{40,32},{48,40},{56,48},{1,57}... | collective-permute-start | bytes 786440 | tf_op jit(solution)/shard_map/ppermute | solution.py:111
  61.0 11.2 %collective-permute-start.6 = (f32[8,32,256]{2,1,0:T(8,128)S(1)}, f32[8,32,256]{2,1,0:T(8,128)S(1)}, u32[]{:S(2)}, u32[]{:S(2)}) collective-permute-start(f32[8,32,256]{2,1,0:T(8,128)S(1)} %get-tuple-element.45), channel_id=1, source_target_pairs={{0,8},{8,16},{16,24},{24,32},{32,40},{40,48},{48,56},{56,0},{1,9},... | collective-permute-start | bytes 786440 | tf_op jit(solution)/shard_map/ppermute | solution.py:111
  61.1 11.1 %collective-permute-start.7 = (f32[8,32,256]{2,1,0:T(8,128)S(1)}, f32[8,32,256]{2,1,0:T(8,128)S(1)}, u32[]{:S(2)}, u32[]{:S(2)}) collective-permute-start(f32[8,32,256]{2,1,0:T(8,128)S(1)} %get-tuple-element.46), channel_id=1, source_target_pairs={{0,56},{8,0},{16,8},{24,16},{32,24},{40,32},{48,40},{56,48},{1,57}... | collective-permute-start | bytes 786440 | tf_op jit(solution)/shard_map/ppermute | solution.py:111
  82.4 5.6 %collective-permute-start.16 = (f32[64,256]{1,0:T(8,128)S(1)}, f32[64,256]{1,0:T(8,128)S(1)}, u32[]{:S(2)}, u32[]{:S(2)}) collective-permute-start(f32[64,256]{1,0:T(8,128)S(1)} %get-tuple-element.57), channel_id=1, source_target_pairs={{0,8},{8,16},{16,24},{24,32},{32,40},{40,48},{48,56},{56,0},{1,9},... | collective-permute-start | bytes 196616 | tf_op jit(solution)/shard_map/ppermute | solution.py:111
  82.4 5.5 %collective-permute-start.17 = (f32[64,256]{1,0:T(8,128)S(1)}, f32[64,256]{1,0:T(8,128)S(1)}, u32[]{:S(2)}, u32[]{:S(2)}) collective-permute-start(f32[64,256]{1,0:T(8,128)S(1)} %get-tuple-element.58), channel_id=1, source_target_pairs={{0,56},{8,0},{16,8},{24,16},{32,24},{40,32},{48,40},{56,48},{1,57}... | collective-permute-start | bytes 196616 | tf_op jit(solution)/shard_map/ppermute | solution.py:111
  88.0 5.2 %collective-permute-start.18 = (f32[128,256]{1,0:T(8,128)S(1)}, f32[128,256]{1,0:T(8,128)S(1)}, u32[]{:S(2)}, u32[]{:S(2)}) collective-permute-start(f32[128,256]{1,0:T(8,128)S(1)} %pad_maximum_fusion.8), channel_id=1, source_target_pairs={{0,8},{8,16},{16,24},{24,32},{32,40},{40,48},{48,56},{56,0},{1,9},... | collective-permute-start | bytes 393224 | tf_op jit(solution)/shard_map/ppermute | solution.py:111
  88.1 5.1 %collective-permute-start.19 = (f32[128,256]{1,0:T(8,128)S(1)}, f32[128,256]{1,0:T(8,128)S(1)}, u32[]{:S(2)}, u32[]{:S(2)}) collective-permute-start(f32[128,256]{1,0:T(8,128)S(1)} %pad_maximum_fusion.9), channel_id=1, source_target_pairs={{0,56},{8,0},{16,8},{24,16},{32,24},{40,32},{48,40},{56,48},{1,57}... | collective-permute-start | bytes 393224 | tf_op jit(solution)/shard_map/ppermute | solution.py:111
  93.2 9.8 %collective-permute-start.20 = (f32[128,256]{1,0:T(8,128)S(1)}, f32[128,256]{1,0:T(8,128)S(1)}, u32[]{:S(2)}, u32[]{:S(2)}) collective-permute-start(f32[128,256]{1,0:T(8,128)S(1)} %get-tuple-element.61), channel_id=1, source_target_pairs={{0,8},{8,16},{16,24},{24,32},{32,40},{40,48},{48,56},{56,0},{1,9},... | collective-permute-start | bytes 393224 | tf_op jit(solution)/shard_map/ppermute | solution.py:111
  95.4 7.6 %collective-permute-start.21 = (f32[128,256]{1,0:T(8,128)S(1)}, f32[128,256]{1,0:T(8,128)S(1)}, u32[]{:S(2)}, u32[]{:S(2)}) collective-permute-start(f32[128,256]{1,0:T(8,128)S(1)} %get-tuple-element.62), channel_id=1, source_target_pairs={{0,56},{8,0},{16,8},{24,16},{32,24},{40,32},{48,40},{56,48},{1,57}... | collective-permute-start | bytes 393224 | tf_op jit(solution)/shard_map/ppermute | solution.py:111
  96.1 16.3 %all-to-all-start.1 = ((f32[8,64,256]{2,1,0:T(8,128)}), f32[8,64,256]{2,1,0:T(8,128)S(1)}, u32[]{:S(2)}, u32[]{:S(2)}) async-start(f32[8,64,256]{2,1,0:T(8,128)} %pad_maximum_fusion), calls=%async_computation.1 | async-start | bytes 1048576 | tf_op jit(solution)/shard_map/all_to_all | solution.py:133
  103.0 5.2 %collective-permute-start.22 = (f32[128,256]{1,0:T(8,128)S(1)}, f32[128,256]{1,0:T(8,128)S(1)}, u32[]{:S(2)}, u32[]{:S(2)}) collective-permute-start(f32[128,256]{1,0:T(8,128)S(1)} %get-tuple-element.63), channel_id=1, source_target_pairs={{0,8},{8,16},{16,24},{24,32},{32,40},{40,48},{48,56},{56,0},{1,9},... | collective-permute-start | bytes 393224 | tf_op jit(solution)/shard_map/ppermute | solution.py:111
  104.4 4.4 %collective-permute-start.23 = (f32[128,256]{1,0:T(8,128)S(1)}, f32[128,256]{1,0:T(8,128)S(1)}, u32[]{:S(2)}, u32[]{:S(2)}) collective-permute-start(f32[128,256]{1,0:T(8,128)S(1)} %get-tuple-element.64), channel_id=1, source_target_pairs={{0,56},{8,0},{16,8},{24,16},{32,24},{40,32},{48,40},{56,48},{1,57}... | collective-permute-start | bytes 393224 | tf_op jit(solution)/shard_map/ppermute | solution.py:111
  113.2 5.4 %collective-permute-start.24 = (f32[256,128]{1,0:T(8,128)S(1)}, f32[256,128]{1,0:T(8,128)S(1)}, u32[]{:S(2)}, u32[]{:S(2)}) collective-permute-start(f32[256,128]{1,0:T(8,128)S(1)} %fusion.3), channel_id=1, source_target_pairs={{0,64},{64,128},{128,192},{192,0},{1,65},{65,129},{129,193},{193,1... | collective-permute-start | bytes 393224 | tf_op jit(solution)/shard_map/ppermute | solution.py:111
  114.5 7.9 %collective-permute-start.25 = (f32[256,128]{1,0:T(8,128)S(1)}, f32[256,128]{1,0:T(8,128)S(1)}, u32[]{:S(2)}, u32[]{:S(2)}) collective-permute-start(f32[256,128]{1,0:T(8,128)S(1)} %fusion.3), channel_id=1, source_target_pairs={{0,128},{64,192},{128,0},{192,64},{1,129},{65,193},{129,1},{193,65... | collective-permute-start | bytes 393224 | tf_op jit(solution)/shard_map/ppermute | solution.py:111
  116.9 5.5 %collective-permute-start.26 = (f32[256,128]{1,0:T(8,128)S(1)}, f32[256,128]{1,0:T(8,128)S(1)}, u32[]{:S(2)}, u32[]{:S(2)}) collective-permute-start(f32[256,128]{1,0:T(8,128)S(1)} %fusion.3), channel_id=1, source_target_pairs={{0,192},{64,0},{128,64},{192,128},{1,193},{65,1},{129,65},{193,129... | collective-permute-start | bytes 393224 | tf_op jit(solution)/shard_map/ppermute | solution.py:111
  (2 other events, 2.9 us)

commit v2 on v1

v2 whole, which is shorter than its diff:
```python
import functools

import jax
import jax.numpy as jnp
import numpy as np
from jax import lax
from jax.experimental import pallas as pl
from jax.experimental.pallas import tpu as pltpu
from jax.sharding import PartitionSpec as P

HIGHEST = lax.Precision.HIGHEST
NT = (((1,), (1,)), ((), ()))
NN = (((1,), (0,)), ((), ()))
VMEM_LIMIT = 20 * 2**20
STEP = 8
SETS = 8
LANES = 4


def split(value):
    high = value.astype(jnp.bfloat16)
    return high, (value - high.astype(jnp.float32)).astype(jnp.bfloat16)


def product(high, both, value):
    rows = high.shape[0]
    v_high, v_low = split(value)
    main = lax.dot_general(both, v_high, NN, preferred_element_type=jnp.float32)
    rest = lax.dot_general(high, v_low, NN, preferred_element_type=jnp.float32)
    return main[:rows] + (main[rows:] + rest)


def mode_kernel(shapes, rolled, share, pick_ref, second_ref, third_ref, *refs):
    field_refs, refs = refs[:LANES], refs[LANES:]
    *out_refs, both_ref = refs
    rows, rank = pick_ref.shape
    ny = second_ref.shape[0]
    steps = pl.num_programs(0) - 1

    @pl.when(pl.program_id(0) == 0)
    def _():
        turned = pltpu.roll(pick_ref[:rolled, :], lax.axis_index("gy") * share, 1)
        pick = jnp.concatenate([turned, pick_ref[rolled:, :]], 0).astype(jnp.bfloat16)
        for part, value in enumerate(split(second_ref[...])):
            value = lax.dot_general(pick, value, NT, preferred_element_type=jnp.float32)
            both_ref[part * rows : (part + 1) * rows, :ny] = value.astype(jnp.bfloat16)
        both_ref[:rows, ny:] = both_ref[:rows, :ny]
        both_ref[rows:, ny:] = jnp.zeros((rows, ny), jnp.bfloat16)

    @pl.when(pl.program_id(0) < steps)
    def _():
        both = both_ref[...]
        for j in range(STEP):
            each = STEP // LANES
            pair = jnp.concatenate(split(field_refs[j // each][j % each]), 1)
            value = lax.dot_general(both, pair, NT, preferred_element_type=jnp.float32)
            value = value[:rows] + value[rows:]
            start = 0
            for (size, _), out_ref in zip(shapes, out_refs):
                out_ref[:, j, :] = value[start : start + size]
                start += size

    @pl.when(pl.program_id(0) == steps)
    def _():
        out_ref = out_refs[0]
        lanes = out_ref.shape[2] // rank
        tiles = third_ref.shape[0] // STEP
        groups = out_ref.shape[0] // SETS
        for r in range(out_ref.shape[0]):
            for lane in range(lanes):
                g = min(r % groups * lanes + lane, tiles - 1)
                out_ref[r, :, lane * rank : (lane + 1) * rank] = third_ref[g * STEP : (g + 1) * STEP, :]


def mode_product(picks, rolled, second, field, third, share):
    depth, nx, ny = field.shape
    steps = depth // STEP
    pick = np.concatenate(picks, 0)
    shapes = [(p.shape[0], depth) for p in picks]
    shapes[0] = (shapes[0][0], depth + STEP)
    rows, rank = pick.shape

    def last(i):
        return jnp.minimum(i, steps - 1)

    def piece(lane):
        return pl.BlockSpec((STEP // LANES, nx, ny), lambda i: (last(i) * LANES + lane, 0, 0))

    out_specs = [pl.BlockSpec((size, STEP, nx), lambda i: (0, last(i), 0)) for size, _ in shapes]
    out_specs[0] = pl.BlockSpec((shapes[0][0], STEP, nx), lambda i: (0, i, 0))
    return pl.pallas_call(
        functools.partial(mode_kernel, shapes, rolled, share),
        grid=(steps + 1,),
        in_specs=[
            pl.BlockSpec((rows, rank), lambda i: (0, 0)),
            pl.BlockSpec(second.shape, lambda i: (0, 0)),
            pl.BlockSpec(third.shape, lambda i: (0, 0)),
        ]
        + [piece(lane) for lane in range(LANES)],
        out_specs=out_specs,
        out_shape=[jax.ShapeDtypeStruct((*shape, nx), jnp.float32) for shape in shapes],
        scratch_shapes=[pltpu.VMEM((2 * rows, 2 * ny), jnp.bfloat16)],
        compiler_params=pltpu.CompilerParams(vmem_limit_bytes=58 * 2**20),
        cost_estimate=pl.CostEstimate(
            flops=6 * depth * nx * ny * rows,
            bytes_accessed=4 * depth * nx * (ny + rows),
            transcendentals=0,
        ),
    )(jnp.asarray(pick), second, third, *[field] * LANES)


def depth_kernel(third_ref, part_ref, out_ref, both_ref):
    rank = third_ref.shape[0]

    @pl.when(pl.program_id(0) == 0)
    def _():
        high, low = split(third_ref[...])
        both_ref[:rank] = high
        both_ref[rank:] = low

    n, groups, depth, nx = part_ref.shape
    for g in range(groups):
        value = part_ref[:, g].reshape(n * depth, nx)
        out_ref[g] = product(both_ref[:rank], both_ref[...], value)


def depth_product(third, part, depth):
    n, groups, _, nx = part.shape
    rank = third.shape[0]
    step = 2 if groups % 2 == 0 else 1
    return pl.pallas_call(
        depth_kernel,
        grid=(groups // step,),
        in_specs=[
            pl.BlockSpec((rank, n * depth), lambda i: (0, 0)),
            pl.BlockSpec((n, step, depth, nx), lambda i: (0, i, 0, 0)),
        ],
        out_specs=pl.BlockSpec((step, rank, nx), lambda i: (i, 0, 0)),
        out_shape=jax.ShapeDtypeStruct((groups, rank, nx), jnp.float32),
        scratch_shapes=[pltpu.VMEM((2 * rank, n * depth), jnp.bfloat16)],
        compiler_params=pltpu.CompilerParams(vmem_limit_bytes=VMEM_LIMIT),
        cost_estimate=pl.CostEstimate(
            flops=6 * n * groups * depth * nx * rank,
            bytes_accessed=4 * n * groups * depth * nx,
            transcendentals=0,
        ),
    )(third, part)


def after(value, other):
    return lax.optimization_barrier((value, other))[0]


def shifts(moves, axis):
    n = lax.axis_size(axis)
    values = lax.optimization_barrier([value for value, _ in moves])
    return [
        lax.ppermute(value, axis, [(i, (i + by) % n) for i in range(n)])
        for value, (_, by) in zip(values, moves)
    ]


def ring_steps(parts, axis, n):
    half = n // 2
    mid = parts[half].shape[0] // 2
    moving = shifts([(parts[half][:mid], 1), (parts[half][mid:], -1)], axis)
    for d in range(half - 1, 0, -1):
        up, down = yield moving
        if d == half - 1:
            up = jnp.concatenate([parts[d][:mid] + up, parts[d][mid:]], 0)
            down = jnp.concatenate([parts[n - d][:mid], parts[n - d][mid:] + down], 0)
        else:
            up = parts[d] + up
            down = parts[n - d] + down
        moving = shifts([(up, 1), (down, -1)], axis)
    up, down = yield moving
    yield parts[0] + up + down


def trade(value, axis):
    return lax.all_to_all(value, axis, 0, 0)


def spread(value, axis):
    n = lax.axis_size(axis)
    return trade(jnp.broadcast_to(value[None], (n,) + value.shape), axis)


def local(snapshot, basis_first, basis_second, basis_third):
    depth = snapshot.shape[0] * snapshot.shape[1]
    nx = snapshot.shape[2]
    ny = snapshot.shape[3]
    rank = basis_second.shape[1]
    gx = lax.axis_size("gx")
    gy = lax.axis_size("gy")
    vert = lax.axis_size("vert")
    share = rank // gy
    part_m = share // 2
    field = snapshot.reshape(depth, nx, ny)
    first = lax.dynamic_slice_in_dim(basis_first, lax.axis_index("gx") * nx, nx, 0)

    third = basis_third.reshape(depth, rank)

    half = gy // 2
    early = [(half + i) % gy for i in range(2 - half, half - 1)]
    late = [-1 % gy, 0, 1]

    def pick(pairs):
        return np.eye(rank, dtype=np.float32)[[place * share + within for place, within in pairs]]

    pick_1 = pick([(place, part_m + v) for v in range(vert) for place in early])
    pick_2 = pick([(place, part_m + v) for v in range(vert) for place in late])
    pick_m = pick([(place, within) for place in range(gy) for within in range(part_m)])

    picks = [pick_1, pick_2, pick_m]
    f1, f2, m = mode_product(picks, rank // 2, basis_second, field, third, share)
    f1 = trade(f1.reshape(vert, len(early), depth + STEP, nx), "vert")
    m = lax.psum_scatter(m, "gy", scatter_dimension=0, tiled=True)

    f1, f2 = lax.optimization_barrier((f1, f2))
    f2 = trade(f2.reshape(vert, len(late), depth, nx), "vert")
    third = f1[:, :, depth:].reshape(vert, len(early), STEP, nx // rank, rank)
    third = jnp.swapaxes(third, 2, 3).reshape(vert, -1, rank)[:, :depth].reshape(vert * depth, rank).T
    f1 = depth_product(third, f1, depth)
    parts = {place: f1[i] for i, place in enumerate(early)}
    ring_f = ring_steps(parts, "gy", gy)
    f = next(ring_f)
    for _ in range(half - 2):
        f = ring_f.send(f)

    f2 = after(f2, f)
    m = trade(after(m, f2), "vert")
    f2 = depth_product(third, f2, depth)
    parts.update({place: f2[i] for i, place in enumerate(late)})
    f = ring_f.send(f)
    m = depth_product(third, after(m, f).reshape(vert, 1, depth, nx), depth)[0]
    f = ring_f.send(f)

    columns = jnp.concatenate([f, m], 0)
    weights = jnp.dot(columns, first, precision=HIGHEST)
    others = shifts([(weights, d) for d in range(1, gx)], "gx")
    for other in others:
        weights = weights + other
    updated = lax.dot_general(columns, weights, (((0,), (0,)), ((), ())), precision=HIGHEST)

    updated = jnp.sum(trade(updated.reshape(vert, nx // vert, rank), "vert"), axis=0)
    updated = jnp.sum(spread(updated, "gy"), axis=0) / float(rank * rank)
    return spread(updated, "vert").reshape(nx, rank)


def solution(mesh):
    placed = (P("vert", None, "gx", "gy"), P(), P("gy", None), P("vert", None, None))
    return jax.shard_map(
        local, mesh=mesh, in_specs=placed, out_specs=P("gx", None), check_vma=False
    )
```

time: 157 us -> 161 us (1.025)
  blocking collectives: 32.6 us -> 74.4 us
  starting transfers between devices: 55.5 us -> 31 us
  waiting for transfers between devices: 36.4 us -> 19.1 us
  between operations: 0.35 us -> 13.5 us
  local copies, waits for them, and re-layouts: 11.5 us -> 5.14 us
  matrix products: 3.18 us -> 0.98 us
    all_to_all x3 -> x4, blocking collectives: 32.6 us -> 74.4 us  [trade(): return lax.all_to_all(value, axis, 0, 0)]
    ppermute x27 -> x11, starting transfers between devices: 40.9 us -> 18.1 us  [shifts(): lax.ppermute(value, axis, [(i, (i + by) % n) for i in range(n)])]
    ppermute x27 -> x11, waiting for transfers between devices: 30.3 us -> 16.3 us  [shifts(): lax.ppermute(value, axis, [(i, (i + by) % n) for i in range(n)])]
    unnamed x11 -> x9, local copies, waits for them, and re-layouts: 10.3 us -> 2.57 us
    all_to_all x2, waiting for transfers between devices: 6.12 us -> 2.79 us  [trade(): return lax.all_to_all(value, axis, 0, 0)]
    dot_general x2 -> x0, matrix products: 2.2 us -> none  [rows(): return lax.dot_general(turn, basis_second, NT, precision=HIGHEST)]
    reshape x1, local copies, waits for them, and re-layouts: 0.13 us -> 1.78 us  [local(): jnp.swapaxes(third, 2, 3).reshape(vert, -1, rank)[:, :depth]]
    pallas_call x5 -> x4, Pallas kernels: 15.3 us -> 15.5 us  [the longest x1 10.7 us: mode_product(): pl.pallas_call(functools.partial(mode_kernel, shapes, rolled, share), gri...]
  transfers between devices with their start and end apart: 29 -> 14, of which waited for: 15 -> 9; matrix products, arithmetic and copies ran while one was open for 1% -> 2% of each run, Pallas kernels for 3% -> 3%
where the time goes in v2:
time: 161 us; the launch traced here: 160 us
  blocking collectives  74.4 us (46%)
  starting transfers between devices  31 us (19%)
  waiting for transfers between devices  19.1 us (12%)
  Pallas kernels  15.5 us (10%)
  between operations  13.5 us (8%)
  local copies, waits for them, and re-layouts  5.14 us (3%)
    all_to_all x4, blocking collectives, trade(): return lax.all_to_all(value, axis, 0, 0)  74.4 us
    ppermute x11, starting transfers between devices, shifts(): lax.ppermute(value, axis, [(i, (i + by) % n) for i in range(n)])  18.1 us
    ppermute x11, waiting for transfers between devices, shifts(): lax.ppermute(value, axis, [(i, (i + by) % n) for i in range(n)])  16.3 us
    all_to_all x2, starting transfers between devices, trade(): return lax.all_to_all(value, axis, 0, 0)  13 us
    pallas_call x1, Pallas kernels, mode_product(): pl.pallas_call(functools.partial(mode_kernel, shapes, rolled, share), gri...  10.7 us
    pallas_call x3, Pallas kernels, depth_product(): pl.pallas_call(depth_kernel, grid=(groups // step,), in_specs=[pl.BlockSp...  4.75 us
  transfers between devices with their start and end apart: 14, of which 9 were waited for; matrix products, arithmetic and copies ran while one was open for 2% of the time, Pallas kernels for 3%

profile of v2, /device:TPU:1, one launch (start us, length us, event | category | flops | bytes accessed | tf_op | source)
XLA Modules:
  0.0 159.8 jit_solution(2979657264320705215)
XLA Ops:
  6.5 10.7 %shard_map.55 = (f32[40,72,256]{2,1,0:T(8,128)}, f32[24,64,256]{2,1,0:T(8,128)}, f32[64,64,256]{2,1,0:T(8,128)}) custom-call(f32[128,128]{1,0:T(8,128)} %constant.19.clone.pick_ref, f32[128,128]{1,0:T(8,128)} %second_ref.1, f32[64,128]{1,0:T(8,128)} %bitcast.69, f32[64,256,128]{2,1,0:T(8,128)} %bitcast.59, f32[64,256,128]{2,1,0:T(8,128)} %bitcast.60, ...), custom_call_target="tpu_custom_call" | custom-call | flops 1610612736 | bytes 16777216 | tf_op jit(solution)/shard_map/pallas_call | solution.py:91
  17.3 42.8 %all_to_all.30.part_ref = f32[8,5,72,256]{3,2,1,0:T(8,128)S(1)} all-to-all(f32[8,5,72,256]{3,2,1,0:T(8,128)} %bitcast.63), channel_id=1, replica_groups=mesh['gx'=4,'gy'=8,'vert'=8] {'vert'}, dimensions={0} | all-to-all | bytes 5898240 | tf_op jit(solution)/shard_map/all_to_all | solution.py:181
  60.1 4.9 %all-to-all-start.1 = ((f32[8,3,64,256]{3,2,1,0:T(8,128)}), f32[8,3,64,256]{3,2,1,0:T(8,128)}, u32[]{:S(2)}, u32[]{:S(2)}) async-start(f32[8,3,64,256]{3,2,1,0:T(8,128)} %bitcast.64), calls=%async_computation.1 | async-start | bytes 3145728 | tf_op jit(solution)/shard_map/all_to_all | solution.py:181
  65.0 0.7 slice.85
  65.8 1.8 %copy.8 = f32[512,128]{0,1:T(8,128)} copy(f32[512,128]{1,0:T(8,128)} %bitcast.66) | data formatting | bytes 524288 | tf_op jit(solution)/shard_map/reshape | solution.py:223
  67.6 1.0 copy-done.1
  68.5 1.7 %shard_map.56 = f32[5,128,256]{2,1,0:T(8,128)S(1)} custom-call(f32[128,512]{1,0:T(8,128)S(1)} %bitcast.53, f32[8,5,72,256]{3,2,1,0:T(8,128)S(1)} %all_to_all.30.part_ref), custom_call_target="tpu_custom_call" | custom-call | flops 503316480 | bytes 2621440 | tf_op jit(solution)/shard_map/pallas_call | solution.py:131
  70.3 0.9 collective-permute-start
  71.2 4.0 %collective-permute-start.1 = (f32[64,256]{1,0:T(8,128)S(1)}, f32[64,256]{1,0:T(8,128)S(1)}, u32[]{:S(2)}, u32[]{:S(2)}) collective-permute-start(f32[64,256]{1,0:T(8,128)S(1)} %get-tuple-element.29), channel_id=1, source_target_pairs={{0,56},{8,0},{16,8},{24,16},{32,24},{40,32},{48,40},{56,48},{1,57}... | collective-permute-start | bytes 196616 | tf_op jit(solution)/shard_map/ppermute | solution.py:158
  75.2 2.4 %collective-permute-done = f32[64,256]{1,0:T(8,128)S(1)} collective-permute-done((f32[64,256]{1,0:T(8,128)S(1)}, f32[64,256]{1,0:T(8,128)S(1)}, u32[]{:S(2)}, u32[]{:S(2)}) %collective-permute-start) | collective-permute-done | bytes 65568 | tf_op jit(solution)/shard_map/ppermute | solution.py:158
  77.7 2.7 %collective-permute-start.3 = (f32[128,256]{1,0:T(8,128)S(1)}, f32[128,256]{1,0:T(8,128)S(1)}, u32[]{:S(2)}, u32[]{:S(2)}) collective-permute-start(f32[128,256]{1,0:T(8,128)S(1)} %get-tuple-element.31), channel_id=1, source_target_pairs={{0,56},{8,0},{16,8},{24,16},{32,24},{40,32},{48,40},{56,48},{1,57}... | collective-permute-start | bytes 393224 | tf_op jit(solution)/shard_map/ppermute | solution.py:158
  80.4 3.1 %collective-permute-done.2 = f32[128,256]{1,0:T(8,128)S(1)} collective-permute-done((f32[128,256]{1,0:T(8,128)S(1)}, f32[128,256]{1,0:T(8,128)S(1)}, u32[]{:S(2)}, u32[]{:S(2)}) %collective-permute-start.2) | collective-permute-done | bytes 131104 | tf_op jit(solution)/shard_map/ppermute | solution.py:158
  83.5 1.5 collective-permute-start.4
  85.1 1.2 collective-permute-start.5
  86.3 2.4 %collective-permute-done.4 = f32[128,256]{1,0:T(8,128)S(1)} collective-permute-done((f32[128,256]{1,0:T(8,128)S(1)}, f32[128,256]{1,0:T(8,128)S(1)}, u32[]{:S(2)}, u32[]{:S(2)}) %collective-permute-start.4) | collective-permute-done | bytes 131104 | tf_op jit(solution)/shard_map/ppermute | solution.py:158
  88.9 0.9 copy-done.2
  89.8 2.7 %shard_map.57 = f32[3,128,256]{2,1,0:T(8,128)S(1)} custom-call(f32[128,512]{1,0:T(8,128)S(1)} %bitcast.54, f32[8,3,64,256]{3,2,1,0:T(8,128)} %all-to-all-done.1.part_ref), custom_call_target="tpu_custom_call" | custom-call | flops 301989888 | bytes 1572864 | tf_op jit(solution)/shard_map/pallas_call | solution.py:131
  92.6 8.0 %all-to-all-start.2 = ((f32[8,64,256]{2,1,0:T(8,128)}), f32[8,64,256]{2,1,0:T(8,128)S(1)}, u32[]{:S(2)}, u32[]{:S(2)}) async-start(f32[8,64,256]{2,1,0:T(8,128)} %reduce-scatter.2.cloned.1.call-done), calls=%async_computation.3 | async-start | bytes 1048576 | tf_op jit(solution)/shard_map/all_to_all | solution.py:181
  100.7 1.8 %collective-permute-start.6 = (f32[128,256]{1,0:T(8,128)S(1)}, f32[128,256]{1,0:T(8,128)S(1)}, u32[]{:S(2)}, u32[]{:S(2)}) collective-permute-start(f32[128,256]{1,0:T(8,128)S(1)} %get-tuple-element.35), channel_id=1, source_target_pairs={{0,8},{8,16},{16,24},{24,32},{32,40},{40,48},{48,56},{56,0},{1,9},... | collective-permute-start | bytes 393224 | tf_op jit(solution)/shard_map/ppermute | solution.py:158
  102.5 0.9 collective-permute-start.7
  103.4 3.7 %collective-permute-done.6 = f32[128,256]{1,0:T(8,128)S(1)} collective-permute-done((f32[128,256]{1,0:T(8,128)S(1)}, f32[128,256]{1,0:T(8,128)S(1)}, u32[]{:S(2)}, u32[]{:S(2)}) %collective-permute-start.6) | collective-permute-done | bytes 131104 | tf_op jit(solution)/shard_map/ppermute | solution.py:158
  107.3 2.8 %all-to-all-done.2 = f32[8,64,256]{2,1,0:T(8,128)S(1)} async-done(((f32[8,64,256]{2,1,0:T(8,128)}), f32[8,64,256]{2,1,0:T(8,128)S(1)}, u32[]{:S(2)}, u32[]{:S(2)}) %all-to-all-start.2) | async-done | bytes 524320 | tf_op jit(solution)/shard_map/all_to_all | solution.py:181
  110.8 1.3 collective-permute-start.8
  112.1 2.5 %collective-permute-start.9 = (f32[256,128]{1,0:T(8,128)S(1)}, f32[256,128]{1,0:T(8,128)S(1)}, u32[]{:S(2)}, u32[]{:S(2)}) collective-permute-start(f32[256,128]{1,0:T(8,128)S(1)} %fusion.1), channel_id=1, source_target_pairs={{0,128},{64,192},{128,0},{192,64},{1,129},{65,193},{129,1},{193,65... | collective-permute-start | bytes 393224 | tf_op jit(solution)/shard_map/ppermute | solution.py:158
  114.5 1.1 collective-permute-start.10
  115.7 0.5 collective-permute-done.8
  116.2 3.8 %collective-permute-done.9 = f32[256,128]{1,0:T(8,128)S(1)} collective-permute-done((f32[256,128]{1,0:T(8,128)S(1)}, f32[256,128]{1,0:T(8,128)S(1)}, u32[]{:S(2)}, u32[]{:S(2)}) %collective-permute-start.9) | collective-permute-done | bytes 131104 | tf_op jit(solution)/shard_map/ppermute | solution.py:158
  120.1 0.6 fusion
  120.7 9.4 %all_to_all.31 = f32[8,32,128]{2,1,0:T(8,128)S(1)} all-to-all(f32[8,32,128]{2,1,0:T(8,128)S(1)} %bitcast.67), channel_id=1, replica_groups=mesh['gx'=4,'gy'=8,'vert'=8] {'vert'}, dimensions={0} | all-to-all | bytes 262144 | tf_op jit(solution)/shard_map/all_to_all | solution.py:181
  130.1 12.1 %all_to_all.32 = f32[8,32,128]{2,1,0:T(8,128)S(1)} all-to-all(f32[8,32,128]{2,1,0:T(8,128)S(1)} %broadcast_in_dim.4), channel_id=1, replica_groups=mesh['gx'=4,'gy'=8,'vert'=8] {'gy'}, dimensions={0} | all-to-all | bytes 262144 | tf_op jit(solution)/shard_map/all_to_all | solution.py:181
  142.3 10.0 %all_to_all.33 = f32[8,32,128]{2,1,0:T(8,128)S(1)} all-to-all(f32[8,32,128]{2,1,0:T(8,128)S(1)} %broadcast_in_dim.5), channel_id=1, replica_groups=mesh['gx'=4,'gy'=8,'vert'=8] {'vert'}, dimensions={0} | all-to-all | bytes 262144 | tf_op jit(solution)/shard_map/all_to_all | solution.py:181
  152.3 0.7 copy.10
  (30 shorter events, 1.5 us)
Async XLA Ops:
  6.5 103.9 %copy-start = (f32[1024,128]{1,0:T(8,128)S(1)}, f32[1024,128]{1,0:T(8,128)}, u32[]{:S(2)}) copy-start(f32[1024,128]{1,0:T(8,128)} %param.6) | copy-start | bytes 1572868
  6.5 86.0 %reduce-scatter.2.cloned.1.call-start = ((), (), s32[]{:S(2)}) async-start(), calls=%async_computation.7 | async-start | bytes 4718592 | tf_op jit(solution)/shard_map/reduce_scatter | solution.py:218
  60.1 28.8 %all-to-all-start.1 = ((f32[8,3,64,256]{3,2,1,0:T(8,128)}), f32[8,3,64,256]{3,2,1,0:T(8,128)}, u32[]{:S(2)}, u32[]{:S(2)}) async-start(f32[8,3,64,256]{3,2,1,0:T(8,128)} %bitcast.64), calls=%async_computation.1 | async-start | bytes 3145728 | tf_op jit(solution)/shard_map/all_to_all | solution.py:181
  67.5 1.0 copy-start.1
  70.3 7.3 %collective-permute-start = (f32[64,256]{1,0:T(8,128)S(1)}, f32[64,256]{1,0:T(8,128)S(1)}, u32[]{:S(2)}, u32[]{:S(2)}) collective-permute-start(f32[64,256]{1,0:T(8,128)S(1)} %get-tuple-element.28), channel_id=1, source_target_pairs={{0,8},{8,16},{16,24},{24,32},{32,40},{40,48},{48,56},{56,0},{1,9},... | collective-permute-start | bytes 196616 | tf_op jit(solution)/shard_map/ppermute | solution.py:158
  71.2 6.4 %collective-permute-start.1 = (f32[64,256]{1,0:T(8,128)S(1)}, f32[64,256]{1,0:T(8,128)S(1)}, u32[]{:S(2)}, u32[]{:S(2)}) collective-permute-start(f32[64,256]{1,0:T(8,128)S(1)} %get-tuple-element.29), channel_id=1, source_target_pairs={{0,56},{8,0},{16,8},{24,16},{32,24},{40,32},{48,40},{56,48},{1,57}... | collective-permute-start | bytes 196616 | tf_op jit(solution)/shard_map/ppermute | solution.py:158
  77.6 32.5 %copy-start.3 = (f32[512,128]{0,1:T(8,128)S(1)}, f32[512,128]{0,1:T(8,128)}, u32[]{:S(2)}) copy-start(f32[512,128]{0,1:T(8,128)} %copy.8) | copy-start | bytes 786436
  77.6 5.8 %collective-permute-start.2 = (f32[128,256]{1,0:T(8,128)S(1)}, f32[128,256]{1,0:T(8,128)S(1)}, u32[]{:S(2)}, u32[]{:S(2)}) collective-permute-start(f32[128,256]{1,0:T(8,128)S(1)} %get-tuple-element.30), channel_id=1, source_target_pairs={{0,8},{8,16},{16,24},{24,32},{32,40},{40,48},{48,56},{56,0},{1,9},... | collective-permute-start | bytes 393224 | tf_op jit(solution)/shard_map/ppermute | solution.py:158
  77.7 5.8 %collective-permute-start.3 = (f32[128,256]{1,0:T(8,128)S(1)}, f32[128,256]{1,0:T(8,128)S(1)}, u32[]{:S(2)}, u32[]{:S(2)}) collective-permute-start(f32[128,256]{1,0:T(8,128)S(1)} %get-tuple-element.31), channel_id=1, source_target_pairs={{0,56},{8,0},{16,8},{24,16},{32,24},{40,32},{48,40},{56,48},{1,57}... | collective-permute-start | bytes 393224 | tf_op jit(solution)/shard_map/ppermute | solution.py:158
  83.5 5.1 %collective-permute-start.4 = (f32[128,256]{1,0:T(8,128)S(1)}, f32[128,256]{1,0:T(8,128)S(1)}, u32[]{:S(2)}, u32[]{:S(2)}) collective-permute-start(f32[128,256]{1,0:T(8,128)S(1)} %get-tuple-element.32), channel_id=1, source_target_pairs={{0,8},{8,16},{16,24},{24,32},{32,40},{40,48},{48,56},{56,0},{1,9},... | collective-permute-start | bytes 393224 | tf_op jit(solution)/shard_map/ppermute | solution.py:158
  85.1 3.8 %collective-permute-start.5 = (f32[128,256]{1,0:T(8,128)S(1)}, f32[128,256]{1,0:T(8,128)S(1)}, u32[]{:S(2)}, u32[]{:S(2)}) collective-permute-start(f32[128,256]{1,0:T(8,128)S(1)} %get-tuple-element.33), channel_id=1, source_target_pairs={{0,56},{8,0},{16,8},{24,16},{32,24},{40,32},{48,40},{56,48},{1,57}... | collective-permute-start | bytes 393224 | tf_op jit(solution)/shard_map/ppermute | solution.py:158
  88.9 1.0 copy-start.2
  92.6 17.5 %all-to-all-start.2 = ((f32[8,64,256]{2,1,0:T(8,128)}), f32[8,64,256]{2,1,0:T(8,128)S(1)}, u32[]{:S(2)}, u32[]{:S(2)}) async-start(f32[8,64,256]{2,1,0:T(8,128)} %reduce-scatter.2.cloned.1.call-done), calls=%async_computation.3 | async-start | bytes 1048576 | tf_op jit(solution)/shard_map/all_to_all | solution.py:181
  100.7 6.4 %collective-permute-start.6 = (f32[128,256]{1,0:T(8,128)S(1)}, f32[128,256]{1,0:T(8,128)S(1)}, u32[]{:S(2)}, u32[]{:S(2)}) collective-permute-start(f32[128,256]{1,0:T(8,128)S(1)} %get-tuple-element.35), channel_id=1, source_target_pairs={{0,8},{8,16},{16,24},{24,32},{32,40},{40,48},{48,56},{56,0},{1,9},... | collective-permute-start | bytes 393224 | tf_op jit(solution)/shard_map/ppermute | solution.py:158
  102.5 4.8 %collective-permute-start.7 = (f32[128,256]{1,0:T(8,128)S(1)}, f32[128,256]{1,0:T(8,128)S(1)}, u32[]{:S(2)}, u32[]{:S(2)}) collective-permute-start(f32[128,256]{1,0:T(8,128)S(1)} %get-tuple-element.36), channel_id=1, source_target_pairs={{0,56},{8,0},{16,8},{24,16},{32,24},{40,32},{48,40},{56,48},{1,57}... | collective-permute-start | bytes 393224 | tf_op jit(solution)/shard_map/ppermute | solution.py:158
  110.8 5.4 %collective-permute-start.8 = (f32[256,128]{1,0:T(8,128)S(1)}, f32[256,128]{1,0:T(8,128)S(1)}, u32[]{:S(2)}, u32[]{:S(2)}) collective-permute-start(f32[256,128]{1,0:T(8,128)S(1)} %fusion.1), channel_id=1, source_target_pairs={{0,64},{64,128},{128,192},{192,0},{1,65},{65,129},{129,193},{193,1... | collective-permute-start | bytes 393224 | tf_op jit(solution)/shard_map/ppermute | solution.py:158
  112.1 7.9 %collective-permute-start.9 = (f32[256,128]{1,0:T(8,128)S(1)}, f32[256,128]{1,0:T(8,128)S(1)}, u32[]{:S(2)}, u32[]{:S(2)}) collective-permute-start(f32[256,128]{1,0:T(8,128)S(1)} %fusion.1), channel_id=1, source_target_pairs={{0,128},{64,192},{128,0},{192,64},{1,129},{65,193},{129,1},{193,65... | collective-permute-start | bytes 393224 | tf_op jit(solution)/shard_map/ppermute | solution.py:158
  114.5 5.5 %collective-permute-start.10 = (f32[256,128]{1,0:T(8,128)S(1)}, f32[256,128]{1,0:T(8,128)S(1)}, u32[]{:S(2)}, u32[]{:S(2)}) collective-permute-start(f32[256,128]{1,0:T(8,128)S(1)} %fusion.1), channel_id=1, source_target_pairs={{0,192},{64,0},{128,64},{192,128},{1,193},{65,1},{129,65},{193,129... | collective-permute-start | bytes 393224 | tf_op jit(solution)/shard_map/ppermute | solution.py:158
Sparse Core Ops, SparseCore 0:
  17.4 59.1 reduce-scatter.1

commit v3 on v1

v3 whole, which is shorter than its diff:
```python
import functools

import jax
import jax.numpy as jnp
import numpy as np
from jax import lax
from jax.experimental import pallas as pl
from jax.experimental.pallas import tpu as pltpu
from jax.sharding import PartitionSpec as P

HIGHEST = lax.Precision.HIGHEST
NT = (((1,), (1,)), ((), ()))
NN = (((1,), (0,)), ((), ()))
VMEM_LIMIT = 20 * 2**20
STEP = 8
SETS = 8


def split(value):
    high = value.astype(jnp.bfloat16)
    return high, (value - high.astype(jnp.float32)).astype(jnp.bfloat16)


def product(high, both, value):
    rows = high.shape[0]
    v_high, v_low = split(value)
    main = lax.dot_general(both, v_high, NN, preferred_element_type=jnp.float32)
    rest = lax.dot_general(high, v_low, NN, preferred_element_type=jnp.float32)
    return main[:rows] + (main[rows:] + rest)


def mode_kernel(roll, first, pick_ref, second_ref, field_ref, third_ref, out_ref, both_ref, held_ref, sems):
    rows, rank = pick_ref.shape
    ny = second_ref.shape[0]
    steps = held_ref.shape[0] // STEP

    def fetch(i):
        return pltpu.make_async_copy(
            field_ref.at[pl.ds((first + i) * STEP, STEP)], held_ref.at[pl.ds(i * STEP, STEP)], sems.at[i]
        )

    @pl.when(pl.program_id(0) == 0)
    def _():
        for i in range(steps):
            fetch(i).start()
        pick = pltpu.roll(pick_ref[...], lax.axis_index("gy") * roll, 1).astype(jnp.bfloat16)
        for part, value in enumerate(split(second_ref[...])):
            value = lax.dot_general(pick, value, NT, preferred_element_type=jnp.float32)
            both_ref[part * rows : (part + 1) * rows, :ny] = value.astype(jnp.bfloat16)
        both_ref[:rows, ny:] = both_ref[:rows, :ny]
        both_ref[rows:, ny:] = jnp.zeros((rows, ny), jnp.bfloat16)

    @pl.when(pl.program_id(0) < steps)
    def _():
        i = pl.program_id(0)
        fetch(i).wait()
        both = both_ref[...]
        for j in range(STEP):
            pair = jnp.concatenate(split(held_ref[i * STEP + j]), 1)
            value = lax.dot_general(both, pair, NT, preferred_element_type=jnp.float32)
            out_ref[:, j, :] = value[:rows] + value[rows:]

    if third_ref is None:
        return

    @pl.when(pl.program_id(0) == steps)
    def _():
        groups = out_ref.shape[0] // SETS
        for r in range(out_ref.shape[0]):
            g = r % groups
            out_ref[r, :, :rank] = third_ref[g * STEP : (g + 1) * STEP, :]
            out_ref[r, :, rank:] = third_ref[g * STEP : (g + 1) * STEP, :]


def plain_kernel(roll, first, pick_ref, second_ref, field_ref, *refs):
    mode_kernel(roll, first, pick_ref, second_ref, field_ref, None, *refs)


def mode_product(pick, second, field, roll, start, count, third=None):
    _, nx, ny = field.shape
    steps = count // STEP
    first = start // STEP
    rows, rank = pick.shape
    extra = 0 if third is None else 1

    in_specs = [
        pl.BlockSpec((rows, rank), lambda i: (0, 0)),
        pl.BlockSpec(second.shape, lambda i: (0, 0)),
        pl.BlockSpec(memory_space=pl.ANY),
    ]
    operands = [jnp.asarray(pick), second, field]
    if extra:
        in_specs.append(pl.BlockSpec(third.shape, lambda i: (0, 0)))
        operands.append(third)
    return pl.pallas_call(
        functools.partial(mode_kernel if extra else plain_kernel, roll, first),
        grid=(steps + extra,),
        in_specs=in_specs,
        out_specs=pl.BlockSpec((rows, STEP, nx), lambda i: (0, i, 0)),
        out_shape=jax.ShapeDtypeStruct((rows, count + extra * STEP, nx), jnp.float32),
        scratch_shapes=[
            pltpu.VMEM((2 * rows, 2 * ny), jnp.bfloat16),
            pltpu.VMEM((count, nx, ny), jnp.float32),
            pltpu.SemaphoreType.DMA((steps,)),
        ],
        compiler_params=pltpu.CompilerParams(vmem_limit_bytes=54 * 2**20),
        cost_estimate=pl.CostEstimate(
            flops=6 * count * nx * ny * rows,
            bytes_accessed=4 * count * nx * (ny + rows),
            transcendentals=0,
        ),
    )(*operands)


def depth_kernel(third_ref, part_ref, out_ref, both_ref):
    rank = third_ref.shape[0]

    @pl.when(pl.program_id(0) == 0)
    def _():
        high, low = split(third_ref[...])
        both_ref[:rank] = high
        both_ref[rank:] = low

    n, groups, depth, nx = part_ref.shape
    for g in range(groups):
        value = part_ref[:, g].reshape(n * depth, nx)
        out_ref[g] = product(both_ref[:rank], both_ref[...], value)


def depth_product(third, part, depth):
    n, groups, _, nx = part.shape
    rank = third.shape[0]
    step = 2 if groups % 2 == 0 else 1
    return pl.pallas_call(
        depth_kernel,
        grid=(groups // step,),
        in_specs=[
            pl.BlockSpec((rank, n * depth), lambda i: (0, 0)),
            pl.BlockSpec((n, step, depth, nx), lambda i: (0, i, 0, 0)),
        ],
        out_specs=pl.BlockSpec((step, rank, nx), lambda i: (i, 0, 0)),
        out_shape=jax.ShapeDtypeStruct((groups, rank, nx), jnp.float32),
        scratch_shapes=[pltpu.VMEM((2 * rank, n * depth), jnp.bfloat16)],
        compiler_params=pltpu.CompilerParams(vmem_limit_bytes=VMEM_LIMIT),
        cost_estimate=pl.CostEstimate(
            flops=6 * n * groups * depth * nx * rank,
            bytes_accessed=4 * n * groups * depth * nx,
            transcendentals=0,
        ),
    )(third, part)


def after(value, other):
    return lax.optimization_barrier((value, other))[0]


def shifts(moves, axis):
    n = lax.axis_size(axis)
    values = lax.optimization_barrier([value for value, _ in moves])
    return [
        lax.ppermute(value, axis, [(i, (i + by) % n) for i in range(n)])
        for value, (_, by) in zip(values, moves)
    ]


def ring_sum(parts, axis):
    n = len(parts)
    half = n // 2
    mid = parts[half].shape[0] // 2
    up, down = shifts([(parts[half][:mid], 1), (parts[half][mid:], -1)], axis)
    for d in range(half - 1, 0, -1):
        if d == half - 1:
            up = jnp.concatenate([parts[d][:mid] + up, parts[d][mid:]], 0)
            down = jnp.concatenate([parts[n - d][:mid], parts[n - d][mid:] + down], 0)
        else:
            up = parts[d] + up
            down = parts[n - d] + down
        up, down = shifts([(up, 1), (down, -1)], axis)
    return parts[0] + up + down


def trade(value, axis):
    return lax.all_to_all(value, axis, 0, 0)


def spread(value, axis):
    n = lax.axis_size(axis)
    return trade(jnp.broadcast_to(value[None], (n,) + value.shape), axis)


def local(snapshot, basis_first, basis_second, basis_third):
    depth = snapshot.shape[0] * snapshot.shape[1]
    nx = snapshot.shape[2]
    ny = snapshot.shape[3]
    rank = basis_second.shape[1]
    gx = lax.axis_size("gx")
    gy = lax.axis_size("gy")
    vert = lax.axis_size("vert")
    share = rank // gy
    part_m = share // 2
    field = snapshot.reshape(depth, nx, ny)
    first = lax.dynamic_slice_in_dim(basis_first, lax.axis_index("gx") * nx, nx, 0)

    third = basis_third.reshape(depth, rank)

    def pick(pairs):
        return np.eye(rank, dtype=np.float32)[[place * share + within for place, within in pairs]]

    pick_f = pick([(place, part_m + v) for v in range(vert) for place in range(gy)])
    pick_m = pick([(place, within) for place in range(gy) for within in range(part_m)])

    f = mode_product(pick_f, basis_second, field, share, 0, depth, third)
    second = after(basis_second, f)
    f = trade(f.reshape(vert, gy, depth + STEP, nx), "vert")

    half = depth // 2
    m = []
    for start in (0, half):
        part = mode_product(pick_m, second, field, share, start, half)
        m.append(ring_sum([part[d * part_m : (d + 1) * part_m] for d in range(gy)], "gy"))
    m, f = lax.optimization_barrier((jnp.concatenate(m, 1), f))
    m = trade(m, "vert")

    third = f[:, :, depth:, :rank].reshape(vert * depth, rank).T
    f = depth_product(third, f, depth)
    f = ring_sum([f[d] for d in range(gy)], "gy")
    f, m = lax.optimization_barrier((f, m))
    m = depth_product(third, m.reshape(vert, 1, depth, nx), depth)[0]

    columns = jnp.concatenate([f, m], 0)
    weights = jnp.dot(columns, first, precision=HIGHEST)
    others = shifts([(weights, d) for d in range(1, gx)], "gx")
    for other in others:
        weights = weights + other
    updated = lax.dot_general(columns, weights, (((0,), (0,)), ((), ())), precision=HIGHEST)

    updated = jnp.sum(trade(updated.reshape(vert, nx // vert, rank), "vert"), axis=0)
    updated = jnp.sum(spread(updated, "gy"), axis=0) / float(rank * rank)
    return spread(updated, "vert").reshape(nx, rank)


def solution(mesh):
    placed = (P("vert", None, "gx", "gy"), P(), P("gy", None), P("vert", None, None))
    return jax.shard_map(
        local, mesh=mesh, in_specs=placed, out_specs=P("gx", None), check_vma=False
    )
```

time: 157 us -> 154 us (0.981)
  Pallas kernels: 15.3 us -> 23.4 us
  local copies, waits for them, and re-layouts: 11.5 us -> 3.93 us
  matrix products: 3.18 us -> 0.98 us
  waiting for transfers between devices: 36.4 us -> 34.7 us
    unnamed x11 -> x7, local copies, waits for them, and re-layouts: 10.3 us -> 0.67 us
    pallas_call x5, Pallas kernels: 15.3 us -> 23.4 us  [the longest x3 19.3 us: mode_product(): pl.pallas_call(functools.partial(mode_kernel if extra else plain_kernel,...]
    all_to_all x2, starting transfers between devices: 14.6 us -> 17.8 us  [trade(): return lax.all_to_all(value, axis, 0, 0)]
    all_to_all x2, waiting for transfers between devices: 6.12 us -> 2.99 us  [trade(): return lax.all_to_all(value, axis, 0, 0)]
    dot_general x2 -> x0, matrix products: 2.2 us -> none  [rows(): return lax.dot_general(turn, basis_second, NT, precision=HIGHEST)]
    slice x2, local copies, waits for them, and re-layouts: 0.04 us -> 2.12 us  [ring_sum(): up, down = shifts([(parts[half][:mid], 1), (parts[half][mid:], -1)], axis)]
    ppermute x27, starting transfers between devices: 40.9 us -> 39.2 us  [shifts(): lax.ppermute(value, axis, [(i, (i + by) % n) for i in range(n)])]
  transfers between devices with their start and end apart: 29 -> 29, of which waited for: 15 -> 14; matrix products, arithmetic and copies ran while one was open for 1% -> 2% of each run, Pallas kernels for 3% -> 7%
where the time goes in v3:
time: 154 us; the launch traced here: 153 us
  starting transfers between devices  57 us (37%)
  waiting for transfers between devices  34.7 us (23%)
  blocking collectives  31.3 us (20%)
  Pallas kernels  23.4 us (15%)
  local copies, waits for them, and re-layouts  3.93 us (3%)
  other arithmetic  1.61 us (1%)
    ppermute x27, starting transfers between devices, shifts(): lax.ppermute(value, axis, [(i, (i + by) % n) for i in range(n)])  39.2 us
    ppermute x27, waiting for transfers between devices, shifts(): lax.ppermute(value, axis, [(i, (i + by) % n) for i in range(n)])  31.7 us
    all_to_all x3, blocking collectives, trade(): return lax.all_to_all(value, axis, 0, 0)  31.3 us
    pallas_call x3, Pallas kernels, mode_product(): pl.pallas_call(functools.partial(mode_kernel if extra else plain_kernel,...  19.3 us
    all_to_all x2, starting transfers between devices, trade(): return lax.all_to_all(value, axis, 0, 0)  17.8 us
    pallas_call x2, Pallas kernels, depth_product(): pl.pallas_call(depth_kernel, grid=(groups // step,), in_specs=[pl.BlockSp...  4.03 us
  transfers between devices with their start and end apart: 29, of which 14 were waited for; matrix products, arithmetic and copies ran while one was open for 2% of the time, Pallas kernels for 7%

profile of v3, /device:TPU:1, one launch (start us, length us, event | category | flops | bytes accessed | tf_op | source)
XLA Modules:
  0.0 153.2 jit_solution(7472757809958062777)
XLA Ops:
  0.0 8.5 %shard_map.64 = f32[64,72,256]{2,1,0:T(8,128)} custom-call(f32[64,128]{1,0:T(8,128)} %constant.21.clone.pick_ref, f32[128,128]{1,0:T(8,128)} %second_ref.3, f32[64,256,128]{2,1,0:T(8,128)} %bitcast.52, f32[64,128]{1,0:T(8,128)} %bitcast.59), custom_call_target="tpu_custom_call" | custom-call | flops 805306368 | bytes 12582912 | tf_op jit(solution)/shard_map/pallas_call | solution.py:95
  8.5 7.7 %all-to-all-start = ((f32[8,8,72,256]{3,2,1,0:T(8,128)}), f32[8,8,72,256]{3,2,1,0:T(8,128)}, u32[]{:S(2)}, u32[]{:S(2)}) async-start(f32[8,8,72,256]{3,2,1,0:T(8,128)} %bitcast.55), calls=%async_computation | async-start | bytes 9437184 | tf_op jit(solution)/shard_map/all_to_all | solution.py:183
  16.3 5.4 %shard_map.66 = f32[64,32,256]{2,1,0:T(8,128)} custom-call(f32[64,128]{1,0:T(8,128)} %constant.22.clone.pick_ref, f32[128,128]{1,0:T(8,128)} %second_ref.3, f32[64,256,128]{2,1,0:T(8,128)} %bitcast.53), custom_call_target="tpu_custom_call" | custom-call | flops 402653184 | bytes 6291456 | tf_op jit(solution)/shard_map/pallas_call | solution.py:95
  22.8 3.9 %collective-permute-start.9 = (f32[4,32,256]{2,1,0:T(8,128)S(1)}, f32[4,32,256]{2,1,0:T(8,128)S(1)}, u32[]{:S(2)}, u32[]{:S(2)}) collective-permute-start(f32[4,32,256]{2,1,0:T(8,128)S(1)} %get-tuple-element.47), channel_id=1, source_target_pairs={{0,56},{8,0},{16,8},{24,16},{32,24},{40,32},{48,40},{56,48},{1,57}... | collective-permute-start | bytes 393224 | tf_op jit(solution)/shard_map/ppermute | solution.py:161
  26.7 5.4 %shard_map.65 = f32[64,32,256]{2,1,0:T(8,128)} custom-call(f32[64,128]{1,0:T(8,128)} %constant.22.clone.pick_ref, f32[128,128]{1,0:T(8,128)} %second_ref.3, f32[64,256,128]{2,1,0:T(8,128)} %bitcast.54), custom_call_target="tpu_custom_call" | custom-call | flops 402653184 | bytes 6291456 | tf_op jit(solution)/shard_map/pallas_call | solution.py:95
  33.3 2.7 %collective-permute-start.1 = (f32[4,32,256]{2,1,0:T(8,128)S(1)}, f32[4,32,256]{2,1,0:T(8,128)S(1)}, u32[]{:S(2)}, u32[]{:S(2)}) collective-permute-start(f32[4,32,256]{2,1,0:T(8,128)S(1)} %get-tuple-element.39), channel_id=1, source_target_pairs={{0,56},{8,0},{16,8},{24,16},{32,24},{40,32},{48,40},{56,48},{1,57}... | collective-permute-start | bytes 393224 | tf_op jit(solution)/shard_map/ppermute | solution.py:161
  36.2 2.7 %collective-permute-start.11 = (f32[8,32,256]{2,1,0:T(8,128)S(1)}, f32[8,32,256]{2,1,0:T(8,128)S(1)}, u32[]{:S(2)}, u32[]{:S(2)}) collective-permute-start(f32[8,32,256]{2,1,0:T(8,128)S(1)} %get-tuple-element.49), channel_id=1, source_target_pairs={{0,56},{8,0},{16,8},{24,16},{32,24},{40,32},{48,40},{56,48},{1,57}... | collective-permute-start | bytes 786440 | tf_op jit(solution)/shard_map/ppermute | solution.py:161
  39.5 2.7 %collective-permute-start.3 = (f32[8,32,256]{2,1,0:T(8,128)S(1)}, f32[8,32,256]{2,1,0:T(8,128)S(1)}, u32[]{:S(2)}, u32[]{:S(2)}) collective-permute-start(f32[8,32,256]{2,1,0:T(8,128)S(1)} %get-tuple-element.41), channel_id=1, source_target_pairs={{0,56},{8,0},{16,8},{24,16},{32,24},{40,32},{48,40},{56,48},{1,57}... | collective-permute-start | bytes 786440 | tf_op jit(solution)/shard_map/ppermute | solution.py:161
  42.2 2.2 %collective-permute-done.10 = f32[8,32,256]{2,1,0:T(8,128)S(1)} collective-permute-done((f32[8,32,256]{2,1,0:T(8,128)S(1)}, f32[8,32,256]{2,1,0:T(8,128)S(1)}, u32[]{:S(2)}, u32[]{:S(2)}) %collective-permute-start.10) | collective-permute-done | bytes 262176 | tf_op jit(solution)/shard_map/ppermute | solution.py:161
  44.5 2.7 %collective-permute-start.13 = (f32[8,32,256]{2,1,0:T(8,128)S(1)}, f32[8,32,256]{2,1,0:T(8,128)S(1)}, u32[]{:S(2)}, u32[]{:S(2)}) collective-permute-start(f32[8,32,256]{2,1,0:T(8,128)S(1)} %get-tuple-element.51), channel_id=1, source_target_pairs={{0,56},{8,0},{16,8},{24,16},{32,24},{40,32},{48,40},{56,48},{1,57}... | collective-permute-start | bytes 786440 | tf_op jit(solution)/shard_map/ppermute | solution.py:161
  47.2 2.8 %collective-permute-done.2 = f32[8,32,256]{2,1,0:T(8,128)S(1)} collective-permute-done((f32[8,32,256]{2,1,0:T(8,128)S(1)}, f32[8,32,256]{2,1,0:T(8,128)S(1)}, u32[]{:S(2)}, u32[]{:S(2)}) %collective-permute-start.2) | collective-permute-done | bytes 262176 | tf_op jit(solution)/shard_map/ppermute | solution.py:161
  50.1 2.7 %collective-permute-start.5 = (f32[8,32,256]{2,1,0:T(8,128)S(1)}, f32[8,32,256]{2,1,0:T(8,128)S(1)}, u32[]{:S(2)}, u32[]{:S(2)}) collective-permute-start(f32[8,32,256]{2,1,0:T(8,128)S(1)} %get-tuple-element.43), channel_id=1, source_target_pairs={{0,56},{8,0},{16,8},{24,16},{32,24},{40,32},{48,40},{56,48},{1,57}... | collective-permute-start | bytes 786440 | tf_op jit(solution)/shard_map/ppermute | solution.py:161
  52.8 2.8 %collective-permute-done.12 = f32[8,32,256]{2,1,0:T(8,128)S(1)} collective-permute-done((f32[8,32,256]{2,1,0:T(8,128)S(1)}, f32[8,32,256]{2,1,0:T(8,128)S(1)}, u32[]{:S(2)}, u32[]{:S(2)}) %collective-permute-start.12) | collective-permute-done | bytes 262176 | tf_op jit(solution)/shard_map/ppermute | solution.py:161
  55.7 2.7 %collective-permute-start.15 = (f32[8,32,256]{2,1,0:T(8,128)S(1)}, f32[8,32,256]{2,1,0:T(8,128)S(1)}, u32[]{:S(2)}, u32[]{:S(2)}) collective-permute-start(f32[8,32,256]{2,1,0:T(8,128)S(1)} %get-tuple-element.53), channel_id=1, source_target_pairs={{0,56},{8,0},{16,8},{24,16},{32,24},{40,32},{48,40},{56,48},{1,57}... | collective-permute-start | bytes 786440 | tf_op jit(solution)/shard_map/ppermute | solution.py:161
  58.4 2.8 %collective-permute-done.4 = f32[8,32,256]{2,1,0:T(8,128)S(1)} collective-permute-done((f32[8,32,256]{2,1,0:T(8,128)S(1)}, f32[8,32,256]{2,1,0:T(8,128)S(1)}, u32[]{:S(2)}, u32[]{:S(2)}) %collective-permute-start.4) | collective-permute-done | bytes 262176 | tf_op jit(solution)/shard_map/ppermute | solution.py:161
  61.4 2.7 %collective-permute-start.7 = (f32[8,32,256]{2,1,0:T(8,128)S(1)}, f32[8,32,256]{2,1,0:T(8,128)S(1)}, u32[]{:S(2)}, u32[]{:S(2)}) collective-permute-start(f32[8,32,256]{2,1,0:T(8,128)S(1)} %get-tuple-element.45), channel_id=1, source_target_pairs={{0,56},{8,0},{16,8},{24,16},{32,24},{40,32},{48,40},{56,48},{1,57}... | collective-permute-start | bytes 786440 | tf_op jit(solution)/shard_map/ppermute | solution.py:161
  64.0 2.8 %collective-permute-done.14 = f32[8,32,256]{2,1,0:T(8,128)S(1)} collective-permute-done((f32[8,32,256]{2,1,0:T(8,128)S(1)}, f32[8,32,256]{2,1,0:T(8,128)S(1)}, u32[]{:S(2)}, u32[]{:S(2)}) %collective-permute-start.14) | collective-permute-done | bytes 262176 | tf_op jit(solution)/shard_map/ppermute | solution.py:161
  66.9 5.4 %collective-permute-done.6 = f32[8,32,256]{2,1,0:T(8,128)S(1)} collective-permute-done((f32[8,32,256]{2,1,0:T(8,128)S(1)}, f32[8,32,256]{2,1,0:T(8,128)S(1)}, u32[]{:S(2)}, u32[]{:S(2)}) %collective-permute-start.6) | collective-permute-done | bytes 262176 | tf_op jit(solution)/shard_map/ppermute | solution.py:161
  74.3 3.8 %shard_map.67 = f32[8,128,256]{2,1,0:T(8,128)S(1)} custom-call(f32[128,512]{1,0:T(8,128)S(1)} %bitcast.47, f32[8,8,72,256]{3,2,1,0:T(8,128)} %all-to-all-done.part_ref), custom_call_target="tpu_custom_call" | custom-call | flops 805306368 | bytes 4194304 | tf_op jit(solution)/shard_map/pallas_call | solution.py:134
  78.2 2.7 %collective-permute-start.17 = (f32[64,256]{1,0:T(8,128)S(1)}, f32[64,256]{1,0:T(8,128)S(1)}, u32[]{:S(2)}, u32[]{:S(2)}) collective-permute-start(f32[64,256]{1,0:T(8,128)S(1)} %get-tuple-element.56), channel_id=1, source_target_pairs={{0,56},{8,0},{16,8},{24,16},{32,24},{40,32},{48,40},{56,48},{1,57}... | collective-permute-start | bytes 196616 | tf_op jit(solution)/shard_map/ppermute | solution.py:161
  80.9 1.6 %collective-permute-done.16 = f32[64,256]{1,0:T(8,128)S(1)} collective-permute-done((f32[64,256]{1,0:T(8,128)S(1)}, f32[64,256]{1,0:T(8,128)S(1)}, u32[]{:S(2)}, u32[]{:S(2)}) %collective-permute-start.16) | collective-permute-done | bytes 65568 | tf_op jit(solution)/shard_map/ppermute | solution.py:161
  82.6 1.9 %collective-permute-start.18 = (f32[128,256]{1,0:T(8,128)S(1)}, f32[128,256]{1,0:T(8,128)S(1)}, u32[]{:S(2)}, u32[]{:S(2)}) collective-permute-start(f32[128,256]{1,0:T(8,128)S(1)} %pad_maximum_fusion.8), channel_id=1, source_target_pairs={{0,8},{8,16},{16,24},{24,32},{32,40},{40,48},{48,56},{56,0},{1,9},... | collective-permute-start | bytes 393224 | tf_op jit(solution)/shard_map/ppermute | solution.py:161
  85.4 2.3 %collective-permute-done.18 = f32[128,256]{1,0:T(8,128)S(1)} collective-permute-done((f32[128,256]{1,0:T(8,128)S(1)}, f32[128,256]{1,0:T(8,128)S(1)}, u32[]{:S(2)}, u32[]{:S(2)}) %collective-permute-start.18) | collective-permute-done | bytes 131104 | tf_op jit(solution)/shard_map/ppermute | solution.py:161
  88.3 1.5 %collective-permute-start.20 = (f32[128,256]{1,0:T(8,128)S(1)}, f32[128,256]{1,0:T(8,128)S(1)}, u32[]{:S(2)}, u32[]{:S(2)}) collective-permute-start(f32[128,256]{1,0:T(8,128)S(1)} %get-tuple-element.59), channel_id=1, source_target_pairs={{0,8},{8,16},{16,24},{24,32},{32,40},{40,48},{48,56},{56,0},{1,9},... | collective-permute-start | bytes 393224 | tf_op jit(solution)/shard_map/ppermute | solution.py:161
  91.1 10.0 %all-to-all-start.1 = ((f32[8,64,256]{2,1,0:T(8,128)}), f32[8,64,256]{2,1,0:T(8,128)S(1)}, u32[]{:S(2)}, u32[]{:S(2)}) async-start(f32[8,64,256]{2,1,0:T(8,128)} %pad_maximum_fusion), calls=%async_computation.1 | async-start | bytes 1048576 | tf_op jit(solution)/shard_map/all_to_all | solution.py:183
  103.9 3.6 %collective-permute-done.22 = f32[128,256]{1,0:T(8,128)S(1)} collective-permute-done((f32[128,256]{1,0:T(8,128)S(1)}, f32[128,256]{1,0:T(8,128)S(1)}, u32[]{:S(2)}, u32[]{:S(2)}) %collective-permute-start.22) | collective-permute-done | bytes 131104 | tf_op jit(solution)/shard_map/ppermute | solution.py:161
  107.6 3.0 %all-to-all-done.1 = f32[8,64,256]{2,1,0:T(8,128)S(1)} async-done(((f32[8,64,256]{2,1,0:T(8,128)}), f32[8,64,256]{2,1,0:T(8,128)S(1)}, u32[]{:S(2)}, u32[]{:S(2)}) %all-to-all-start.1) | async-done | bytes 524320 | tf_op jit(solution)/shard_map/all_to_all | solution.py:183
  112.6 2.5 %collective-permute-start.25 = (f32[256,128]{1,0:T(8,128)S(1)}, f32[256,128]{1,0:T(8,128)S(1)}, u32[]{:S(2)}, u32[]{:S(2)}) collective-permute-start(f32[256,128]{1,0:T(8,128)S(1)} %fusion.3), channel_id=1, source_target_pairs={{0,128},{64,192},{128,0},{192,64},{1,129},{65,193},{129,1},{193,65... | collective-permute-start | bytes 393224 | tf_op jit(solution)/shard_map/ppermute | solution.py:161
  116.7 3.8 %collective-permute-done.25 = f32[256,128]{1,0:T(8,128)S(1)} collective-permute-done((f32[256,128]{1,0:T(8,128)S(1)}, f32[256,128]{1,0:T(8,128)S(1)}, u32[]{:S(2)}, u32[]{:S(2)}) %collective-permute-start.25) | collective-permute-done | bytes 131104 | tf_op jit(solution)/shard_map/ppermute | solution.py:161
  121.1 9.4 %all_to_all.25 = f32[8,32,128]{2,1,0:T(8,128)S(1)} all-to-all(f32[8,32,128]{2,1,0:T(8,128)S(1)} %bitcast.57), channel_id=1, replica_groups=mesh['gx'=4,'gy'=8,'vert'=8] {'vert'}, dimensions={0} | all-to-all | bytes 262144 | tf_op jit(solution)/shard_map/all_to_all | solution.py:183
  130.6 11.9 %all_to_all.26 = f32[8,32,128]{2,1,0:T(8,128)S(1)} all-to-all(f32[8,32,128]{2,1,0:T(8,128)S(1)} %broadcast_in_dim.4), channel_id=1, replica_groups=mesh['gx'=4,'gy'=8,'vert'=8] {'gy'}, dimensions={0} | all-to-all | bytes 262144 | tf_op jit(solution)/shard_map/all_to_all | solution.py:183
  142.5 10.0 %all_to_all.27 = f32[8,32,128]{2,1,0:T(8,128)S(1)} all-to-all(f32[8,32,128]{2,1,0:T(8,128)S(1)} %broadcast_in_dim.5), channel_id=1, replica_groups=mesh['gx'=4,'gy'=8,'vert'=8] {'vert'}, dimensions={0} | all-to-all | bytes 262144 | tf_op jit(solution)/shard_map/all_to_all | solution.py:183
  (70 shorter events, 16.5 us)
Async XLA Ops:
  0.0 110.9 %copy-start = (f32[1024,128]{1,0:T(8,128)S(1)}, f32[1024,128]{1,0:T(8,128)}, u32[]{:S(2)}) copy-start(f32[1024,128]{1,0:T(8,128)} %param.7) | copy-start | bytes 1572868
  8.5 64.7 %all-to-all-start = ((f32[8,8,72,256]{3,2,1,0:T(8,128)}), f32[8,8,72,256]{3,2,1,0:T(8,128)}, u32[]{:S(2)}, u32[]{:S(2)}) async-start(f32[8,8,72,256]{3,2,1,0:T(8,128)} %bitcast.55), calls=%async_computation | async-start | bytes 9437184 | tf_op jit(solution)/shard_map/all_to_all | solution.py:183
  22.7 13.3 %copy-start.1 = (f32[64,32,256]{2,1,0:T(8,128)S(1)}, f32[64,32,256]{2,1,0:T(8,128)}, u32[]{:S(2)}) copy-start(f32[64,32,256]{2,1,0:T(8,128)} %shard_map.66) | copy-start | bytes 6291460
  22.7 13.3 %collective-permute-start.8 = (f32[4,32,256]{2,1,0:T(8,128)S(1)}, f32[4,32,256]{2,1,0:T(8,128)S(1)}, u32[]{:S(2)}, u32[]{:S(2)}) collective-permute-start(f32[4,32,256]{2,1,0:T(8,128)S(1)} %get-tuple-element.46), channel_id=1, source_target_pairs={{0,8},{8,16},{16,24},{24,32},{32,40},{40,48},{48,56},{56,0},{1,9},... | collective-permute-start | bytes 393224 | tf_op jit(solution)/shard_map/ppermute | solution.py:161
  22.8 13.2 %collective-permute-start.9 = (f32[4,32,256]{2,1,0:T(8,128)S(1)}, f32[4,32,256]{2,1,0:T(8,128)S(1)}, u32[]{:S(2)}, u32[]{:S(2)}) collective-permute-start(f32[4,32,256]{2,1,0:T(8,128)S(1)} %get-tuple-element.47), channel_id=1, source_target_pairs={{0,56},{8,0},{16,8},{24,16},{32,24},{40,32},{48,40},{56,48},{1,57}... | collective-permute-start | bytes 393224 | tf_op jit(solution)/shard_map/ppermute | solution.py:161
  32.1 7.2 %copy-start.2 = (f32[64,32,256]{2,1,0:T(8,128)S(1)}, f32[64,32,256]{2,1,0:T(8,128)}, u32[]{:S(2)}) copy-start(f32[64,32,256]{2,1,0:T(8,128)} %shard_map.65) | copy-start | bytes 6291460
  33.3 6.0 %collective-permute-start = (f32[4,32,256]{2,1,0:T(8,128)S(1)}, f32[4,32,256]{2,1,0:T(8,128)S(1)}, u32[]{:S(2)}, u32[]{:S(2)}) collective-permute-start(f32[4,32,256]{2,1,0:T(8,128)S(1)} %get-tuple-element.38), channel_id=1, source_target_pairs={{0,8},{8,16},{16,24},{24,32},{32,40},{40,48},{48,56},{56,0},{1,9},... | collective-permute-start | bytes 393224 | tf_op jit(solution)/shard_map/ppermute | solution.py:161
  33.3 5.9 %collective-permute-start.1 = (f32[4,32,256]{2,1,0:T(8,128)S(1)}, f32[4,32,256]{2,1,0:T(8,128)S(1)}, u32[]{:S(2)}, u32[]{:S(2)}) collective-permute-start(f32[4,32,256]{2,1,0:T(8,128)S(1)} %get-tuple-element.39), channel_id=1, source_target_pairs={{0,56},{8,0},{16,8},{24,16},{32,24},{40,32},{48,40},{56,48},{1,57}... | collective-permute-start | bytes 393224 | tf_op jit(solution)/shard_map/ppermute | solution.py:161
  36.1 8.2 %collective-permute-start.10 = (f32[8,32,256]{2,1,0:T(8,128)S(1)}, f32[8,32,256]{2,1,0:T(8,128)S(1)}, u32[]{:S(2)}, u32[]{:S(2)}) collective-permute-start(f32[8,32,256]{2,1,0:T(8,128)S(1)} %get-tuple-element.48), channel_id=1, source_target_pairs={{0,8},{8,16},{16,24},{24,32},{32,40},{40,48},{48,56},{56,0},{1,9},... | collective-permute-start | bytes 786440 | tf_op jit(solution)/shard_map/ppermute | solution.py:161
  36.2 8.1 %collective-permute-start.11 = (f32[8,32,256]{2,1,0:T(8,128)S(1)}, f32[8,32,256]{2,1,0:T(8,128)S(1)}, u32[]{:S(2)}, u32[]{:S(2)}) collective-permute-start(f32[8,32,256]{2,1,0:T(8,128)S(1)} %get-tuple-element.49), channel_id=1, source_target_pairs={{0,56},{8,0},{16,8},{24,16},{32,24},{40,32},{48,40},{56,48},{1,57}... | collective-permute-start | bytes 786440 | tf_op jit(solution)/shard_map/ppermute | solution.py:161
  39.4 10.5 %collective-permute-start.2 = (f32[8,32,256]{2,1,0:T(8,128)S(1)}, f32[8,32,256]{2,1,0:T(8,128)S(1)}, u32[]{:S(2)}, u32[]{:S(2)}) collective-permute-start(f32[8,32,256]{2,1,0:T(8,128)S(1)} %get-tuple-element.40), channel_id=1, source_target_pairs={{0,8},{8,16},{16,24},{24,32},{32,40},{40,48},{48,56},{56,0},{1,9},... | collective-permute-start | bytes 786440 | tf_op jit(solution)/shard_map/ppermute | solution.py:161
  39.5 10.5 %collective-permute-start.3 = (f32[8,32,256]{2,1,0:T(8,128)S(1)}, f32[8,32,256]{2,1,0:T(8,128)S(1)}, u32[]{:S(2)}, u32[]{:S(2)}) collective-permute-start(f32[8,32,256]{2,1,0:T(8,128)S(1)} %get-tuple-element.41), channel_id=1, source_target_pairs={{0,56},{8,0},{16,8},{24,16},{32,24},{40,32},{48,40},{56,48},{1,57}... | collective-permute-start | bytes 786440 | tf_op jit(solution)/shard_map/ppermute | solution.py:161
  44.4 11.2 %collective-permute-start.12 = (f32[8,32,256]{2,1,0:T(8,128)S(1)}, f32[8,32,256]{2,1,0:T(8,128)S(1)}, u32[]{:S(2)}, u32[]{:S(2)}) collective-permute-start(f32[8,32,256]{2,1,0:T(8,128)S(1)} %get-tuple-element.50), channel_id=1, source_target_pairs={{0,8},{8,16},{16,24},{24,32},{32,40},{40,48},{48,56},{56,0},{1,9},... | collective-permute-start | bytes 786440 | tf_op jit(solution)/shard_map/ppermute | solution.py:161
  44.5 11.1 %collective-permute-start.13 = (f32[8,32,256]{2,1,0:T(8,128)S(1)}, f32[8,32,256]{2,1,0:T(8,128)S(1)}, u32[]{:S(2)}, u32[]{:S(2)}) collective-permute-start(f32[8,32,256]{2,1,0:T(8,128)S(1)} %get-tuple-element.51), channel_id=1, source_target_pairs={{0,56},{8,0},{16,8},{24,16},{32,24},{40,32},{48,40},{56,48},{1,57}... | collective-permute-start | bytes 786440 | tf_op jit(solution)/shard_map/ppermute | solution.py:161
  50.0 11.1 %collective-permute-start.4 = (f32[8,32,256]{2,1,0:T(8,128)S(1)}, f32[8,32,256]{2,1,0:T(8,128)S(1)}, u32[]{:S(2)}, u32[]{:S(2)}) collective-permute-start(f32[8,32,256]{2,1,0:T(8,128)S(1)} %get-tuple-element.42), channel_id=1, source_target_pairs={{0,8},{8,16},{16,24},{24,32},{32,40},{40,48},{48,56},{56,0},{1,9},... | collective-permute-start | bytes 786440 | tf_op jit(solution)/shard_map/ppermute | solution.py:161
  50.1 11.1 %collective-permute-start.5 = (f32[8,32,256]{2,1,0:T(8,128)S(1)}, f32[8,32,256]{2,1,0:T(8,128)S(1)}, u32[]{:S(2)}, u32[]{:S(2)}) collective-permute-start(f32[8,32,256]{2,1,0:T(8,128)S(1)} %get-tuple-element.43), channel_id=1, source_target_pairs={{0,56},{8,0},{16,8},{24,16},{32,24},{40,32},{48,40},{56,48},{1,57}... | collective-permute-start | bytes 786440 | tf_op jit(solution)/shard_map/ppermute | solution.py:161
  55.6 11.2 %collective-permute-start.14 = (f32[8,32,256]{2,1,0:T(8,128)S(1)}, f32[8,32,256]{2,1,0:T(8,128)S(1)}, u32[]{:S(2)}, u32[]{:S(2)}) collective-permute-start(f32[8,32,256]{2,1,0:T(8,128)S(1)} %get-tuple-element.52), channel_id=1, source_target_pairs={{0,8},{8,16},{16,24},{24,32},{32,40},{40,48},{48,56},{56,0},{1,9},... | collective-permute-start | bytes 786440 | tf_op jit(solution)/shard_map/ppermute | solution.py:161
  55.7 11.1 %collective-permute-start.15 = (f32[8,32,256]{2,1,0:T(8,128)S(1)}, f32[8,32,256]{2,1,0:T(8,128)S(1)}, u32[]{:S(2)}, u32[]{:S(2)}) collective-permute-start(f32[8,32,256]{2,1,0:T(8,128)S(1)} %get-tuple-element.53), channel_id=1, source_target_pairs={{0,56},{8,0},{16,8},{24,16},{32,24},{40,32},{48,40},{56,48},{1,57}... | collective-permute-start | bytes 786440 | tf_op jit(solution)/shard_map/ppermute | solution.py:161
  61.3 11.0 %collective-permute-start.6 = (f32[8,32,256]{2,1,0:T(8,128)S(1)}, f32[8,32,256]{2,1,0:T(8,128)S(1)}, u32[]{:S(2)}, u32[]{:S(2)}) collective-permute-start(f32[8,32,256]{2,1,0:T(8,128)S(1)} %get-tuple-element.44), channel_id=1, source_target_pairs={{0,8},{8,16},{16,24},{24,32},{32,40},{40,48},{48,56},{56,0},{1,9},... | collective-permute-start | bytes 786440 | tf_op jit(solution)/shard_map/ppermute | solution.py:161
  61.4 11.0 %collective-permute-start.7 = (f32[8,32,256]{2,1,0:T(8,128)S(1)}, f32[8,32,256]{2,1,0:T(8,128)S(1)}, u32[]{:S(2)}, u32[]{:S(2)}) collective-permute-start(f32[8,32,256]{2,1,0:T(8,128)S(1)} %get-tuple-element.45), channel_id=1, source_target_pairs={{0,56},{8,0},{16,8},{24,16},{32,24},{40,32},{48,40},{56,48},{1,57}... | collective-permute-start | bytes 786440 | tf_op jit(solution)/shard_map/ppermute | solution.py:161
  78.1 4.4 %collective-permute-start.16 = (f32[64,256]{1,0:T(8,128)S(1)}, f32[64,256]{1,0:T(8,128)S(1)}, u32[]{:S(2)}, u32[]{:S(2)}) collective-permute-start(f32[64,256]{1,0:T(8,128)S(1)} %get-tuple-element.55), channel_id=1, source_target_pairs={{0,8},{8,16},{16,24},{24,32},{32,40},{40,48},{48,56},{56,0},{1,9},... | collective-permute-start | bytes 196616 | tf_op jit(solution)/shard_map/ppermute | solution.py:161
  78.2 4.3 %collective-permute-start.17 = (f32[64,256]{1,0:T(8,128)S(1)}, f32[64,256]{1,0:T(8,128)S(1)}, u32[]{:S(2)}, u32[]{:S(2)}) collective-permute-start(f32[64,256]{1,0:T(8,128)S(1)} %get-tuple-element.56), channel_id=1, source_target_pairs={{0,56},{8,0},{16,8},{24,16},{32,24},{40,32},{48,40},{56,48},{1,57}... | collective-permute-start | bytes 196616 | tf_op jit(solution)/shard_map/ppermute | solution.py:161
  82.6 5.1 %collective-permute-start.18 = (f32[128,256]{1,0:T(8,128)S(1)}, f32[128,256]{1,0:T(8,128)S(1)}, u32[]{:S(2)}, u32[]{:S(2)}) collective-permute-start(f32[128,256]{1,0:T(8,128)S(1)} %pad_maximum_fusion.8), channel_id=1, source_target_pairs={{0,8},{8,16},{16,24},{24,32},{32,40},{40,48},{48,56},{56,0},{1,9},... | collective-permute-start | bytes 393224 | tf_op jit(solution)/shard_map/ppermute | solution.py:161
  84.5 3.8 %collective-permute-start.19 = (f32[128,256]{1,0:T(8,128)S(1)}, f32[128,256]{1,0:T(8,128)S(1)}, u32[]{:S(2)}, u32[]{:S(2)}) collective-permute-start(f32[128,256]{1,0:T(8,128)S(1)} %pad_maximum_fusion.9), channel_id=1, source_target_pairs={{0,56},{8,0},{16,8},{24,16},{32,24},{40,32},{48,40},{56,48},{1,57}... | collective-permute-start | bytes 393224 | tf_op jit(solution)/shard_map/ppermute | solution.py:161
  88.3 12.8 %collective-permute-start.20 = (f32[128,256]{1,0:T(8,128)S(1)}, f32[128,256]{1,0:T(8,128)S(1)}, u32[]{:S(2)}, u32[]{:S(2)}) collective-permute-start(f32[128,256]{1,0:T(8,128)S(1)} %get-tuple-element.59), channel_id=1, source_target_pairs={{0,8},{8,16},{16,24},{24,32},{32,40},{40,48},{48,56},{56,0},{1,9},... | collective-permute-start | bytes 393224 | tf_op jit(solution)/shard_map/ppermute | solution.py:161
  89.9 11.3 %collective-permute-start.21 = (f32[128,256]{1,0:T(8,128)S(1)}, f32[128,256]{1,0:T(8,128)S(1)}, u32[]{:S(2)}, u32[]{:S(2)}) collective-permute-start(f32[128,256]{1,0:T(8,128)S(1)} %get-tuple-element.60), channel_id=1, source_target_pairs={{0,56},{8,0},{16,8},{24,16},{32,24},{40,32},{48,40},{56,48},{1,57}... | collective-permute-start | bytes 393224 | tf_op jit(solution)/shard_map/ppermute | solution.py:161
  91.1 19.5 %all-to-all-start.1 = ((f32[8,64,256]{2,1,0:T(8,128)}), f32[8,64,256]{2,1,0:T(8,128)S(1)}, u32[]{:S(2)}, u32[]{:S(2)}) async-start(f32[8,64,256]{2,1,0:T(8,128)} %pad_maximum_fusion), calls=%async_computation.1 | async-start | bytes 1048576 | tf_op jit(solution)/shard_map/all_to_all | solution.py:183
  101.2 6.4 %collective-permute-start.22 = (f32[128,256]{1,0:T(8,128)S(1)}, f32[128,256]{1,0:T(8,128)S(1)}, u32[]{:S(2)}, u32[]{:S(2)}) collective-permute-start(f32[128,256]{1,0:T(8,128)S(1)} %get-tuple-element.61), channel_id=1, source_target_pairs={{0,8},{8,16},{16,24},{24,32},{32,40},{40,48},{48,56},{56,0},{1,9},... | collective-permute-start | bytes 393224 | tf_op jit(solution)/shard_map/ppermute | solution.py:161
  102.6 5.0 %collective-permute-start.23 = (f32[128,256]{1,0:T(8,128)S(1)}, f32[128,256]{1,0:T(8,128)S(1)}, u32[]{:S(2)}, u32[]{:S(2)}) collective-permute-start(f32[128,256]{1,0:T(8,128)S(1)} %get-tuple-element.62), channel_id=1, source_target_pairs={{0,56},{8,0},{16,8},{24,16},{32,24},{40,32},{48,40},{56,48},{1,57}... | collective-permute-start | bytes 393224 | tf_op jit(solution)/shard_map/ppermute | solution.py:161
  111.3 5.4 %collective-permute-start.24 = (f32[256,128]{1,0:T(8,128)S(1)}, f32[256,128]{1,0:T(8,128)S(1)}, u32[]{:S(2)}, u32[]{:S(2)}) collective-permute-start(f32[256,128]{1,0:T(8,128)S(1)} %fusion.3), channel_id=1, source_target_pairs={{0,64},{64,128},{128,192},{192,0},{1,65},{65,129},{129,193},{193,1... | collective-permute-start | bytes 393224 | tf_op jit(solution)/shard_map/ppermute | solution.py:161
  112.6 7.9 %collective-permute-start.25 = (f32[256,128]{1,0:T(8,128)S(1)}, f32[256,128]{1,0:T(8,128)S(1)}, u32[]{:S(2)}, u32[]{:S(2)}) collective-permute-start(f32[256,128]{1,0:T(8,128)S(1)} %fusion.3), channel_id=1, source_target_pairs={{0,128},{64,192},{128,0},{192,64},{1,129},{65,193},{129,1},{193,65... | collective-permute-start | bytes 393224 | tf_op jit(solution)/shard_map/ppermute | solution.py:161
  115.0 5.5 %collective-permute-start.26 = (f32[256,128]{1,0:T(8,128)S(1)}, f32[256,128]{1,0:T(8,128)S(1)}, u32[]{:S(2)}, u32[]{:S(2)}) collective-permute-start(f32[256,128]{1,0:T(8,128)S(1)} %fusion.3), channel_id=1, source_target_pairs={{0,192},{64,0},{128,64},{192,128},{1,193},{65,1},{129,65},{193,129... | collective-permute-start | bytes 393224 | tf_op jit(solution)/shard_map/ppermute | solution.py:161

commit v4 on v3

--- a/solution.py
+++ b/solution.py
@@ -29,8 +29,11 @@
     return main[:rows] + (main[rows:] + rest)
 
 
-def mode_kernel(roll, first, pick_ref, second_ref, field_ref, third_ref, out_ref, both_ref, held_ref, sems):
-    rows, rank = pick_ref.shape
+def mode_kernel(roll, first, halves, pick_ref, second_ref, field_ref, *refs):
+    count = len(halves)
+    third_ref, refs = (refs[0], refs[1:]) if len(refs) > count + 3 else (None, refs)
+    out_refs, (both_ref, held_ref, sems) = refs[:count], refs[count:]
+    rows = pick_ref.shape[0] // count
     ny = second_ref.shape[0]
     steps = held_ref.shape[0] // STEP
 
@@ -44,27 +47,49 @@
         for i in range(steps):
             fetch(i).start()
         pick = pltpu.roll(pick_ref[...], lax.axis_index("gy") * roll, 1).astype(jnp.bfloat16)
+        both_ref[...] = jnp.zeros_like(both_ref)
         for part, value in enumerate(split(second_ref[...])):
-            value = lax.dot_general(pick, value, NT, preferred_element_type=jnp.float32)
-            both_ref[part * rows : (part + 1) * rows, :ny] = value.astype(jnp.bfloat16)
-        both_ref[:rows, ny:] = both_ref[:rows, :ny]
-        both_ref[rows:, ny:] = jnp.zeros((rows, ny), jnp.bfloat16)
-
-    @pl.when(pl.program_id(0) < steps)
-    def _():
+            value = lax.dot_general(pick, value, NT, preferred_element_type=jnp.float32).astype(jnp.bfloat16)
+            for n in range(count):
+                place = (2 * n + part) * rows
+                both_ref[place : place + rows, :ny] = value[n * rows : (n + 1) * rows]
+                if part == 0:
+                    both_ref[place : place + rows, ny:] = value[n * rows : (n + 1) * rows]
+
+    def multiply(outs):
         i = pl.program_id(0)
         fetch(i).wait()
-        both = both_ref[...]
+        both = both_ref[: 2 * rows * len(outs)]
         for j in range(STEP):
             pair = jnp.concatenate(split(held_ref[i * STEP + j]), 1)
             value = lax.dot_general(both, pair, NT, preferred_element_type=jnp.float32)
-            out_ref[:, j, :] = value[:rows] + value[rows:]
+            for n, out_ref in enumerate(outs):
+                base = 2 * n * rows
+                out_ref[:, j, :] = value[base : base + rows] + value[base + rows : base + 2 * rows]
+
+    if any(halves):
+
+        @pl.when(pl.program_id(0) < steps // 2)
+        def _():
+            multiply(out_refs)
+
+        @pl.when((pl.program_id(0) >= steps // 2) & (pl.program_id(0) < steps))
+        def _():
+            multiply([out_ref for out_ref, half in zip(out_refs, halves) if not half])
+
+    else:
+
+        @pl.when(pl.program_id(0) < steps)
+        def _():
+            multiply(out_refs)
 
     if third_ref is None:
         return
 
     @pl.when(pl.program_id(0) == steps)
     def _():
+        out_ref = out_refs[0]
+        rank = third_ref.shape[1]
         groups = out_ref.shape[0] // SETS
         for r in range(out_ref.shape[0]):
             g = r % groups
@@ -72,19 +97,21 @@
             out_ref[r, :, rank:] = third_ref[g * STEP : (g + 1) * STEP, :]
 
 
-def plain_kernel(roll, first, pick_ref, second_ref, field_ref, *refs):
-    mode_kernel(roll, first, pick_ref, second_ref, field_ref, None, *refs)
-
-
-def mode_product(pick, second, field, roll, start, count, third=None):
+def mode_product(picks, halves, second, field, roll, start, count, third=None):
     _, nx, ny = field.shape
     steps = count // STEP
     first = start // STEP
-    rows, rank = pick.shape
+    pick = np.concatenate(picks, 0)
+    rows = picks[0].shape[0]
     extra = 0 if third is None else 1
+    planes = [count // 2 if half else count for half in halves]
+    planes[0] += extra * STEP
+
+    def out(size):
+        return pl.BlockSpec((rows, STEP, nx), lambda i: (0, jnp.minimum(i, size // STEP - 1), 0))
 
     in_specs = [
-        pl.BlockSpec((rows, rank), lambda i: (0, 0)),
+        pl.BlockSpec(pick.shape, lambda i: (0, 0)),
         pl.BlockSpec(second.shape, lambda i: (0, 0)),
         pl.BlockSpec(memory_space=pl.ANY),
     ]
@@ -93,31 +120,31 @@
         in_specs.append(pl.BlockSpec(third.shape, lambda i: (0, 0)))
         operands.append(third)
     return pl.pallas_call(
-        functools.partial(mode_kernel if extra else plain_kernel, roll, first),
+        functools.partial(mode_kernel, roll, first, halves),
         grid=(steps + extra,),
         in_specs=in_specs,
-        out_specs=pl.BlockSpec((rows, STEP, nx), lambda i: (0, i, 0)),
-        out_shape=jax.ShapeDtypeStruct((rows, count + extra * STEP, nx), jnp.float32),
+        out_specs=[out(size) for size in planes],
+        out_shape=[jax.ShapeDtypeStruct((rows, size, nx), jnp.float32) for size in planes],
         scratch_shapes=[
-            pltpu.VMEM((2 * rows, 2 * ny), jnp.bfloat16),
+            pltpu.VMEM((2 * pick.shape[0], 2 * ny), jnp.bfloat16),
             pltpu.VMEM((count, nx, ny), jnp.float32),
             pltpu.SemaphoreType.DMA((steps,)),
         ],
         compiler_params=pltpu.CompilerParams(vmem_limit_bytes=54 * 2**20),
         cost_estimate=pl.CostEstimate(
-            flops=6 * count * nx * ny * rows,
-            bytes_accessed=4 * count * nx * (ny + rows),
+            flops=6 * count * nx * ny * pick.shape[0],
+            bytes_accessed=4 * count * nx * (ny + pick.shape[0]),
             transcendentals=0,
         ),
     )(*operands)
 
 
 def depth_kernel(third_ref, part_ref, out_ref, both_ref):
-    rank = third_ref.shape[0]
+    rank = third_ref.shape[3]
 
     @pl.when(pl.program_id(0) == 0)
     def _():
-        high, low = split(third_ref[...])
+        high, low = split(third_ref[...].reshape(-1, rank).T)
         both_ref[:rank] = high
         both_ref[rank:] = low
 
@@ -127,15 +154,16 @@
         out_ref[g] = product(both_ref[:rank], both_ref[...], value)
 
 
-def depth_product(third, part, depth):
-    n, groups, _, nx = part.shape
-    rank = third.shape[0]
+def depth_product(gathered, part, rank):
+    n, tiles, planes, _ = gathered.shape
+    _, groups, _, nx = part.shape
+    depth = planes - STEP
     step = 2 if groups % 2 == 0 else 1
     return pl.pallas_call(
         depth_kernel,
         grid=(groups // step,),
         in_specs=[
-            pl.BlockSpec((rank, n * depth), lambda i: (0, 0)),
+            pl.BlockSpec((n, tiles, STEP, rank), lambda i: (0, 0, depth // STEP, 0)),
             pl.BlockSpec((n, step, depth, nx), lambda i: (0, i, 0, 0)),
         ],
         out_specs=pl.BlockSpec((step, rank, nx), lambda i: (i, 0, 0)),
@@ -147,7 +175,7 @@
             bytes_accessed=4 * n * groups * depth * nx,
             transcendentals=0,
         ),
-    )(third, part)
+    )(gathered, part)
 
 
 def after(value, other):
@@ -163,20 +191,30 @@
     ]
 
 
-def ring_sum(parts, axis):
+def ring_steps(parts, axis):
     n = len(parts)
     half = n // 2
     mid = parts[half].shape[0] // 2
-    up, down = shifts([(parts[half][:mid], 1), (parts[half][mid:], -1)], axis)
+    moving = shifts([(parts[half][:mid], 1), (parts[half][mid:], -1)], axis)
     for d in range(half - 1, 0, -1):
+        up, down = yield moving
         if d == half - 1:
             up = jnp.concatenate([parts[d][:mid] + up, parts[d][mid:]], 0)
             down = jnp.concatenate([parts[n - d][:mid], parts[n - d][mid:] + down], 0)
         else:
             up = parts[d] + up
             down = parts[n - d] + down
-        up, down = shifts([(up, 1), (down, -1)], axis)
-    return parts[0] + up + down
+        moving = shifts([(up, 1), (down, -1)], axis)
+    up, down = yield moving
+    yield parts[0] + up + down
+
+
+def ring_sum(parts, axis):
+    steps = ring_steps(parts, axis)
+    value = next(steps)
+    for _ in range(len(parts) // 2):
+        value = steps.send(value)
+    return value
 
 
 def trade(value, axis):
@@ -209,23 +247,24 @@
     pick_f = pick([(place, part_m + v) for v in range(vert) for place in range(gy)])
     pick_m = pick([(place, within) for place in range(gy) for within in range(part_m)])
 
-    f = mode_product(pick_f, basis_second, field, share, 0, depth, third)
+    half = depth // 2
+    f, m1 = mode_product([pick_f, pick_m], (False, True), basis_second, field, share, 0, depth, third)
     second = after(basis_second, f)
     f = trade(f.reshape(vert, gy, depth + STEP, nx), "vert")
 
-    half = depth // 2
-    m = []
-    for start in (0, half):
-        part = mode_product(pick_m, second, field, share, start, half)
-        m.append(ring_sum([part[d * part_m : (d + 1) * part_m] for d in range(gy)], "gy"))
+    (m2,) = mode_product([pick_m], (False,), second, field, share, half, half)
+    m = [ring_sum([part[d * part_m : (d + 1) * part_m] for d in range(gy)], "gy") for part in (m1, m2)]
     m, f = lax.optimization_barrier((jnp.concatenate(m, 1), f))
     m = trade(m, "vert")
 
-    third = f[:, :, depth:, :rank].reshape(vert * depth, rank).T
-    f = depth_product(third, f, depth)
-    f = ring_sum([f[d] for d in range(gy)], "gy")
-    f, m = lax.optimization_barrier((f, m))
-    m = depth_product(third, m.reshape(vert, 1, depth, nx), depth)[0]
+    parts = depth_product(f, f, rank)
+    ring = ring_steps([parts[d] for d in range(gy)], "gy")
+    moving = next(ring)
+    for _ in range(gy // 2 - 2):
+        moving = ring.send(moving)
+    moving, m = lax.optimization_barrier((moving, m))
+    m = depth_product(f, m.reshape(vert, 1, depth, nx), rank)[0]
+    f = ring.send(ring.send(moving))
 
     columns = jnp.concatenate([f, m], 0)
     weights = jnp.dot(columns, first, precision=HIGHEST)

time: 154 us -> 149 us (0.968)
  Pallas kernels: 23.4 us -> 19.9 us
  starting transfers between devices: 57 us -> 54.2 us
  blocking collectives: 31.3 us -> 33.7 us
    pallas_call x3 -> x2, Pallas kernels: 19.3 us -> 14.7 us  [mode_product(): pl.pallas_call(functools.partial(mode_kernel, roll, first, halves), grid=...]
    all_to_all x2, starting transfers between devices: 17.8 us -> 13.4 us  [trade(): return lax.all_to_all(value, axis, 0, 0)]
    all_to_all x2, waiting for transfers between devices: 2.99 us -> 6.06 us  [trade(): return lax.all_to_all(value, axis, 0, 0)]
    ppermute x27, waiting for transfers between devices: 31.7 us -> 29.3 us  [shifts(): lax.ppermute(value, axis, [(i, (i + by) % n) for i in range(n)])]
    all_to_all x3, blocking collectives: 31.3 us -> 33.7 us  [trade(): return lax.all_to_all(value, axis, 0, 0)]
    ppermute x27, starting transfers between devices: 39.2 us -> 40.8 us  [shifts(): lax.ppermute(value, axis, [(i, (i + by) % n) for i in range(n)])]
    slice x4 -> x3, local copies, waits for them, and re-layouts: 3.11 us -> 2.14 us  [the longest x2 2.12 us: ring_steps(): moving = shifts([(parts[half][:mid], 1), (parts[half][mid:], -1)], axis)]
  transfers between devices with their start and end apart: 29 -> 29, of which waited for: 14 -> 15; matrix products, arithmetic and copies ran while one was open for 2% -> 2% of each run, Pallas kernels for 7% -> 4%
where the time goes in v4:
time: 149 us
  starting transfers between devices  54.2 us (36%)
  waiting for transfers between devices  35.4 us (24%)
  blocking collectives  33.7 us (23%)
  Pallas kernels  19.9 us (13%)
  local copies, waits for them, and re-layouts  2.83 us (2%)
  other arithmetic  1.6 us (1%)
    ppermute x27, starting transfers between devices, shifts(): lax.ppermute(value, axis, [(i, (i + by) % n) for i in range(n)])  40.8 us
    all_to_all x3, blocking collectives, trade(): return lax.all_to_all(value, axis, 0, 0)  33.7 us
    ppermute x27, waiting for transfers between devices, shifts(): lax.ppermute(value, axis, [(i, (i + by) % n) for i in range(n)])  29.3 us
    pallas_call x2, Pallas kernels, mode_product(): pl.pallas_call(functools.partial(mode_kernel, roll, first, halves), grid=...  14.7 us
    all_to_all x2, starting transfers between devices, trade(): return lax.all_to_all(value, axis, 0, 0)  13.4 us
    all_to_all x2, waiting for transfers between devices, trade(): return lax.all_to_all(value, axis, 0, 0)  6.06 us
    pallas_call x2, Pallas kernels, depth_product(): pl.pallas_call(depth_kernel, grid=(groups // step,), in_specs=[pl.BlockSp...  5.18 us
  transfers between devices with their start and end apart: 29, of which 15 were waited for; matrix products, arithmetic and copies ran while one was open for 2% of the time, Pallas kernels for 4%

profile of v4, /device:TPU:1, one launch (start us, length us, event | category | flops | bytes accessed | tf_op | source)
XLA Modules:
  0.0 148.8 jit_solution(10856094785975923619)
XLA Ops:
  0.0 9.3 %shard_map.64 = (f32[64,72,256]{2,1,0:T(8,128)}, f32[64,32,256]{2,1,0:T(8,128)}) custom-call(f32[128,128]{1,0:T(8,128)} %constant.21.clone.pick_ref, f32[128,128]{1,0:T(8,128)} %second_ref.2, f32[64,256,128]{2,1,0:T(8,128)} %bitcast.48, f32[64,128]{1,0:T(8,128)} %bitcast.53), custom_call_target="tpu_custom_call" | custom-call | flops 1610612736 | bytes 16777216 | tf_op jit(solution)/shard_map/pallas_call | solution.py:122
  9.3 7.7 %all-to-all-start = ((f32[8,8,72,256]{3,2,1,0:T(8,128)}), f32[8,8,72,256]{3,2,1,0:T(8,128)}, u32[]{:S(2)}, u32[]{:S(2)}) async-start(f32[8,8,72,256]{3,2,1,0:T(8,128)} %bitcast.50), calls=%async_computation | async-start | bytes 9437184 | tf_op jit(solution)/shard_map/all_to_all | solution.py:221
  18.1 3.9 %collective-permute-start.1 = (f32[4,32,256]{2,1,0:T(8,128)S(1)}, f32[4,32,256]{2,1,0:T(8,128)S(1)}, u32[]{:S(2)}, u32[]{:S(2)}) collective-permute-start(f32[4,32,256]{2,1,0:T(8,128)S(1)} %get-tuple-element.42), channel_id=1, source_target_pairs={{0,56},{8,0},{16,8},{24,16},{32,24},{40,32},{48,40},{56,48},{1,57}... | collective-permute-start | bytes 393224 | tf_op jit(solution)/shard_map/ppermute | solution.py:189
  22.0 5.4 %shard_map.65 = f32[64,32,256]{2,1,0:T(8,128)} custom-call(f32[64,128]{1,0:T(8,128)} %constant.22.clone.pick_ref, f32[128,128]{1,0:T(8,128)} %second_ref.2, f32[64,256,128]{2,1,0:T(8,128)} %bitcast.49), custom_call_target="tpu_custom_call" | custom-call | flops 402653184 | bytes 6291456 | tf_op jit(solution)/shard_map/pallas_call | solution.py:122
  28.7 2.7 %collective-permute-start.9 = (f32[4,32,256]{2,1,0:T(8,128)S(1)}, f32[4,32,256]{2,1,0:T(8,128)S(1)}, u32[]{:S(2)}, u32[]{:S(2)}) collective-permute-start(f32[4,32,256]{2,1,0:T(8,128)S(1)} %get-tuple-element.52), channel_id=1, source_target_pairs={{0,56},{8,0},{16,8},{24,16},{32,24},{40,32},{48,40},{56,48},{1,57}... | collective-permute-start | bytes 393224 | tf_op jit(solution)/shard_map/ppermute | solution.py:189
  31.5 2.7 %collective-permute-start.3 = (f32[8,32,256]{2,1,0:T(8,128)S(1)}, f32[8,32,256]{2,1,0:T(8,128)S(1)}, u32[]{:S(2)}, u32[]{:S(2)}) collective-permute-start(f32[8,32,256]{2,1,0:T(8,128)S(1)} %get-tuple-element.44), channel_id=1, source_target_pairs={{0,56},{8,0},{16,8},{24,16},{32,24},{40,32},{48,40},{56,48},{1,57}... | collective-permute-start | bytes 786440 | tf_op jit(solution)/shard_map/ppermute | solution.py:189
  34.7 2.7 %collective-permute-start.11 = (f32[8,32,256]{2,1,0:T(8,128)S(1)}, f32[8,32,256]{2,1,0:T(8,128)S(1)}, u32[]{:S(2)}, u32[]{:S(2)}) collective-permute-start(f32[8,32,256]{2,1,0:T(8,128)S(1)} %get-tuple-element.54), channel_id=1, source_target_pairs={{0,56},{8,0},{16,8},{24,16},{32,24},{40,32},{48,40},{56,48},{1,57}... | collective-permute-start | bytes 786440 | tf_op jit(solution)/shard_map/ppermute | solution.py:189
  37.4 2.2 %collective-permute-done.2 = f32[8,32,256]{2,1,0:T(8,128)S(1)} collective-permute-done((f32[8,32,256]{2,1,0:T(8,128)S(1)}, f32[8,32,256]{2,1,0:T(8,128)S(1)}, u32[]{:S(2)}, u32[]{:S(2)}) %collective-permute-start.2) | collective-permute-done | bytes 262176 | tf_op jit(solution)/shard_map/ppermute | solution.py:189
  39.7 2.7 %collective-permute-start.5 = (f32[8,32,256]{2,1,0:T(8,128)S(1)}, f32[8,32,256]{2,1,0:T(8,128)S(1)}, u32[]{:S(2)}, u32[]{:S(2)}) collective-permute-start(f32[8,32,256]{2,1,0:T(8,128)S(1)} %get-tuple-element.46), channel_id=1, source_target_pairs={{0,56},{8,0},{16,8},{24,16},{32,24},{40,32},{48,40},{56,48},{1,57}... | collective-permute-start | bytes 786440 | tf_op jit(solution)/shard_map/ppermute | solution.py:189
  42.4 2.9 %collective-permute-done.10 = f32[8,32,256]{2,1,0:T(8,128)S(1)} collective-permute-done((f32[8,32,256]{2,1,0:T(8,128)S(1)}, f32[8,32,256]{2,1,0:T(8,128)S(1)}, u32[]{:S(2)}, u32[]{:S(2)}) %collective-permute-start.10) | collective-permute-done | bytes 262176 | tf_op jit(solution)/shard_map/ppermute | solution.py:189
  45.5 2.7 %collective-permute-start.13 = (f32[8,32,256]{2,1,0:T(8,128)S(1)}, f32[8,32,256]{2,1,0:T(8,128)S(1)}, u32[]{:S(2)}, u32[]{:S(2)}) collective-permute-start(f32[8,32,256]{2,1,0:T(8,128)S(1)} %get-tuple-element.56), channel_id=1, source_target_pairs={{0,56},{8,0},{16,8},{24,16},{32,24},{40,32},{48,40},{56,48},{1,57}... | collective-permute-start | bytes 786440 | tf_op jit(solution)/shard_map/ppermute | solution.py:189
  48.1 2.8 %collective-permute-done.4 = f32[8,32,256]{2,1,0:T(8,128)S(1)} collective-permute-done((f32[8,32,256]{2,1,0:T(8,128)S(1)}, f32[8,32,256]{2,1,0:T(8,128)S(1)}, u32[]{:S(2)}, u32[]{:S(2)}) %collective-permute-start.4) | collective-permute-done | bytes 262176 | tf_op jit(solution)/shard_map/ppermute | solution.py:189
  51.3 2.7 %collective-permute-start.7 = (f32[8,32,256]{2,1,0:T(8,128)S(1)}, f32[8,32,256]{2,1,0:T(8,128)S(1)}, u32[]{:S(2)}, u32[]{:S(2)}) collective-permute-start(f32[8,32,256]{2,1,0:T(8,128)S(1)} %get-tuple-element.48), channel_id=1, source_target_pairs={{0,56},{8,0},{16,8},{24,16},{32,24},{40,32},{48,40},{56,48},{1,57}... | collective-permute-start | bytes 786440 | tf_op jit(solution)/shard_map/ppermute | solution.py:189
  53.9 2.6 %collective-permute-done.12 = f32[8,32,256]{2,1,0:T(8,128)S(1)} collective-permute-done((f32[8,32,256]{2,1,0:T(8,128)S(1)}, f32[8,32,256]{2,1,0:T(8,128)S(1)}, u32[]{:S(2)}, u32[]{:S(2)}) %collective-permute-start.12) | collective-permute-done | bytes 262176 | tf_op jit(solution)/shard_map/ppermute | solution.py:189
  56.7 2.7 %collective-permute-start.15 = (f32[8,32,256]{2,1,0:T(8,128)S(1)}, f32[8,32,256]{2,1,0:T(8,128)S(1)}, u32[]{:S(2)}, u32[]{:S(2)}) collective-permute-start(f32[8,32,256]{2,1,0:T(8,128)S(1)} %get-tuple-element.58), channel_id=1, source_target_pairs={{0,56},{8,0},{16,8},{24,16},{32,24},{40,32},{48,40},{56,48},{1,57}... | collective-permute-start | bytes 786440 | tf_op jit(solution)/shard_map/ppermute | solution.py:189
  59.4 2.8 %collective-permute-done.6 = f32[8,32,256]{2,1,0:T(8,128)S(1)} collective-permute-done((f32[8,32,256]{2,1,0:T(8,128)S(1)}, f32[8,32,256]{2,1,0:T(8,128)S(1)}, u32[]{:S(2)}, u32[]{:S(2)}) %collective-permute-start.6) | collective-permute-done | bytes 262176 | tf_op jit(solution)/shard_map/ppermute | solution.py:189
  62.2 5.6 %collective-permute-done.14 = f32[8,32,256]{2,1,0:T(8,128)S(1)} collective-permute-done((f32[8,32,256]{2,1,0:T(8,128)S(1)}, f32[8,32,256]{2,1,0:T(8,128)S(1)}, u32[]{:S(2)}, u32[]{:S(2)}) %collective-permute-start.14) | collective-permute-done | bytes 262176 | tf_op jit(solution)/shard_map/ppermute | solution.py:189
  68.7 2.9 %all-to-all-done.third_ref.part_ref = f32[8,8,72,256]{3,2,1,0:T(8,128)} async-done(((f32[8,8,72,256]{3,2,1,0:T(8,128)}), f32[8,8,72,256]{3,2,1,0:T(8,128)}, u32[]{:S(2)}, u32[]{:S(2)}) %all-to-all-start) | async-done | bytes 4718624 | tf_op jit(solution)/shard_map/all_to_all | solution.py:221
  71.5 3.9 %shard_map.66 = f32[8,128,256]{2,1,0:T(8,128)S(1)} custom-call(f32[8,8,72,256]{3,2,1,0:T(8,128)} %all-to-all-done.third_ref.part_ref, f32[8,8,72,256]{3,2,1,0:T(8,128)} %all-to-all-done.third_ref.part_ref), custom_call_target="tpu_custom_call" | custom-call | flops 805306368 | bytes 4194304 | tf_op jit(solution)/shard_map/pallas_call | solution.py:162
  75.5 3.9 %collective-permute-start.17 = (f32[64,256]{1,0:T(8,128)S(1)}, f32[64,256]{1,0:T(8,128)S(1)}, u32[]{:S(2)}, u32[]{:S(2)}) collective-permute-start(f32[64,256]{1,0:T(8,128)S(1)} %get-tuple-element.61), channel_id=1, source_target_pairs={{0,56},{8,0},{16,8},{24,16},{32,24},{40,32},{48,40},{56,48},{1,57}... | collective-permute-start | bytes 196616 | tf_op jit(solution)/shard_map/ppermute | solution.py:189
  79.5 1.6 %collective-permute-done.16 = f32[64,256]{1,0:T(8,128)S(1)} collective-permute-done((f32[64,256]{1,0:T(8,128)S(1)}, f32[64,256]{1,0:T(8,128)S(1)}, u32[]{:S(2)}, u32[]{:S(2)}) %collective-permute-start.16) | collective-permute-done | bytes 65568 | tf_op jit(solution)/shard_map/ppermute | solution.py:189
  81.2 2.8 %collective-permute-start.19 = (f32[128,256]{1,0:T(8,128)S(1)}, f32[128,256]{1,0:T(8,128)S(1)}, u32[]{:S(2)}, u32[]{:S(2)}) collective-permute-start(f32[128,256]{1,0:T(8,128)S(1)} %pad_maximum_fusion.9), channel_id=1, source_target_pairs={{0,56},{8,0},{16,8},{24,16},{32,24},{40,32},{48,40},{56,48},{1,57}... | collective-permute-start | bytes 393224 | tf_op jit(solution)/shard_map/ppermute | solution.py:189
  84.0 5.7 %all-to-all-start.1 = ((f32[8,64,256]{2,1,0:T(8,128)}), f32[8,64,256]{2,1,0:T(8,128)S(1)}, u32[]{:S(2)}, u32[]{:S(2)}) async-start(f32[8,64,256]{2,1,0:T(8,128)} %pad_maximum_fusion), calls=%async_computation.1 | async-start | bytes 1048576 | tf_op jit(solution)/shard_map/all_to_all | solution.py:221
  89.9 2.7 %collective-permute-start.21 = (f32[128,256]{1,0:T(8,128)S(1)}, f32[128,256]{1,0:T(8,128)S(1)}, u32[]{:S(2)}, u32[]{:S(2)}) collective-permute-start(f32[128,256]{1,0:T(8,128)S(1)} %get-tuple-element.65), channel_id=1, source_target_pairs={{0,56},{8,0},{16,8},{24,16},{32,24},{40,32},{48,40},{56,48},{1,57}... | collective-permute-start | bytes 393224 | tf_op jit(solution)/shard_map/ppermute | solution.py:189
  92.5 3.5 %collective-permute-done.20 = f32[128,256]{1,0:T(8,128)S(1)} collective-permute-done((f32[128,256]{1,0:T(8,128)S(1)}, f32[128,256]{1,0:T(8,128)S(1)}, u32[]{:S(2)}, u32[]{:S(2)}) %collective-permute-start.20) | collective-permute-done | bytes 131104 | tf_op jit(solution)/shard_map/ppermute | solution.py:189
  96.0 3.2 %all-to-all-done.1 = f32[8,64,256]{2,1,0:T(8,128)S(1)} async-done(((f32[8,64,256]{2,1,0:T(8,128)}), f32[8,64,256]{2,1,0:T(8,128)S(1)}, u32[]{:S(2)}, u32[]{:S(2)}) %all-to-all-start.1) | async-done | bytes 524320 | tf_op jit(solution)/shard_map/all_to_all | solution.py:221
  99.4 2.7 %collective-permute-start.23 = (f32[128,256]{1,0:T(8,128)S(1)}, f32[128,256]{1,0:T(8,128)S(1)}, u32[]{:S(2)}, u32[]{:S(2)}) collective-permute-start(f32[128,256]{1,0:T(8,128)S(1)} %get-tuple-element.70), channel_id=1, source_target_pairs={{0,56},{8,0},{16,8},{24,16},{32,24},{40,32},{48,40},{56,48},{1,57}... | collective-permute-start | bytes 393224 | tf_op jit(solution)/shard_map/ppermute | solution.py:189
  106.4 2.4 %collective-permute-start.25 = (f32[256,128]{1,0:T(8,128)S(1)}, f32[256,128]{1,0:T(8,128)S(1)}, u32[]{:S(2)}, u32[]{:S(2)}) collective-permute-start(f32[256,128]{1,0:T(8,128)S(1)} %fusion.2), channel_id=1, source_target_pairs={{0,128},{64,192},{128,0},{192,64},{1,129},{65,193},{129,1},{193,65... | collective-permute-start | bytes 393224 | tf_op jit(solution)/shard_map/ppermute | solution.py:189
  110.2 2.9 %collective-permute-done.25 = f32[256,128]{1,0:T(8,128)S(1)} collective-permute-done((f32[256,128]{1,0:T(8,128)S(1)}, f32[256,128]{1,0:T(8,128)S(1)}, u32[]{:S(2)}, u32[]{:S(2)}) %collective-permute-start.25) | collective-permute-done | bytes 131104 | tf_op jit(solution)/shard_map/ppermute | solution.py:189
  114.4 10.0 %all_to_all.25 = f32[8,32,128]{2,1,0:T(8,128)S(1)} all-to-all(f32[8,32,128]{2,1,0:T(8,128)S(1)} %bitcast.51), channel_id=1, replica_groups=mesh['gx'=4,'gy'=8,'vert'=8] {'vert'}, dimensions={0} | all-to-all | bytes 262144 | tf_op jit(solution)/shard_map/all_to_all | solution.py:221
  124.5 13.6 %all_to_all.26 = f32[8,32,128]{2,1,0:T(8,128)S(1)} all-to-all(f32[8,32,128]{2,1,0:T(8,128)S(1)} %broadcast_in_dim.4), channel_id=1, replica_groups=mesh['gx'=4,'gy'=8,'vert'=8] {'gy'}, dimensions={0} | all-to-all | bytes 262144 | tf_op jit(solution)/shard_map/all_to_all | solution.py:221
  138.1 10.0 %all_to_all.27 = f32[8,32,128]{2,1,0:T(8,128)S(1)} all-to-all(f32[8,32,128]{2,1,0:T(8,128)S(1)} %broadcast_in_dim.5), channel_id=1, replica_groups=mesh['gx'=4,'gy'=8,'vert'=8] {'vert'}, dimensions={0} | all-to-all | bytes 262144 | tf_op jit(solution)/shard_map/all_to_all | solution.py:221
  (67 shorter events, 12.9 us)
Async XLA Ops:
  0.0 104.7 %copy-start = (f32[1024,128]{1,0:T(8,128)S(1)}, f32[1024,128]{1,0:T(8,128)}, u32[]{:S(2)}) copy-start(f32[1024,128]{1,0:T(8,128)} %param.7) | copy-start | bytes 1572868
  9.3 62.2 %all-to-all-start = ((f32[8,8,72,256]{3,2,1,0:T(8,128)}), f32[8,8,72,256]{3,2,1,0:T(8,128)}, u32[]{:S(2)}, u32[]{:S(2)}) async-start(f32[8,8,72,256]{3,2,1,0:T(8,128)} %bitcast.50), calls=%async_computation | async-start | bytes 9437184 | tf_op jit(solution)/shard_map/all_to_all | solution.py:221
  18.0 13.4 %copy-start.2 = (f32[64,32,256]{2,1,0:T(8,128)S(1)}, f32[64,32,256]{2,1,0:T(8,128)}, u32[]{:S(2)}) copy-start(f32[64,32,256]{2,1,0:T(8,128)} %get-tuple-element.40) | copy-start | bytes 6291460
  18.0 13.4 %collective-permute-start = (f32[4,32,256]{2,1,0:T(8,128)S(1)}, f32[4,32,256]{2,1,0:T(8,128)S(1)}, u32[]{:S(2)}, u32[]{:S(2)}) collective-permute-start(f32[4,32,256]{2,1,0:T(8,128)S(1)} %get-tuple-element.41), channel_id=1, source_target_pairs={{0,8},{8,16},{16,24},{24,32},{32,40},{40,48},{48,56},{56,0},{1,9},... | collective-permute-start | bytes 393224 | tf_op jit(solution)/shard_map/ppermute | solution.py:189
  18.1 13.3 %collective-permute-start.1 = (f32[4,32,256]{2,1,0:T(8,128)S(1)}, f32[4,32,256]{2,1,0:T(8,128)S(1)}, u32[]{:S(2)}, u32[]{:S(2)}) collective-permute-start(f32[4,32,256]{2,1,0:T(8,128)S(1)} %get-tuple-element.42), channel_id=1, source_target_pairs={{0,56},{8,0},{16,8},{24,16},{32,24},{40,32},{48,40},{56,48},{1,57}... | collective-permute-start | bytes 393224 | tf_op jit(solution)/shard_map/ppermute | solution.py:189
  27.4 7.1 %copy-start.1 = (f32[64,32,256]{2,1,0:T(8,128)S(1)}, f32[64,32,256]{2,1,0:T(8,128)}, u32[]{:S(2)}) copy-start(f32[64,32,256]{2,1,0:T(8,128)} %shard_map.65) | copy-start | bytes 6291460
  28.6 5.9 %collective-permute-start.8 = (f32[4,32,256]{2,1,0:T(8,128)S(1)}, f32[4,32,256]{2,1,0:T(8,128)S(1)}, u32[]{:S(2)}, u32[]{:S(2)}) collective-permute-start(f32[4,32,256]{2,1,0:T(8,128)S(1)} %get-tuple-element.51), channel_id=1, source_target_pairs={{0,8},{8,16},{16,24},{24,32},{32,40},{40,48},{48,56},{56,0},{1,9},... | collective-permute-start | bytes 393224 | tf_op jit(solution)/shard_map/ppermute | solution.py:189
  28.7 5.8 %collective-permute-start.9 = (f32[4,32,256]{2,1,0:T(8,128)S(1)}, f32[4,32,256]{2,1,0:T(8,128)S(1)}, u32[]{:S(2)}, u32[]{:S(2)}) collective-permute-start(f32[4,32,256]{2,1,0:T(8,128)S(1)} %get-tuple-element.52), channel_id=1, source_target_pairs={{0,56},{8,0},{16,8},{24,16},{32,24},{40,32},{48,40},{56,48},{1,57}... | collective-permute-start | bytes 393224 | tf_op jit(solution)/shard_map/ppermute | solution.py:189
  31.5 8.1 %collective-permute-start.2 = (f32[8,32,256]{2,1,0:T(8,128)S(1)}, f32[8,32,256]{2,1,0:T(8,128)S(1)}, u32[]{:S(2)}, u32[]{:S(2)}) collective-permute-start(f32[8,32,256]{2,1,0:T(8,128)S(1)} %get-tuple-element.43), channel_id=1, source_target_pairs={{0,8},{8,16},{16,24},{24,32},{32,40},{40,48},{48,56},{56,0},{1,9},... | collective-permute-start | bytes 786440 | tf_op jit(solution)/shard_map/ppermute | solution.py:189
  31.5 8.0 %collective-permute-start.3 = (f32[8,32,256]{2,1,0:T(8,128)S(1)}, f32[8,32,256]{2,1,0:T(8,128)S(1)}, u32[]{:S(2)}, u32[]{:S(2)}) collective-permute-start(f32[8,32,256]{2,1,0:T(8,128)S(1)} %get-tuple-element.44), channel_id=1, source_target_pairs={{0,56},{8,0},{16,8},{24,16},{32,24},{40,32},{48,40},{56,48},{1,57}... | collective-permute-start | bytes 786440 | tf_op jit(solution)/shard_map/ppermute | solution.py:189
  34.6 10.7 %collective-permute-start.10 = (f32[8,32,256]{2,1,0:T(8,128)S(1)}, f32[8,32,256]{2,1,0:T(8,128)S(1)}, u32[]{:S(2)}, u32[]{:S(2)}) collective-permute-start(f32[8,32,256]{2,1,0:T(8,128)S(1)} %get-tuple-element.53), channel_id=1, source_target_pairs={{0,8},{8,16},{16,24},{24,32},{32,40},{40,48},{48,56},{56,0},{1,9},... | collective-permute-start | bytes 786440 | tf_op jit(solution)/shard_map/ppermute | solution.py:189
  34.7 10.6 %collective-permute-start.11 = (f32[8,32,256]{2,1,0:T(8,128)S(1)}, f32[8,32,256]{2,1,0:T(8,128)S(1)}, u32[]{:S(2)}, u32[]{:S(2)}) collective-permute-start(f32[8,32,256]{2,1,0:T(8,128)S(1)} %get-tuple-element.54), channel_id=1, source_target_pairs={{0,56},{8,0},{16,8},{24,16},{32,24},{40,32},{48,40},{56,48},{1,57}... | collective-permute-start | bytes 786440 | tf_op jit(solution)/shard_map/ppermute | solution.py:189
  39.6 11.3 %collective-permute-start.4 = (f32[8,32,256]{2,1,0:T(8,128)S(1)}, f32[8,32,256]{2,1,0:T(8,128)S(1)}, u32[]{:S(2)}, u32[]{:S(2)}) collective-permute-start(f32[8,32,256]{2,1,0:T(8,128)S(1)} %get-tuple-element.45), channel_id=1, source_target_pairs={{0,8},{8,16},{16,24},{24,32},{32,40},{40,48},{48,56},{56,0},{1,9},... | collective-permute-start | bytes 786440 | tf_op jit(solution)/shard_map/ppermute | solution.py:189
  39.7 11.2 %collective-permute-start.5 = (f32[8,32,256]{2,1,0:T(8,128)S(1)}, f32[8,32,256]{2,1,0:T(8,128)S(1)}, u32[]{:S(2)}, u32[]{:S(2)}) collective-permute-start(f32[8,32,256]{2,1,0:T(8,128)S(1)} %get-tuple-element.46), channel_id=1, source_target_pairs={{0,56},{8,0},{16,8},{24,16},{32,24},{40,32},{48,40},{56,48},{1,57}... | collective-permute-start | bytes 786440 | tf_op jit(solution)/shard_map/ppermute | solution.py:189
  45.4 11.2 %collective-permute-start.12 = (f32[8,32,256]{2,1,0:T(8,128)S(1)}, f32[8,32,256]{2,1,0:T(8,128)S(1)}, u32[]{:S(2)}, u32[]{:S(2)}) collective-permute-start(f32[8,32,256]{2,1,0:T(8,128)S(1)} %get-tuple-element.55), channel_id=1, source_target_pairs={{0,8},{8,16},{16,24},{24,32},{32,40},{40,48},{48,56},{56,0},{1,9},... | collective-permute-start | bytes 786440 | tf_op jit(solution)/shard_map/ppermute | solution.py:189
  45.5 11.1 %collective-permute-start.13 = (f32[8,32,256]{2,1,0:T(8,128)S(1)}, f32[8,32,256]{2,1,0:T(8,128)S(1)}, u32[]{:S(2)}, u32[]{:S(2)}) collective-permute-start(f32[8,32,256]{2,1,0:T(8,128)S(1)} %get-tuple-element.56), channel_id=1, source_target_pairs={{0,56},{8,0},{16,8},{24,16},{32,24},{40,32},{48,40},{56,48},{1,57}... | collective-permute-start | bytes 786440 | tf_op jit(solution)/shard_map/ppermute | solution.py:189
  51.0 11.2 %collective-permute-start.6 = (f32[8,32,256]{2,1,0:T(8,128)S(1)}, f32[8,32,256]{2,1,0:T(8,128)S(1)}, u32[]{:S(2)}, u32[]{:S(2)}) collective-permute-start(f32[8,32,256]{2,1,0:T(8,128)S(1)} %get-tuple-element.47), channel_id=1, source_target_pairs={{0,8},{8,16},{16,24},{24,32},{32,40},{40,48},{48,56},{56,0},{1,9},... | collective-permute-start | bytes 786440 | tf_op jit(solution)/shard_map/ppermute | solution.py:189
  51.3 10.9 %collective-permute-start.7 = (f32[8,32,256]{2,1,0:T(8,128)S(1)}, f32[8,32,256]{2,1,0:T(8,128)S(1)}, u32[]{:S(2)}, u32[]{:S(2)}) collective-permute-start(f32[8,32,256]{2,1,0:T(8,128)S(1)} %get-tuple-element.48), channel_id=1, source_target_pairs={{0,56},{8,0},{16,8},{24,16},{32,24},{40,32},{48,40},{56,48},{1,57}... | collective-permute-start | bytes 786440 | tf_op jit(solution)/shard_map/ppermute | solution.py:189
  56.6 11.2 %collective-permute-start.14 = (f32[8,32,256]{2,1,0:T(8,128)S(1)}, f32[8,32,256]{2,1,0:T(8,128)S(1)}, u32[]{:S(2)}, u32[]{:S(2)}) collective-permute-start(f32[8,32,256]{2,1,0:T(8,128)S(1)} %get-tuple-element.57), channel_id=1, source_target_pairs={{0,8},{8,16},{16,24},{24,32},{32,40},{40,48},{48,56},{56,0},{1,9},... | collective-permute-start | bytes 786440 | tf_op jit(solution)/shard_map/ppermute | solution.py:189
  56.7 11.1 %collective-permute-start.15 = (f32[8,32,256]{2,1,0:T(8,128)S(1)}, f32[8,32,256]{2,1,0:T(8,128)S(1)}, u32[]{:S(2)}, u32[]{:S(2)}) collective-permute-start(f32[8,32,256]{2,1,0:T(8,128)S(1)} %get-tuple-element.58), channel_id=1, source_target_pairs={{0,56},{8,0},{16,8},{24,16},{32,24},{40,32},{48,40},{56,48},{1,57}... | collective-permute-start | bytes 786440 | tf_op jit(solution)/shard_map/ppermute | solution.py:189
  75.4 5.6 %collective-permute-start.16 = (f32[64,256]{1,0:T(8,128)S(1)}, f32[64,256]{1,0:T(8,128)S(1)}, u32[]{:S(2)}, u32[]{:S(2)}) collective-permute-start(f32[64,256]{1,0:T(8,128)S(1)} %get-tuple-element.60), channel_id=1, source_target_pairs={{0,8},{8,16},{16,24},{24,32},{32,40},{40,48},{48,56},{56,0},{1,9},... | collective-permute-start | bytes 196616 | tf_op jit(solution)/shard_map/ppermute | solution.py:189
  75.5 5.5 %collective-permute-start.17 = (f32[64,256]{1,0:T(8,128)S(1)}, f32[64,256]{1,0:T(8,128)S(1)}, u32[]{:S(2)}, u32[]{:S(2)}) collective-permute-start(f32[64,256]{1,0:T(8,128)S(1)} %get-tuple-element.61), channel_id=1, source_target_pairs={{0,56},{8,0},{16,8},{24,16},{32,24},{40,32},{48,40},{56,48},{1,57}... | collective-permute-start | bytes 196616 | tf_op jit(solution)/shard_map/ppermute | solution.py:189
  81.1 8.6 %collective-permute-start.18 = (f32[128,256]{1,0:T(8,128)S(1)}, f32[128,256]{1,0:T(8,128)S(1)}, u32[]{:S(2)}, u32[]{:S(2)}) collective-permute-start(f32[128,256]{1,0:T(8,128)S(1)} %pad_maximum_fusion.8), channel_id=1, source_target_pairs={{0,8},{8,16},{16,24},{24,32},{32,40},{40,48},{48,56},{56,0},{1,9},... | collective-permute-start | bytes 393224 | tf_op jit(solution)/shard_map/ppermute | solution.py:189
  81.2 8.5 %collective-permute-start.19 = (f32[128,256]{1,0:T(8,128)S(1)}, f32[128,256]{1,0:T(8,128)S(1)}, u32[]{:S(2)}, u32[]{:S(2)}) collective-permute-start(f32[128,256]{1,0:T(8,128)S(1)} %pad_maximum_fusion.9), channel_id=1, source_target_pairs={{0,56},{8,0},{16,8},{24,16},{32,24},{40,32},{48,40},{56,48},{1,57}... | collective-permute-start | bytes 393224 | tf_op jit(solution)/shard_map/ppermute | solution.py:189
  84.0 15.2 %all-to-all-start.1 = ((f32[8,64,256]{2,1,0:T(8,128)}), f32[8,64,256]{2,1,0:T(8,128)S(1)}, u32[]{:S(2)}, u32[]{:S(2)}) async-start(f32[8,64,256]{2,1,0:T(8,128)} %pad_maximum_fusion), calls=%async_computation.1 | async-start | bytes 1048576 | tf_op jit(solution)/shard_map/all_to_all | solution.py:221
  89.8 6.3 %collective-permute-start.20 = (f32[128,256]{1,0:T(8,128)S(1)}, f32[128,256]{1,0:T(8,128)S(1)}, u32[]{:S(2)}, u32[]{:S(2)}) collective-permute-start(f32[128,256]{1,0:T(8,128)S(1)} %get-tuple-element.64), channel_id=1, source_target_pairs={{0,8},{8,16},{16,24},{24,32},{32,40},{40,48},{48,56},{56,0},{1,9},... | collective-permute-start | bytes 393224 | tf_op jit(solution)/shard_map/ppermute | solution.py:189
  89.9 6.2 %collective-permute-start.21 = (f32[128,256]{1,0:T(8,128)S(1)}, f32[128,256]{1,0:T(8,128)S(1)}, u32[]{:S(2)}, u32[]{:S(2)}) collective-permute-start(f32[128,256]{1,0:T(8,128)S(1)} %get-tuple-element.65), channel_id=1, source_target_pairs={{0,56},{8,0},{16,8},{24,16},{32,24},{40,32},{48,40},{56,48},{1,57}... | collective-permute-start | bytes 393224 | tf_op jit(solution)/shard_map/ppermute | solution.py:189
  99.3 5.4 %collective-permute-start.22 = (f32[128,256]{1,0:T(8,128)S(1)}, f32[128,256]{1,0:T(8,128)S(1)}, u32[]{:S(2)}, u32[]{:S(2)}) collective-permute-start(f32[128,256]{1,0:T(8,128)S(1)} %get-tuple-element.69), channel_id=1, source_target_pairs={{0,8},{8,16},{16,24},{24,32},{32,40},{40,48},{48,56},{56,0},{1,9},... | collective-permute-start | bytes 393224 | tf_op jit(solution)/shard_map/ppermute | solution.py:189
  99.4 5.3 %collective-permute-start.23 = (f32[128,256]{1,0:T(8,128)S(1)}, f32[128,256]{1,0:T(8,128)S(1)}, u32[]{:S(2)}, u32[]{:S(2)}) collective-permute-start(f32[128,256]{1,0:T(8,128)S(1)} %get-tuple-element.70), channel_id=1, source_target_pairs={{0,56},{8,0},{16,8},{24,16},{32,24},{40,32},{48,40},{56,48},{1,57}... | collective-permute-start | bytes 393224 | tf_op jit(solution)/shard_map/ppermute | solution.py:189
  105.1 5.1 %collective-permute-start.24 = (f32[256,128]{1,0:T(8,128)S(1)}, f32[256,128]{1,0:T(8,128)S(1)}, u32[]{:S(2)}, u32[]{:S(2)}) collective-permute-start(f32[256,128]{1,0:T(8,128)S(1)} %fusion.2), channel_id=1, source_target_pairs={{0,64},{64,128},{128,192},{192,0},{1,65},{65,129},{129,193},{193,1... | collective-permute-start | bytes 393224 | tf_op jit(solution)/shard_map/ppermute | solution.py:189
  106.4 6.7 %collective-permute-start.25 = (f32[256,128]{1,0:T(8,128)S(1)}, f32[256,128]{1,0:T(8,128)S(1)}, u32[]{:S(2)}, u32[]{:S(2)}) collective-permute-start(f32[256,128]{1,0:T(8,128)S(1)} %fusion.2), channel_id=1, source_target_pairs={{0,128},{64,192},{128,0},{192,64},{1,129},{65,193},{129,1},{193,65... | collective-permute-start | bytes 393224 | tf_op jit(solution)/shard_map/ppermute | solution.py:189
  108.9 4.9 %collective-permute-start.26 = (f32[256,128]{1,0:T(8,128)S(1)}, f32[256,128]{1,0:T(8,128)S(1)}, u32[]{:S(2)}, u32[]{:S(2)}) collective-permute-start(f32[256,128]{1,0:T(8,128)S(1)} %fusion.2), channel_id=1, source_target_pairs={{0,192},{64,0},{128,64},{192,128},{1,193},{65,1},{129,65},{193,129... | collective-permute-start | bytes 393224 | tf_op jit(solution)/shard_map/ppermute | solution.py:189

commit v5 on v4

--- a/solution.py
+++ b/solution.py
@@ -11,7 +11,7 @@
 HIGHEST = lax.Precision.HIGHEST
 NT = (((1,), (1,)), ((), ()))
 NN = (((1,), (0,)), ((), ()))
-VMEM_LIMIT = 20 * 2**20
+VMEM_LIMIT = 8 * 2**20
 STEP = 8
 SETS = 8
 
@@ -97,7 +97,7 @@
             out_ref[r, :, rank:] = third_ref[g * STEP : (g + 1) * STEP, :]
 
 
-def mode_product(picks, halves, second, field, roll, start, count, third=None):
+def mode_product(picks, halves, second, field, roll, start, count, limit, third=None):
     _, nx, ny = field.shape
     steps = count // STEP
     first = start // STEP
@@ -130,7 +130,7 @@
             pltpu.VMEM((count, nx, ny), jnp.float32),
             pltpu.SemaphoreType.DMA((steps,)),
         ],
-        compiler_params=pltpu.CompilerParams(vmem_limit_bytes=54 * 2**20),
+        compiler_params=pltpu.CompilerParams(vmem_limit_bytes=limit * 2**20),
         cost_estimate=pl.CostEstimate(
             flops=6 * count * nx * ny * pick.shape[0],
             bytes_accessed=4 * count * nx * (ny + pick.shape[0]),
@@ -178,10 +178,6 @@
     )(gathered, part)
 
 
-def after(value, other):
-    return lax.optimization_barrier((value, other))[0]
-
-
 def shifts(moves, axis):
     n = lax.axis_size(axis)
     values = lax.optimization_barrier([value for value, _ in moves])
@@ -248,11 +244,11 @@
     pick_m = pick([(place, within) for place in range(gy) for within in range(part_m)])
 
     half = depth // 2
-    f, m1 = mode_product([pick_f, pick_m], (False, True), basis_second, field, share, 0, depth, third)
-    second = after(basis_second, f)
+    f, m1 = mode_product([pick_f, pick_m], (False, True), basis_second, field, share, 0, depth, 54, third)
+    second, f = lax.optimization_barrier((basis_second, f))
     f = trade(f.reshape(vert, gy, depth + STEP, nx), "vert")
 
-    (m2,) = mode_product([pick_m], (False,), second, field, share, half, half)
+    (m2,) = mode_product([pick_m], (False,), second, field, share, half, half, 46)
     m = [ring_sum([part[d * part_m : (d + 1) * part_m] for d in range(gy)], "gy") for part in (m1, m2)]
     m, f = lax.optimization_barrier((jnp.concatenate(m, 1), f))
     m = trade(m, "vert")

time: 149 us -> 149 us (level)
  waiting for transfers between devices: 35.4 us -> 38.3 us
  Pallas kernels: 19.9 us -> 18 us
    all_to_all x2, waiting for transfers between devices: 6.06 us -> 8.96 us  [trade(): return lax.all_to_all(value, axis, 0, 0)]
    pallas_call x2, Pallas kernels: 14.7 us -> 12.9 us  [mode_product(): pl.pallas_call(functools.partial(mode_kernel, roll, first, halves), grid=...]
  transfers between devices with their start and end apart: 29 -> 29, of which waited for: 15 -> 15; matrix products, arithmetic and copies ran while one was open for 2% -> 2% of each run, Pallas kernels for 4% -> 3%
where the time goes in v5:
time: 149 us
  starting transfers between devices  54.3 us (36%)
  waiting for transfers between devices  38.3 us (26%)
  blocking collectives  33.7 us (23%)
  Pallas kernels  18 us (12%)
  local copies, waits for them, and re-layouts  1.72 us (1%)
  other arithmetic  1.61 us (1%)
    ppermute x27, starting transfers between devices, shifts(): lax.ppermute(value, axis, [(i, (i + by) % n) for i in range(n)])  40.8 us
    all_to_all x3, blocking collectives, trade(): return lax.all_to_all(value, axis, 0, 0)  33.7 us
    ppermute x27, waiting for transfers between devices, shifts(): lax.ppermute(value, axis, [(i, (i + by) % n) for i in range(n)])  29.3 us
    all_to_all x2, starting transfers between devices, trade(): return lax.all_to_all(value, axis, 0, 0)  13.5 us
    pallas_call x2, Pallas kernels, mode_product(): pl.pallas_call(functools.partial(mode_kernel, roll, first, halves), grid=...  12.9 us
    all_to_all x2, waiting for transfers between devices, trade(): return lax.all_to_all(value, axis, 0, 0)  8.96 us
    pallas_call x2, Pallas kernels, depth_product(): pl.pallas_call(depth_kernel, grid=(groups // step,), in_specs=[pl.BlockSp...  5.17 us
  transfers between devices with their start and end apart: 29, of which 15 were waited for; matrix products, arithmetic and copies ran while one was open for 2% of the time, Pallas kernels for 3%

profile of v5, /device:TPU:1, one launch (start us, length us, event | category | flops | bytes accessed | tf_op | source)
XLA Modules:
  0.0 149.0 jit_solution(4065347338414725)
XLA Ops:
  0.0 9.3 %shard_map.64 = (f32[64,72,256]{2,1,0:T(8,128)}, f32[64,32,256]{2,1,0:T(8,128)}) custom-call(f32[128,128]{1,0:T(8,128)} %constant.21.clone.pick_ref, f32[128,128]{1,0:T(8,128)} %second_ref.2, f32[64,256,128]{2,1,0:T(8,128)} %bitcast.48, f32[64,128]{1,0:T(8,128)} %bitcast.53), custom_call_target="tpu_custom_call" | custom-call | flops 1610612736 | bytes 16777216 | tf_op jit(solution)/shard_map/pallas_call | solution.py:122
  9.3 7.8 %all-to-all-start = ((f32[8,8,72,256]{3,2,1,0:T(8,128)}), f32[8,8,72,256]{3,2,1,0:T(8,128)}, u32[]{:S(2)}, u32[]{:S(2)}) async-start(f32[8,8,72,256]{3,2,1,0:T(8,128)} %bitcast.50), calls=%async_computation | async-start | bytes 9437184 | tf_op jit(solution)/shard_map/all_to_all | solution.py:217
  18.2 4.0 %collective-permute-start.1 = (f32[4,32,256]{2,1,0:T(8,128)S(1)}, f32[4,32,256]{2,1,0:T(8,128)S(1)}, u32[]{:S(2)}, u32[]{:S(2)}) collective-permute-start(f32[4,32,256]{2,1,0:T(8,128)S(1)} %get-tuple-element.43), channel_id=1, source_target_pairs={{0,56},{8,0},{16,8},{24,16},{32,24},{40,32},{48,40},{56,48},{1,57}... | collective-permute-start | bytes 393224 | tf_op jit(solution)/shard_map/ppermute | solution.py:185
  22.2 3.6 %shard_map.65 = f32[64,32,256]{2,1,0:T(8,128)S(1)} custom-call(f32[64,128]{1,0:T(8,128)S(1)} %copy-done.2, f32[128,128]{1,0:T(8,128)S(1)} %copy-done.1, f32[64,256,128]{2,1,0:T(8,128)} %bitcast.49), custom_call_target="tpu_custom_call" | custom-call | flops 402653184 | bytes 6291456 | tf_op jit(solution)/shard_map/pallas_call | solution.py:122
  25.9 2.7 %collective-permute-start.9 = (f32[4,32,256]{2,1,0:T(8,128)S(1)}, f32[4,32,256]{2,1,0:T(8,128)S(1)}, u32[]{:S(2)}, u32[]{:S(2)}) collective-permute-start(f32[4,32,256]{2,1,0:T(8,128)S(1)} %get-tuple-element.53), channel_id=1, source_target_pairs={{0,56},{8,0},{16,8},{24,16},{32,24},{40,32},{48,40},{56,48},{1,57}... | collective-permute-start | bytes 393224 | tf_op jit(solution)/shard_map/ppermute | solution.py:185
  28.8 2.7 %collective-permute-start.3 = (f32[8,32,256]{2,1,0:T(8,128)S(1)}, f32[8,32,256]{2,1,0:T(8,128)S(1)}, u32[]{:S(2)}, u32[]{:S(2)}) collective-permute-start(f32[8,32,256]{2,1,0:T(8,128)S(1)} %get-tuple-element.45), channel_id=1, source_target_pairs={{0,56},{8,0},{16,8},{24,16},{32,24},{40,32},{48,40},{56,48},{1,57}... | collective-permute-start | bytes 786440 | tf_op jit(solution)/shard_map/ppermute | solution.py:185
  32.1 2.7 %collective-permute-start.11 = (f32[8,32,256]{2,1,0:T(8,128)S(1)}, f32[8,32,256]{2,1,0:T(8,128)S(1)}, u32[]{:S(2)}, u32[]{:S(2)}) collective-permute-start(f32[8,32,256]{2,1,0:T(8,128)S(1)} %get-tuple-element.55), channel_id=1, source_target_pairs={{0,56},{8,0},{16,8},{24,16},{32,24},{40,32},{48,40},{56,48},{1,57}... | collective-permute-start | bytes 786440 | tf_op jit(solution)/shard_map/ppermute | solution.py:185
  34.7 2.1 %collective-permute-done.2 = f32[8,32,256]{2,1,0:T(8,128)S(1)} collective-permute-done((f32[8,32,256]{2,1,0:T(8,128)S(1)}, f32[8,32,256]{2,1,0:T(8,128)S(1)}, u32[]{:S(2)}, u32[]{:S(2)}) %collective-permute-start.2) | collective-permute-done | bytes 262176 | tf_op jit(solution)/shard_map/ppermute | solution.py:185
  37.0 2.7 %collective-permute-start.5 = (f32[8,32,256]{2,1,0:T(8,128)S(1)}, f32[8,32,256]{2,1,0:T(8,128)S(1)}, u32[]{:S(2)}, u32[]{:S(2)}) collective-permute-start(f32[8,32,256]{2,1,0:T(8,128)S(1)} %get-tuple-element.47), channel_id=1, source_target_pairs={{0,56},{8,0},{16,8},{24,16},{32,24},{40,32},{48,40},{56,48},{1,57}... | collective-permute-start | bytes 786440 | tf_op jit(solution)/shard_map/ppermute | solution.py:185
  39.6 2.9 %collective-permute-done.10 = f32[8,32,256]{2,1,0:T(8,128)S(1)} collective-permute-done((f32[8,32,256]{2,1,0:T(8,128)S(1)}, f32[8,32,256]{2,1,0:T(8,128)S(1)}, u32[]{:S(2)}, u32[]{:S(2)}) %collective-permute-start.10) | collective-permute-done | bytes 262176 | tf_op jit(solution)/shard_map/ppermute | solution.py:185
  42.7 2.7 %collective-permute-start.13 = (f32[8,32,256]{2,1,0:T(8,128)S(1)}, f32[8,32,256]{2,1,0:T(8,128)S(1)}, u32[]{:S(2)}, u32[]{:S(2)}) collective-permute-start(f32[8,32,256]{2,1,0:T(8,128)S(1)} %get-tuple-element.57), channel_id=1, source_target_pairs={{0,56},{8,0},{16,8},{24,16},{32,24},{40,32},{48,40},{56,48},{1,57}... | collective-permute-start | bytes 786440 | tf_op jit(solution)/shard_map/ppermute | solution.py:185
  45.4 2.8 %collective-permute-done.4 = f32[8,32,256]{2,1,0:T(8,128)S(1)} collective-permute-done((f32[8,32,256]{2,1,0:T(8,128)S(1)}, f32[8,32,256]{2,1,0:T(8,128)S(1)}, u32[]{:S(2)}, u32[]{:S(2)}) %collective-permute-start.4) | collective-permute-done | bytes 262176 | tf_op jit(solution)/shard_map/ppermute | solution.py:185
  48.5 2.7 %collective-permute-start.7 = (f32[8,32,256]{2,1,0:T(8,128)S(1)}, f32[8,32,256]{2,1,0:T(8,128)S(1)}, u32[]{:S(2)}, u32[]{:S(2)}) collective-permute-start(f32[8,32,256]{2,1,0:T(8,128)S(1)} %get-tuple-element.49), channel_id=1, source_target_pairs={{0,56},{8,0},{16,8},{24,16},{32,24},{40,32},{48,40},{56,48},{1,57}... | collective-permute-start | bytes 786440 | tf_op jit(solution)/shard_map/ppermute | solution.py:185
  51.2 2.6 %collective-permute-done.12 = f32[8,32,256]{2,1,0:T(8,128)S(1)} collective-permute-done((f32[8,32,256]{2,1,0:T(8,128)S(1)}, f32[8,32,256]{2,1,0:T(8,128)S(1)}, u32[]{:S(2)}, u32[]{:S(2)}) %collective-permute-start.12) | collective-permute-done | bytes 262176 | tf_op jit(solution)/shard_map/ppermute | solution.py:185
  53.9 2.7 %collective-permute-start.15 = (f32[8,32,256]{2,1,0:T(8,128)S(1)}, f32[8,32,256]{2,1,0:T(8,128)S(1)}, u32[]{:S(2)}, u32[]{:S(2)}) collective-permute-start(f32[8,32,256]{2,1,0:T(8,128)S(1)} %get-tuple-element.59), channel_id=1, source_target_pairs={{0,56},{8,0},{16,8},{24,16},{32,24},{40,32},{48,40},{56,48},{1,57}... | collective-permute-start | bytes 786440 | tf_op jit(solution)/shard_map/ppermute | solution.py:185
  56.6 2.7 %collective-permute-done.6 = f32[8,32,256]{2,1,0:T(8,128)S(1)} collective-permute-done((f32[8,32,256]{2,1,0:T(8,128)S(1)}, f32[8,32,256]{2,1,0:T(8,128)S(1)}, u32[]{:S(2)}, u32[]{:S(2)}) %collective-permute-start.6) | collective-permute-done | bytes 262176 | tf_op jit(solution)/shard_map/ppermute | solution.py:185
  59.3 5.7 %collective-permute-done.14 = f32[8,32,256]{2,1,0:T(8,128)S(1)} collective-permute-done((f32[8,32,256]{2,1,0:T(8,128)S(1)}, f32[8,32,256]{2,1,0:T(8,128)S(1)}, u32[]{:S(2)}, u32[]{:S(2)}) %collective-permute-start.14) | collective-permute-done | bytes 262176 | tf_op jit(solution)/shard_map/ppermute | solution.py:185
  65.9 5.8 %all-to-all-done.third_ref.part_ref = f32[8,8,72,256]{3,2,1,0:T(8,128)} async-done(((f32[8,8,72,256]{3,2,1,0:T(8,128)}), f32[8,8,72,256]{3,2,1,0:T(8,128)}, u32[]{:S(2)}, u32[]{:S(2)}) %all-to-all-start) | async-done | bytes 4718624 | tf_op jit(solution)/shard_map/all_to_all | solution.py:217
  71.7 3.9 %shard_map.66 = f32[8,128,256]{2,1,0:T(8,128)S(1)} custom-call(f32[8,8,72,256]{3,2,1,0:T(8,128)} %all-to-all-done.third_ref.part_ref, f32[8,8,72,256]{3,2,1,0:T(8,128)} %all-to-all-done.third_ref.part_ref), custom_call_target="tpu_custom_call" | custom-call | flops 805306368 | bytes 4194304 | tf_op jit(solution)/shard_map/pallas_call | solution.py:162
  75.7 4.0 %collective-permute-start.17 = (f32[64,256]{1,0:T(8,128)S(1)}, f32[64,256]{1,0:T(8,128)S(1)}, u32[]{:S(2)}, u32[]{:S(2)}) collective-permute-start(f32[64,256]{1,0:T(8,128)S(1)} %get-tuple-element.63), channel_id=1, source_target_pairs={{0,56},{8,0},{16,8},{24,16},{32,24},{40,32},{48,40},{56,48},{1,57}... | collective-permute-start | bytes 196616 | tf_op jit(solution)/shard_map/ppermute | solution.py:185
  79.6 1.6 %collective-permute-done.16 = f32[64,256]{1,0:T(8,128)S(1)} collective-permute-done((f32[64,256]{1,0:T(8,128)S(1)}, f32[64,256]{1,0:T(8,128)S(1)}, u32[]{:S(2)}, u32[]{:S(2)}) %collective-permute-start.16) | collective-permute-done | bytes 65568 | tf_op jit(solution)/shard_map/ppermute | solution.py:185
  81.4 2.8 %collective-permute-start.19 = (f32[128,256]{1,0:T(8,128)S(1)}, f32[128,256]{1,0:T(8,128)S(1)}, u32[]{:S(2)}, u32[]{:S(2)}) collective-permute-start(f32[128,256]{1,0:T(8,128)S(1)} %pad_maximum_fusion.9), channel_id=1, source_target_pairs={{0,56},{8,0},{16,8},{24,16},{32,24},{40,32},{48,40},{56,48},{1,57}... | collective-permute-start | bytes 393224 | tf_op jit(solution)/shard_map/ppermute | solution.py:185
  84.2 5.7 %all-to-all-start.1 = ((f32[8,64,256]{2,1,0:T(8,128)}), f32[8,64,256]{2,1,0:T(8,128)S(1)}, u32[]{:S(2)}, u32[]{:S(2)}) async-start(f32[8,64,256]{2,1,0:T(8,128)} %pad_maximum_fusion), calls=%async_computation.1 | async-start | bytes 1048576 | tf_op jit(solution)/shard_map/all_to_all | solution.py:217
  90.0 2.7 %collective-permute-start.21 = (f32[128,256]{1,0:T(8,128)S(1)}, f32[128,256]{1,0:T(8,128)S(1)}, u32[]{:S(2)}, u32[]{:S(2)}) collective-permute-start(f32[128,256]{1,0:T(8,128)S(1)} %get-tuple-element.67), channel_id=1, source_target_pairs={{0,56},{8,0},{16,8},{24,16},{32,24},{40,32},{48,40},{56,48},{1,57}... | collective-permute-start | bytes 393224 | tf_op jit(solution)/shard_map/ppermute | solution.py:185
  92.7 3.5 %collective-permute-done.20 = f32[128,256]{1,0:T(8,128)S(1)} collective-permute-done((f32[128,256]{1,0:T(8,128)S(1)}, f32[128,256]{1,0:T(8,128)S(1)}, u32[]{:S(2)}, u32[]{:S(2)}) %collective-permute-start.20) | collective-permute-done | bytes 131104 | tf_op jit(solution)/shard_map/ppermute | solution.py:185
  96.2 3.2 %all-to-all-done.1 = f32[8,64,256]{2,1,0:T(8,128)S(1)} async-done(((f32[8,64,256]{2,1,0:T(8,128)}), f32[8,64,256]{2,1,0:T(8,128)S(1)}, u32[]{:S(2)}, u32[]{:S(2)}) %all-to-all-start.1) | async-done | bytes 524320 | tf_op jit(solution)/shard_map/all_to_all | solution.py:217
  99.5 2.7 %collective-permute-start.23 = (f32[128,256]{1,0:T(8,128)S(1)}, f32[128,256]{1,0:T(8,128)S(1)}, u32[]{:S(2)}, u32[]{:S(2)}) collective-permute-start(f32[128,256]{1,0:T(8,128)S(1)} %get-tuple-element.72), channel_id=1, source_target_pairs={{0,56},{8,0},{16,8},{24,16},{32,24},{40,32},{48,40},{56,48},{1,57}... | collective-permute-start | bytes 393224 | tf_op jit(solution)/shard_map/ppermute | solution.py:185
  106.6 2.4 %collective-permute-start.25 = (f32[256,128]{1,0:T(8,128)S(1)}, f32[256,128]{1,0:T(8,128)S(1)}, u32[]{:S(2)}, u32[]{:S(2)}) collective-permute-start(f32[256,128]{1,0:T(8,128)S(1)} %fusion.2), channel_id=1, source_target_pairs={{0,128},{64,192},{128,0},{192,64},{1,129},{65,193},{129,1},{193,65... | collective-permute-start | bytes 393224 | tf_op jit(solution)/shard_map/ppermute | solution.py:185
  110.4 2.9 %collective-permute-done.25 = f32[256,128]{1,0:T(8,128)S(1)} collective-permute-done((f32[256,128]{1,0:T(8,128)S(1)}, f32[256,128]{1,0:T(8,128)S(1)}, u32[]{:S(2)}, u32[]{:S(2)}) %collective-permute-start.25) | collective-permute-done | bytes 131104 | tf_op jit(solution)/shard_map/ppermute | solution.py:185
  114.5 10.0 %all_to_all.25 = f32[8,32,128]{2,1,0:T(8,128)S(1)} all-to-all(f32[8,32,128]{2,1,0:T(8,128)S(1)} %bitcast.51), channel_id=1, replica_groups=mesh['gx'=4,'gy'=8,'vert'=8] {'vert'}, dimensions={0} | all-to-all | bytes 262144 | tf_op jit(solution)/shard_map/all_to_all | solution.py:217
  124.6 13.6 %all_to_all.26 = f32[8,32,128]{2,1,0:T(8,128)S(1)} all-to-all(f32[8,32,128]{2,1,0:T(8,128)S(1)} %broadcast_in_dim.4), channel_id=1, replica_groups=mesh['gx'=4,'gy'=8,'vert'=8] {'gy'}, dimensions={0} | all-to-all | bytes 262144 | tf_op jit(solution)/shard_map/all_to_all | solution.py:217
  138.3 10.0 %all_to_all.27 = f32[8,32,128]{2,1,0:T(8,128)S(1)} all-to-all(f32[8,32,128]{2,1,0:T(8,128)S(1)} %broadcast_in_dim.5), channel_id=1, replica_groups=mesh['gx'=4,'gy'=8,'vert'=8] {'vert'}, dimensions={0} | all-to-all | bytes 262144 | tf_op jit(solution)/shard_map/all_to_all | solution.py:217
  (69 shorter events, 11.9 us)
Async XLA Ops:
  0.0 104.9 %copy-start = (f32[1024,128]{1,0:T(8,128)S(1)}, f32[1024,128]{1,0:T(8,128)}, u32[]{:S(2)}) copy-start(f32[1024,128]{1,0:T(8,128)} %param.7) | copy-start | bytes 1572868
  9.3 12.9 %copy-start.1 = (f32[128,128]{1,0:T(8,128)S(1)}, f32[128,128]{1,0:T(8,128)}, u32[]{:S(2)}) copy-start(f32[128,128]{1,0:T(8,128)} %second_ref.2) | copy-start | bytes 196612
  9.3 12.9 %copy-start.2 = (f32[64,128]{1,0:T(8,128)S(1)}, f32[64,128]{1,0:T(8,128)}, u32[]{:S(2)}) copy-start(f32[64,128]{1,0:T(8,128)} %constant.22.clone.pick_ref) | copy-start | bytes 98308
  9.3 62.4 %all-to-all-start = ((f32[8,8,72,256]{3,2,1,0:T(8,128)}), f32[8,8,72,256]{3,2,1,0:T(8,128)}, u32[]{:S(2)}, u32[]{:S(2)}) async-start(f32[8,8,72,256]{3,2,1,0:T(8,128)} %bitcast.50), calls=%async_computation | async-start | bytes 9437184 | tf_op jit(solution)/shard_map/all_to_all | solution.py:217
  18.1 10.4 %collective-permute-start = (f32[4,32,256]{2,1,0:T(8,128)S(1)}, f32[4,32,256]{2,1,0:T(8,128)S(1)}, u32[]{:S(2)}, u32[]{:S(2)}) collective-permute-start(f32[4,32,256]{2,1,0:T(8,128)S(1)} %get-tuple-element.42), channel_id=1, source_target_pairs={{0,8},{8,16},{16,24},{24,32},{32,40},{40,48},{48,56},{56,0},{1,9},... | collective-permute-start | bytes 393224 | tf_op jit(solution)/shard_map/ppermute | solution.py:185
  18.2 10.4 %collective-permute-start.1 = (f32[4,32,256]{2,1,0:T(8,128)S(1)}, f32[4,32,256]{2,1,0:T(8,128)S(1)}, u32[]{:S(2)}, u32[]{:S(2)}) collective-permute-start(f32[4,32,256]{2,1,0:T(8,128)S(1)} %get-tuple-element.43), channel_id=1, source_target_pairs={{0,56},{8,0},{16,8},{24,16},{32,24},{40,32},{48,40},{56,48},{1,57}... | collective-permute-start | bytes 393224 | tf_op jit(solution)/shard_map/ppermute | solution.py:185
  25.8 6.0 %collective-permute-start.8 = (f32[4,32,256]{2,1,0:T(8,128)S(1)}, f32[4,32,256]{2,1,0:T(8,128)S(1)}, u32[]{:S(2)}, u32[]{:S(2)}) collective-permute-start(f32[4,32,256]{2,1,0:T(8,128)S(1)} %get-tuple-element.52), channel_id=1, source_target_pairs={{0,8},{8,16},{16,24},{24,32},{32,40},{40,48},{48,56},{56,0},{1,9},... | collective-permute-start | bytes 393224 | tf_op jit(solution)/shard_map/ppermute | solution.py:185
  25.9 6.0 %collective-permute-start.9 = (f32[4,32,256]{2,1,0:T(8,128)S(1)}, f32[4,32,256]{2,1,0:T(8,128)S(1)}, u32[]{:S(2)}, u32[]{:S(2)}) collective-permute-start(f32[4,32,256]{2,1,0:T(8,128)S(1)} %get-tuple-element.53), channel_id=1, source_target_pairs={{0,56},{8,0},{16,8},{24,16},{32,24},{40,32},{48,40},{56,48},{1,57}... | collective-permute-start | bytes 393224 | tf_op jit(solution)/shard_map/ppermute | solution.py:185
  28.7 8.1 %collective-permute-start.2 = (f32[8,32,256]{2,1,0:T(8,128)S(1)}, f32[8,32,256]{2,1,0:T(8,128)S(1)}, u32[]{:S(2)}, u32[]{:S(2)}) collective-permute-start(f32[8,32,256]{2,1,0:T(8,128)S(1)} %get-tuple-element.44), channel_id=1, source_target_pairs={{0,8},{8,16},{16,24},{24,32},{32,40},{40,48},{48,56},{56,0},{1,9},... | collective-permute-start | bytes 786440 | tf_op jit(solution)/shard_map/ppermute | solution.py:185
  28.8 8.0 %collective-permute-start.3 = (f32[8,32,256]{2,1,0:T(8,128)S(1)}, f32[8,32,256]{2,1,0:T(8,128)S(1)}, u32[]{:S(2)}, u32[]{:S(2)}) collective-permute-start(f32[8,32,256]{2,1,0:T(8,128)S(1)} %get-tuple-element.45), channel_id=1, source_target_pairs={{0,56},{8,0},{16,8},{24,16},{32,24},{40,32},{48,40},{56,48},{1,57}... | collective-permute-start | bytes 786440 | tf_op jit(solution)/shard_map/ppermute | solution.py:185
  32.0 10.6 %collective-permute-start.10 = (f32[8,32,256]{2,1,0:T(8,128)S(1)}, f32[8,32,256]{2,1,0:T(8,128)S(1)}, u32[]{:S(2)}, u32[]{:S(2)}) collective-permute-start(f32[8,32,256]{2,1,0:T(8,128)S(1)} %get-tuple-element.54), channel_id=1, source_target_pairs={{0,8},{8,16},{16,24},{24,32},{32,40},{40,48},{48,56},{56,0},{1,9},... | collective-permute-start | bytes 786440 | tf_op jit(solution)/shard_map/ppermute | solution.py:185
  32.1 10.5 %collective-permute-start.11 = (f32[8,32,256]{2,1,0:T(8,128)S(1)}, f32[8,32,256]{2,1,0:T(8,128)S(1)}, u32[]{:S(2)}, u32[]{:S(2)}) collective-permute-start(f32[8,32,256]{2,1,0:T(8,128)S(1)} %get-tuple-element.55), channel_id=1, source_target_pairs={{0,56},{8,0},{16,8},{24,16},{32,24},{40,32},{48,40},{56,48},{1,57}... | collective-permute-start | bytes 786440 | tf_op jit(solution)/shard_map/ppermute | solution.py:185
  36.9 11.3 %collective-permute-start.4 = (f32[8,32,256]{2,1,0:T(8,128)S(1)}, f32[8,32,256]{2,1,0:T(8,128)S(1)}, u32[]{:S(2)}, u32[]{:S(2)}) collective-permute-start(f32[8,32,256]{2,1,0:T(8,128)S(1)} %get-tuple-element.46), channel_id=1, source_target_pairs={{0,8},{8,16},{16,24},{24,32},{32,40},{40,48},{48,56},{56,0},{1,9},... | collective-permute-start | bytes 786440 | tf_op jit(solution)/shard_map/ppermute | solution.py:185
  37.0 11.2 %collective-permute-start.5 = (f32[8,32,256]{2,1,0:T(8,128)S(1)}, f32[8,32,256]{2,1,0:T(8,128)S(1)}, u32[]{:S(2)}, u32[]{:S(2)}) collective-permute-start(f32[8,32,256]{2,1,0:T(8,128)S(1)} %get-tuple-element.47), channel_id=1, source_target_pairs={{0,56},{8,0},{16,8},{24,16},{32,24},{40,32},{48,40},{56,48},{1,57}... | collective-permute-start | bytes 786440 | tf_op jit(solution)/shard_map/ppermute | solution.py:185
  42.6 11.2 %collective-permute-start.12 = (f32[8,32,256]{2,1,0:T(8,128)S(1)}, f32[8,32,256]{2,1,0:T(8,128)S(1)}, u32[]{:S(2)}, u32[]{:S(2)}) collective-permute-start(f32[8,32,256]{2,1,0:T(8,128)S(1)} %get-tuple-element.56), channel_id=1, source_target_pairs={{0,8},{8,16},{16,24},{24,32},{32,40},{40,48},{48,56},{56,0},{1,9},... | collective-permute-start | bytes 786440 | tf_op jit(solution)/shard_map/ppermute | solution.py:185
  42.7 11.1 %collective-permute-start.13 = (f32[8,32,256]{2,1,0:T(8,128)S(1)}, f32[8,32,256]{2,1,0:T(8,128)S(1)}, u32[]{:S(2)}, u32[]{:S(2)}) collective-permute-start(f32[8,32,256]{2,1,0:T(8,128)S(1)} %get-tuple-element.57), channel_id=1, source_target_pairs={{0,56},{8,0},{16,8},{24,16},{32,24},{40,32},{48,40},{56,48},{1,57}... | collective-permute-start | bytes 786440 | tf_op jit(solution)/shard_map/ppermute | solution.py:185
  48.2 11.0 %collective-permute-start.6 = (f32[8,32,256]{2,1,0:T(8,128)S(1)}, f32[8,32,256]{2,1,0:T(8,128)S(1)}, u32[]{:S(2)}, u32[]{:S(2)}) collective-permute-start(f32[8,32,256]{2,1,0:T(8,128)S(1)} %get-tuple-element.48), channel_id=1, source_target_pairs={{0,8},{8,16},{16,24},{24,32},{32,40},{40,48},{48,56},{56,0},{1,9},... | collective-permute-start | bytes 786440 | tf_op jit(solution)/shard_map/ppermute | solution.py:185
  48.5 10.8 %collective-permute-start.7 = (f32[8,32,256]{2,1,0:T(8,128)S(1)}, f32[8,32,256]{2,1,0:T(8,128)S(1)}, u32[]{:S(2)}, u32[]{:S(2)}) collective-permute-start(f32[8,32,256]{2,1,0:T(8,128)S(1)} %get-tuple-element.49), channel_id=1, source_target_pairs={{0,56},{8,0},{16,8},{24,16},{32,24},{40,32},{48,40},{56,48},{1,57}... | collective-permute-start | bytes 786440 | tf_op jit(solution)/shard_map/ppermute | solution.py:185
  53.8 11.2 %collective-permute-start.14 = (f32[8,32,256]{2,1,0:T(8,128)S(1)}, f32[8,32,256]{2,1,0:T(8,128)S(1)}, u32[]{:S(2)}, u32[]{:S(2)}) collective-permute-start(f32[8,32,256]{2,1,0:T(8,128)S(1)} %get-tuple-element.58), channel_id=1, source_target_pairs={{0,8},{8,16},{16,24},{24,32},{32,40},{40,48},{48,56},{56,0},{1,9},... | collective-permute-start | bytes 786440 | tf_op jit(solution)/shard_map/ppermute | solution.py:185
  53.9 11.1 %collective-permute-start.15 = (f32[8,32,256]{2,1,0:T(8,128)S(1)}, f32[8,32,256]{2,1,0:T(8,128)S(1)}, u32[]{:S(2)}, u32[]{:S(2)}) collective-permute-start(f32[8,32,256]{2,1,0:T(8,128)S(1)} %get-tuple-element.59), channel_id=1, source_target_pairs={{0,56},{8,0},{16,8},{24,16},{32,24},{40,32},{48,40},{56,48},{1,57}... | collective-permute-start | bytes 786440 | tf_op jit(solution)/shard_map/ppermute | solution.py:185
  75.6 5.6 %collective-permute-start.16 = (f32[64,256]{1,0:T(8,128)S(1)}, f32[64,256]{1,0:T(8,128)S(1)}, u32[]{:S(2)}, u32[]{:S(2)}) collective-permute-start(f32[64,256]{1,0:T(8,128)S(1)} %get-tuple-element.62), channel_id=1, source_target_pairs={{0,8},{8,16},{16,24},{24,32},{32,40},{40,48},{48,56},{56,0},{1,9},... | collective-permute-start | bytes 196616 | tf_op jit(solution)/shard_map/ppermute | solution.py:185
  75.7 5.5 %collective-permute-start.17 = (f32[64,256]{1,0:T(8,128)S(1)}, f32[64,256]{1,0:T(8,128)S(1)}, u32[]{:S(2)}, u32[]{:S(2)}) collective-permute-start(f32[64,256]{1,0:T(8,128)S(1)} %get-tuple-element.63), channel_id=1, source_target_pairs={{0,56},{8,0},{16,8},{24,16},{32,24},{40,32},{48,40},{56,48},{1,57}... | collective-permute-start | bytes 196616 | tf_op jit(solution)/shard_map/ppermute | solution.py:185
  81.3 8.6 %collective-permute-start.18 = (f32[128,256]{1,0:T(8,128)S(1)}, f32[128,256]{1,0:T(8,128)S(1)}, u32[]{:S(2)}, u32[]{:S(2)}) collective-permute-start(f32[128,256]{1,0:T(8,128)S(1)} %pad_maximum_fusion.8), channel_id=1, source_target_pairs={{0,8},{8,16},{16,24},{24,32},{32,40},{40,48},{48,56},{56,0},{1,9},... | collective-permute-start | bytes 393224 | tf_op jit(solution)/shard_map/ppermute | solution.py:185
  81.4 8.5 %collective-permute-start.19 = (f32[128,256]{1,0:T(8,128)S(1)}, f32[128,256]{1,0:T(8,128)S(1)}, u32[]{:S(2)}, u32[]{:S(2)}) collective-permute-start(f32[128,256]{1,0:T(8,128)S(1)} %pad_maximum_fusion.9), channel_id=1, source_target_pairs={{0,56},{8,0},{16,8},{24,16},{32,24},{40,32},{48,40},{56,48},{1,57}... | collective-permute-start | bytes 393224 | tf_op jit(solution)/shard_map/ppermute | solution.py:185
  84.2 15.2 %all-to-all-start.1 = ((f32[8,64,256]{2,1,0:T(8,128)}), f32[8,64,256]{2,1,0:T(8,128)S(1)}, u32[]{:S(2)}, u32[]{:S(2)}) async-start(f32[8,64,256]{2,1,0:T(8,128)} %pad_maximum_fusion), calls=%async_computation.1 | async-start | bytes 1048576 | tf_op jit(solution)/shard_map/all_to_all | solution.py:217
  89.9 6.3 %collective-permute-start.20 = (f32[128,256]{1,0:T(8,128)S(1)}, f32[128,256]{1,0:T(8,128)S(1)}, u32[]{:S(2)}, u32[]{:S(2)}) collective-permute-start(f32[128,256]{1,0:T(8,128)S(1)} %get-tuple-element.66), channel_id=1, source_target_pairs={{0,8},{8,16},{16,24},{24,32},{32,40},{40,48},{48,56},{56,0},{1,9},... | collective-permute-start | bytes 393224 | tf_op jit(solution)/shard_map/ppermute | solution.py:185
  90.0 6.2 %collective-permute-start.21 = (f32[128,256]{1,0:T(8,128)S(1)}, f32[128,256]{1,0:T(8,128)S(1)}, u32[]{:S(2)}, u32[]{:S(2)}) collective-permute-start(f32[128,256]{1,0:T(8,128)S(1)} %get-tuple-element.67), channel_id=1, source_target_pairs={{0,56},{8,0},{16,8},{24,16},{32,24},{40,32},{48,40},{56,48},{1,57}... | collective-permute-start | bytes 393224 | tf_op jit(solution)/shard_map/ppermute | solution.py:185
  99.4 5.4 %collective-permute-start.22 = (f32[128,256]{1,0:T(8,128)S(1)}, f32[128,256]{1,0:T(8,128)S(1)}, u32[]{:S(2)}, u32[]{:S(2)}) collective-permute-start(f32[128,256]{1,0:T(8,128)S(1)} %get-tuple-element.71), channel_id=1, source_target_pairs={{0,8},{8,16},{16,24},{24,32},{32,40},{40,48},{48,56},{56,0},{1,9},... | collective-permute-start | bytes 393224 | tf_op jit(solution)/shard_map/ppermute | solution.py:185
  99.5 5.3 %collective-permute-start.23 = (f32[128,256]{1,0:T(8,128)S(1)}, f32[128,256]{1,0:T(8,128)S(1)}, u32[]{:S(2)}, u32[]{:S(2)}) collective-permute-start(f32[128,256]{1,0:T(8,128)S(1)} %get-tuple-element.72), channel_id=1, source_target_pairs={{0,56},{8,0},{16,8},{24,16},{32,24},{40,32},{48,40},{56,48},{1,57}... | collective-permute-start | bytes 393224 | tf_op jit(solution)/shard_map/ppermute | solution.py:185
  105.3 5.1 %collective-permute-start.24 = (f32[256,128]{1,0:T(8,128)S(1)}, f32[256,128]{1,0:T(8,128)S(1)}, u32[]{:S(2)}, u32[]{:S(2)}) collective-permute-start(f32[256,128]{1,0:T(8,128)S(1)} %fusion.2), channel_id=1, source_target_pairs={{0,64},{64,128},{128,192},{192,0},{1,65},{65,129},{129,193},{193,1... | collective-permute-start | bytes 393224 | tf_op jit(solution)/shard_map/ppermute | solution.py:185
  106.6 6.7 %collective-permute-start.25 = (f32[256,128]{1,0:T(8,128)S(1)}, f32[256,128]{1,0:T(8,128)S(1)}, u32[]{:S(2)}, u32[]{:S(2)}) collective-permute-start(f32[256,128]{1,0:T(8,128)S(1)} %fusion.2), channel_id=1, source_target_pairs={{0,128},{64,192},{128,0},{192,64},{1,129},{65,193},{129,1},{193,65... | collective-permute-start | bytes 393224 | tf_op jit(solution)/shard_map/ppermute | solution.py:185
  109.0 4.9 %collective-permute-start.26 = (f32[256,128]{1,0:T(8,128)S(1)}, f32[256,128]{1,0:T(8,128)S(1)}, u32[]{:S(2)}, u32[]{:S(2)}) collective-permute-start(f32[256,128]{1,0:T(8,128)S(1)} %fusion.2), channel_id=1, source_target_pairs={{0,192},{64,0},{128,64},{192,128},{1,193},{65,1},{129,65},{193,129... | collective-permute-start | bytes 393224 | tf_op jit(solution)/shard_map/ppermute | solution.py:185
  (1 other events, 10.5 us)

commit v6 on v5

v6 whole, which is shorter than its diff:
```python
import functools

import jax
import jax.numpy as jnp
import numpy as np
from jax import lax
from jax.experimental import pallas as pl
from jax.experimental.pallas import tpu as pltpu
from jax.sharding import PartitionSpec as P

HIGHEST = lax.Precision.HIGHEST
NT = (((1,), (1,)), ((), ()))
NN = (((1,), (0,)), ((), ()))
VMEM_LIMIT = 10 * 2**20
STEP = 8
SETS = 8


def split(value):
    high = value.astype(jnp.bfloat16)
    return high, (value - high.astype(jnp.float32)).astype(jnp.bfloat16)


def product(high, both, value):
    rows = high.shape[0]
    v_high, v_low = split(value)
    main = lax.dot_general(both, v_high, NN, preferred_element_type=jnp.float32)
    rest = lax.dot_general(high, v_low, NN, preferred_element_type=jnp.float32)
    return main[:rows] + (main[rows:] + rest)


def mode_kernel(roll, first, pick_ref, second_ref, field_ref, out_ref, both_ref, held_ref, sems):
    rows = pick_ref.shape[0]
    ny = second_ref.shape[0]
    steps = held_ref.shape[0] // STEP
    now = pl.program_id(0)

    def fetch(i):
        return pltpu.make_async_copy(
            field_ref.at[pl.ds((first + i) * STEP, STEP)], held_ref.at[pl.ds(i * STEP, STEP)], sems.at[i]
        )

    @pl.when(now == 0)
    def _():
        for i in range(steps):
            fetch(i).start()
        pick = pltpu.roll(pick_ref[...], lax.axis_index("gy") * roll, 1).astype(jnp.bfloat16)
        both_ref[...] = jnp.zeros_like(both_ref)
        for part, value in enumerate(split(second_ref[...])):
            value = lax.dot_general(pick, value, NT, preferred_element_type=jnp.float32).astype(jnp.bfloat16)
            both_ref[part * rows : (part + 1) * rows, :ny] = value
            if part == 0:
                both_ref[:rows, ny:] = value

    fetch(now).wait()
    both = both_ref[...]
    for j in range(STEP):
        pair = jnp.concatenate(split(held_ref[now * STEP + j]), 1)
        value = lax.dot_general(both, pair, NT, preferred_element_type=jnp.float32)
        out_ref[:, j, :] = value[:rows] + value[rows:]


def mode_product(pick, second, field, roll, start, count):
    _, nx, ny = field.shape
    steps = count // STEP
    rows = pick.shape[0]
    return pl.pallas_call(
        functools.partial(mode_kernel, roll, start // STEP),
        grid=(steps,),
        in_specs=[
            pl.BlockSpec(pick.shape, lambda i: (0, 0)),
            pl.BlockSpec(second.shape, lambda i: (0, 0)),
            pl.BlockSpec(memory_space=pl.ANY),
        ],
        out_specs=pl.BlockSpec((rows, STEP, nx), lambda i: (0, i, 0)),
        out_shape=jax.ShapeDtypeStruct((rows, count, nx), jnp.float32),
        scratch_shapes=[
            pltpu.VMEM((2 * rows, 2 * ny), jnp.bfloat16),
            pltpu.VMEM((count, nx, ny), jnp.float32),
            pltpu.SemaphoreType.DMA((steps,)),
        ],
        compiler_params=pltpu.CompilerParams(vmem_limit_bytes=46 * 2**20),
        cost_estimate=pl.CostEstimate(
            flops=6 * count * nx * ny * rows,
            bytes_accessed=4 * count * nx * (ny + rows),
            transcendentals=0,
        ),
    )(jnp.asarray(pick), second, field)


def lead_kernel(
    roll, pick_ref, second_ref, third_ref, field_ref, f_ref, m_ref, both_ref, held_ref, stage_ref, pack_ref, sems, out_sems, third_sem
):
    rows = pick_ref.shape[0] // 2
    ny = second_ref.shape[0]
    rank = third_ref.shape[1]
    steps = held_ref.shape[0] // STEP
    sets = f_ref.shape[0]
    groups = rows // sets
    per_half = steps // 2
    now = pl.program_id(0)

    def fetch(i):
        return pltpu.make_async_copy(
            field_ref.at[pl.ds(i * STEP, STEP)], held_ref.at[pl.ds(i * STEP, STEP)], sems.at[i]
        )

    def send(i):
        plane = pl.multiple_of(i % per_half * STEP, STEP)
        target = f_ref.at[:, pl.ds(i // per_half * groups, groups), pl.ds(plane, STEP), :]
        return pltpu.make_async_copy(stage_ref.at[i % 2], target, out_sems.at[i % 2])

    def send_third(v):
        return pltpu.make_async_copy(pack_ref, f_ref.at[v, 2 * groups], third_sem.at[v])

    @pl.when(now == 0)
    def _():
        for i in range(steps):
            fetch(i).start()
        for half in range(2):
            pack_ref[:, half * rank : (half + 1) * rank] = third_ref[half * per_half * STEP : (half + 1) * per_half * STEP, :]
        for v in range(sets):
            send_third(v).start()
        pick = pltpu.roll(pick_ref[...], lax.axis_index("gy") * roll, 1).astype(jnp.bfloat16)
        both_ref[...] = jnp.zeros_like(both_ref)
        for part, value in enumerate(split(second_ref[...])):
            value = lax.dot_general(pick, value, NT, preferred_element_type=jnp.float32).astype(jnp.bfloat16)
            for n in range(2):
                place = (2 * n + part) * rows
                both_ref[place : place + rows, :ny] = value[n * rows : (n + 1) * rows]
                if part == 0:
                    both_ref[place : place + rows, ny:] = value[n * rows : (n + 1) * rows]

    @pl.when(now >= 2)
    def _():
        send(now - 2).wait()

    fetch(now).wait()

    def multiply(with_m):
        both = both_ref[...] if with_m else both_ref[: 2 * rows]
        for j in range(STEP):
            pair = jnp.concatenate(split(held_ref[now * STEP + j]), 1)
            value = lax.dot_general(both, pair, NT, preferred_element_type=jnp.float32)
            f = value[:rows] + value[rows : 2 * rows]
            for v in range(sets):
                stage_ref[now % 2, v, :, j, :] = f[v * groups : (v + 1) * groups]
            if with_m:
                m_ref[:, j, :] = value[2 * rows : 3 * rows] + value[3 * rows :]

    @pl.when(now < per_half)
    def _():
        multiply(True)

    @pl.when(now >= per_half)
    def _():
        multiply(False)

    send(now).start()

    @pl.when(now == steps - 1)
    def _():
        send(now - 1).wait()
        send(now).wait()
        for v in range(sets):
            send_third(v).wait()


def lead_product(pick_f, pick_m, second, field, roll, third):
    depth, nx, ny = field.shape
    steps = depth // STEP
    pick = np.concatenate([pick_f, pick_m], 0)
    rows = pick_f.shape[0]
    groups = rows // SETS
    return pl.pallas_call(
        functools.partial(lead_kernel, roll),
        grid=(steps,),
        in_specs=[
            pl.BlockSpec(pick.shape, lambda i: (0, 0)),
            pl.BlockSpec(second.shape, lambda i: (0, 0)),
            pl.BlockSpec(third.shape, lambda i: (0, 0)),
            pl.BlockSpec(memory_space=pl.ANY),
        ],
        out_specs=[
            pl.BlockSpec(memory_space=pl.ANY),
            pl.BlockSpec((rows, STEP, nx), lambda i: (0, jnp.minimum(i, steps // 2 - 1), 0)),
        ],
        out_shape=[
            jax.ShapeDtypeStruct((SETS, 2 * groups + 1, depth // 2, nx), jnp.float32),
            jax.ShapeDtypeStruct((rows, depth // 2, nx), jnp.float32),
        ],
        scratch_shapes=[
            pltpu.VMEM((4 * rows, 2 * ny), jnp.bfloat16),
            pltpu.VMEM((depth, nx, ny), jnp.float32),
            pltpu.VMEM((2, SETS, groups, STEP, nx), jnp.float32),
            pltpu.VMEM((depth // 2, nx), jnp.float32),
            pltpu.SemaphoreType.DMA((steps,)),
            pltpu.SemaphoreType.DMA((2,)),
            pltpu.SemaphoreType.DMA((SETS,)),
        ],
        compiler_params=pltpu.CompilerParams(vmem_limit_bytes=54 * 2**20),
        cost_estimate=pl.CostEstimate(
            flops=6 * depth * nx * ny * pick.shape[0],
            bytes_accessed=4 * depth * nx * (ny + pick.shape[0]),
            transcendentals=0,
        ),
    )(jnp.asarray(pick), second, third, field)


def depth_kernel(third_ref, one_ref, two_ref, out_ref, both_ref):
    rank, nx = out_ref.shape[1:]

    @pl.when(pl.program_id(0) == 0)
    def _():
        halves = [third_ref[:, 0, :, half * rank : (half + 1) * rank].reshape(-1, rank) for half in range(2)]
        high, low = split(jnp.concatenate(halves, 0).T)
        both_ref[:rank] = high
        both_ref[rank:] = low

    for g in range(out_ref.shape[0]):
        value = jnp.concatenate([ref[:, g].reshape(-1, nx) for ref in (one_ref, two_ref)], 0)
        out_ref[g] = product(both_ref[:rank], both_ref[...], value)


def depth_product(gathered, part, rank, groups):
    n, count, planes, nx = gathered.shape
    step = 2 if groups % 2 == 0 else 1
    block = (n, step, planes, nx)
    return pl.pallas_call(
        depth_kernel,
        grid=(groups // step,),
        in_specs=[
            pl.BlockSpec((n, 1, planes, nx), lambda i: (0, count - 1, 0, 0)),
            pl.BlockSpec(block, lambda i: (0, i, 0, 0)),
            pl.BlockSpec(block, lambda i: (0, groups // step + i, 0, 0)),
        ],
        out_specs=pl.BlockSpec((step, rank, nx), lambda i: (i, 0, 0)),
        out_shape=jax.ShapeDtypeStruct((groups, rank, nx), jnp.float32),
        scratch_shapes=[pltpu.VMEM((2 * rank, 2 * n * planes), jnp.bfloat16)],
        compiler_params=pltpu.CompilerParams(vmem_limit_bytes=VMEM_LIMIT),
        cost_estimate=pl.CostEstimate(
            flops=12 * n * groups * planes * nx * rank,
            bytes_accessed=8 * n * groups * planes * nx,
            transcendentals=0,
        ),
    )(gathered, part, part)


def shifts(moves, axis):
    n = lax.axis_size(axis)
    values = lax.optimization_barrier([value for value, _ in moves])
    return [
        lax.ppermute(value, axis, [(i, (i + by) % n) for i in range(n)])
        for value, (_, by) in zip(values, moves)
    ]


def ring_steps(parts, axis):
    n = len(parts)
    half = n // 2
    mid = parts[half].shape[0] // 2
    moving = shifts([(parts[half][:mid], 1), (parts[half][mid:], -1)], axis)
    for d in range(half - 1, 0, -1):
        up, down = yield moving
        if d == half - 1:
            up = jnp.concatenate([parts[d][:mid] + up, parts[d][mid:]], 0)
            down = jnp.concatenate([parts[n - d][:mid], parts[n - d][mid:] + down], 0)
        else:
            up = parts[d] + up
            down = parts[n - d] + down
        moving = shifts([(up, 1), (down, -1)], axis)
    up, down = yield moving
    yield parts[0] + up + down


def ring_sum(parts, axis):
    steps = ring_steps(parts, axis)
    value = next(steps)
    for _ in range(len(parts) // 2):
        value = steps.send(value)
    return value


def trade(value, axis):
    return lax.all_to_all(value, axis, 0, 0)


def spread(value, axis):
    n = lax.axis_size(axis)
    return trade(jnp.broadcast_to(value[None], (n,) + value.shape), axis)


def local(snapshot, basis_first, basis_second, basis_third):
    depth = snapshot.shape[0] * snapshot.shape[1]
    nx = snapshot.shape[2]
    ny = snapshot.shape[3]
    rank = basis_second.shape[1]
    gx = lax.axis_size("gx")
    gy = lax.axis_size("gy")
    vert = lax.axis_size("vert")
    share = rank // gy
    part_m = share // 2
    field = snapshot.reshape(depth, nx, ny)
    first = lax.dynamic_slice_in_dim(basis_first, lax.axis_index("gx") * nx, nx, 0)

    third = basis_third.reshape(depth, rank)

    def pick(pairs):
        return np.eye(rank, dtype=np.float32)[[place * share + within for place, within in pairs]]

    pick_f = pick([(place, part_m + v) for v in range(vert) for place in range(gy)])
    pick_m = pick([(place, within) for place in range(gy) for within in range(part_m)])

    half = depth // 2
    f, m1 = lead_product(pick_f, pick_m, basis_second, field, share, third)
    second, f = lax.optimization_barrier((basis_second, f))
    f = trade(f, "vert")

    m2 = mode_product(pick_m, second, field, share, half, half)
    m = [ring_sum([part[d * part_m : (d + 1) * part_m] for d in range(gy)], "gy") for part in (m1, m2)]
    m, f = lax.optimization_barrier((jnp.concatenate(m, 1), f))
    m = trade(m, "vert")

    parts = depth_product(f, f, rank, gy)
    ring = ring_steps([parts[d] for d in range(gy)], "gy")
    moving = next(ring)
    for _ in range(gy // 2 - 2):
        moving = ring.send(moving)
    moving, m = lax.optimization_barrier((moving, m))
    m = depth_product(f, m.reshape(vert, 2, half, nx), rank, 1)[0]
    f = ring.send(ring.send(moving))

    columns = jnp.concatenate([f, m], 0)
    weights = jnp.dot(columns, first, precision=HIGHEST)
    others = shifts([(weights, d) for d in range(1, gx)], "gx")
    for other in others:
        weights = weights + other
    updated = lax.dot_general(columns, weights, (((0,), (0,)), ((), ())), precision=HIGHEST)

    updated = jnp.sum(trade(updated.reshape(vert, nx // vert, rank), "vert"), axis=0)
    updated = jnp.sum(spread(updated, "gy"), axis=0) / float(rank * rank)
    return spread(updated, "vert").reshape(nx, rank)


def solution(mesh):
    placed = (P("vert", None, "gx", "gy"), P(), P("gy", None), P("vert", None, None))
    return jax.shard_map(
        local, mesh=mesh, in_specs=placed, out_specs=P("gx", None), check_vma=False
    )
```

time: 149 us -> 147 us (0.987)
  waiting for transfers between devices: 38.3 us -> 35.6 us
    all_to_all x2, waiting for transfers between devices: 8.96 us -> 6.21 us  [trade(): return lax.all_to_all(value, axis, 0, 0)]
where the time goes in v6:
time: 147 us
  starting transfers between devices  54.3 us (37%)
  waiting for transfers between devices  35.6 us (24%)
  blocking collectives  33.7 us (23%)
  Pallas kernels  18.6 us (13%)
  local copies, waits for them, and re-layouts  1.72 us (1%)
  other arithmetic  1.61 us (1%)
    ppermute x27, starting transfers between devices, shifts(): lax.ppermute(value, axis, [(i, (i + by) % n) for i in range(n)])  40.7 us
    all_to_all x3, blocking collectives, trade(): return lax.all_to_all(value, axis, 0, 0)  33.7 us
    ppermute x27, waiting for transfers between devices, shifts(): lax.ppermute(value, axis, [(i, (i + by) % n) for i in range(n)])  29.3 us
    all_to_all x2, starting transfers between devices, trade(): return lax.all_to_all(value, axis, 0, 0)  13.5 us
    pallas_call x1, Pallas kernels, lead_product(): pl.pallas_call(functools.partial(lead_kernel, roll), grid=(steps,), in_sp...  9.87 us
    all_to_all x2, waiting for transfers between devices, trade(): return lax.all_to_all(value, axis, 0, 0)  6.21 us
    pallas_call x2, Pallas kernels, depth_product(): pl.pallas_call(depth_kernel, grid=(groups // step,), in_specs=[pl.BlockSp...  5.2 us
    pallas_call x1, Pallas kernels, mode_product(): pl.pallas_call(functools.partial(mode_kernel, roll, start // STEP), grid=...  3.58 us
  transfers between devices with their start and end apart: 29, of which 15 were waited for; matrix products, arithmetic and copies ran while one was open for 2% of the time, Pallas kernels for 3%

profile of v6, /device:TPU:1, one launch (start us, length us, event | category | flops | bytes accessed | tf_op | source)
XLA Modules:
  0.0 146.8 jit_solution(2263314250004196649)
XLA Ops:
  0.0 9.9 %shard_map.64 = (f32[8,17,32,256]{3,2,1,0:T(8,128)}, f32[64,32,256]{2,1,0:T(8,128)}) custom-call(f32[128,128]{1,0:T(8,128)} %constant.21.clone.pick_ref, f32[128,128]{1,0:T(8,128)} %second_ref.2, f32[64,128]{1,0:T(8,128)} %bitcast.52, f32[64,256,128]{2,1,0:T(8,128)} %bitcast.48), custom_call_target="tpu_custom_call" | custom-call | flops 1610612736 | bytes 16777216 | tf_op jit(solution)/shard_map/pallas_call | solution.py:175
  9.9 7.8 %all-to-all-start = ((f32[8,17,32,256]{3,2,1,0:T(8,128)}), f32[8,17,32,256]{3,2,1,0:T(8,128)}, u32[]{:S(2)}, u32[]{:S(2)}) async-start(f32[8,17,32,256]{3,2,1,0:T(8,128)} %get-tuple-element.60), calls=%async_computation | async-start | bytes 8912896 | tf_op jit(solution)/shard_map/all_to_all | solution.py:285
  18.8 3.9 %collective-permute-start.1 = (f32[4,32,256]{2,1,0:T(8,128)S(1)}, f32[4,32,256]{2,1,0:T(8,128)S(1)}, u32[]{:S(2)}, u32[]{:S(2)}) collective-permute-start(f32[4,32,256]{2,1,0:T(8,128)S(1)} %get-tuple-element.43), channel_id=1, source_target_pairs={{0,56},{8,0},{16,8},{24,16},{32,24},{40,32},{48,40},{56,48},{1,57}... | collective-permute-start | bytes 393224 | tf_op jit(solution)/shard_map/ppermute | solution.py:253
  22.8 3.6 %shard_map.65 = f32[64,32,256]{2,1,0:T(8,128)S(1)} custom-call(f32[64,128]{1,0:T(8,128)S(1)} %copy-done.2, f32[128,128]{1,0:T(8,128)S(1)} %copy-done.1, f32[64,256,128]{2,1,0:T(8,128)} %bitcast.49), custom_call_target="tpu_custom_call" | custom-call | flops 402653184 | bytes 6291456 | tf_op jit(solution)/shard_map/pallas_call | solution.py:67
  26.5 2.7 %collective-permute-start.9 = (f32[4,32,256]{2,1,0:T(8,128)S(1)}, f32[4,32,256]{2,1,0:T(8,128)S(1)}, u32[]{:S(2)}, u32[]{:S(2)}) collective-permute-start(f32[4,32,256]{2,1,0:T(8,128)S(1)} %get-tuple-element.53), channel_id=1, source_target_pairs={{0,56},{8,0},{16,8},{24,16},{32,24},{40,32},{48,40},{56,48},{1,57}... | collective-permute-start | bytes 393224 | tf_op jit(solution)/shard_map/ppermute | solution.py:253
  29.3 2.7 %collective-permute-start.3 = (f32[8,32,256]{2,1,0:T(8,128)S(1)}, f32[8,32,256]{2,1,0:T(8,128)S(1)}, u32[]{:S(2)}, u32[]{:S(2)}) collective-permute-start(f32[8,32,256]{2,1,0:T(8,128)S(1)} %get-tuple-element.45), channel_id=1, source_target_pairs={{0,56},{8,0},{16,8},{24,16},{32,24},{40,32},{48,40},{56,48},{1,57}... | collective-permute-start | bytes 786440 | tf_op jit(solution)/shard_map/ppermute | solution.py:253
  32.6 2.7 %collective-permute-start.11 = (f32[8,32,256]{2,1,0:T(8,128)S(1)}, f32[8,32,256]{2,1,0:T(8,128)S(1)}, u32[]{:S(2)}, u32[]{:S(2)}) collective-permute-start(f32[8,32,256]{2,1,0:T(8,128)S(1)} %get-tuple-element.55), channel_id=1, source_target_pairs={{0,56},{8,0},{16,8},{24,16},{32,24},{40,32},{48,40},{56,48},{1,57}... | collective-permute-start | bytes 786440 | tf_op jit(solution)/shard_map/ppermute | solution.py:253
  35.3 2.1 %collective-permute-done.2 = f32[8,32,256]{2,1,0:T(8,128)S(1)} collective-permute-done((f32[8,32,256]{2,1,0:T(8,128)S(1)}, f32[8,32,256]{2,1,0:T(8,128)S(1)}, u32[]{:S(2)}, u32[]{:S(2)}) %collective-permute-start.2) | collective-permute-done | bytes 262176 | tf_op jit(solution)/shard_map/ppermute | solution.py:253
  37.5 2.7 %collective-permute-start.5 = (f32[8,32,256]{2,1,0:T(8,128)S(1)}, f32[8,32,256]{2,1,0:T(8,128)S(1)}, u32[]{:S(2)}, u32[]{:S(2)}) collective-permute-start(f32[8,32,256]{2,1,0:T(8,128)S(1)} %get-tuple-element.47), channel_id=1, source_target_pairs={{0,56},{8,0},{16,8},{24,16},{32,24},{40,32},{48,40},{56,48},{1,57}... | collective-permute-start | bytes 786440 | tf_op jit(solution)/shard_map/ppermute | solution.py:253
  40.2 2.9 %collective-permute-done.10 = f32[8,32,256]{2,1,0:T(8,128)S(1)} collective-permute-done((f32[8,32,256]{2,1,0:T(8,128)S(1)}, f32[8,32,256]{2,1,0:T(8,128)S(1)}, u32[]{:S(2)}, u32[]{:S(2)}) %collective-permute-start.10) | collective-permute-done | bytes 262176 | tf_op jit(solution)/shard_map/ppermute | solution.py:253
  43.3 2.7 %collective-permute-start.13 = (f32[8,32,256]{2,1,0:T(8,128)S(1)}, f32[8,32,256]{2,1,0:T(8,128)S(1)}, u32[]{:S(2)}, u32[]{:S(2)}) collective-permute-start(f32[8,32,256]{2,1,0:T(8,128)S(1)} %get-tuple-element.57), channel_id=1, source_target_pairs={{0,56},{8,0},{16,8},{24,16},{32,24},{40,32},{48,40},{56,48},{1,57}... | collective-permute-start | bytes 786440 | tf_op jit(solution)/shard_map/ppermute | solution.py:253
  45.9 2.8 %collective-permute-done.4 = f32[8,32,256]{2,1,0:T(8,128)S(1)} collective-permute-done((f32[8,32,256]{2,1,0:T(8,128)S(1)}, f32[8,32,256]{2,1,0:T(8,128)S(1)}, u32[]{:S(2)}, u32[]{:S(2)}) %collective-permute-start.4) | collective-permute-done | bytes 262176 | tf_op jit(solution)/shard_map/ppermute | solution.py:253
  49.1 2.7 %collective-permute-start.7 = (f32[8,32,256]{2,1,0:T(8,128)S(1)}, f32[8,32,256]{2,1,0:T(8,128)S(1)}, u32[]{:S(2)}, u32[]{:S(2)}) collective-permute-start(f32[8,32,256]{2,1,0:T(8,128)S(1)} %get-tuple-element.49), channel_id=1, source_target_pairs={{0,56},{8,0},{16,8},{24,16},{32,24},{40,32},{48,40},{56,48},{1,57}... | collective-permute-start | bytes 786440 | tf_op jit(solution)/shard_map/ppermute | solution.py:253
  51.7 2.6 %collective-permute-done.12 = f32[8,32,256]{2,1,0:T(8,128)S(1)} collective-permute-done((f32[8,32,256]{2,1,0:T(8,128)S(1)}, f32[8,32,256]{2,1,0:T(8,128)S(1)}, u32[]{:S(2)}, u32[]{:S(2)}) %collective-permute-start.12) | collective-permute-done | bytes 262176 | tf_op jit(solution)/shard_map/ppermute | solution.py:253
  54.5 2.7 %collective-permute-start.15 = (f32[8,32,256]{2,1,0:T(8,128)S(1)}, f32[8,32,256]{2,1,0:T(8,128)S(1)}, u32[]{:S(2)}, u32[]{:S(2)}) collective-permute-start(f32[8,32,256]{2,1,0:T(8,128)S(1)} %get-tuple-element.59), channel_id=1, source_target_pairs={{0,56},{8,0},{16,8},{24,16},{32,24},{40,32},{48,40},{56,48},{1,57}... | collective-permute-start | bytes 786440 | tf_op jit(solution)/shard_map/ppermute | solution.py:253
  57.2 2.8 %collective-permute-done.6 = f32[8,32,256]{2,1,0:T(8,128)S(1)} collective-permute-done((f32[8,32,256]{2,1,0:T(8,128)S(1)}, f32[8,32,256]{2,1,0:T(8,128)S(1)}, u32[]{:S(2)}, u32[]{:S(2)}) %collective-permute-start.6) | collective-permute-done | bytes 262176 | tf_op jit(solution)/shard_map/ppermute | solution.py:253
  60.0 5.6 %collective-permute-done.14 = f32[8,32,256]{2,1,0:T(8,128)S(1)} collective-permute-done((f32[8,32,256]{2,1,0:T(8,128)S(1)}, f32[8,32,256]{2,1,0:T(8,128)S(1)}, u32[]{:S(2)}, u32[]{:S(2)}) %collective-permute-start.14) | collective-permute-done | bytes 262176 | tf_op jit(solution)/shard_map/ppermute | solution.py:253
  66.5 3.0 %all-to-all-done.third_ref.one_ref.two_ref = f32[8,17,32,256]{3,2,1,0:T(8,128)} async-done(((f32[8,17,32,256]{3,2,1,0:T(8,128)}), f32[8,17,32,256]{3,2,1,0:T(8,128)}, u32[]{:S(2)}, u32[]{:S(2)}) %all-to-all-start) | async-done | bytes 4456480 | tf_op jit(solution)/shard_map/all_to_all | solution.py:285
  69.5 3.9 %shard_map.66 = f32[8,128,256]{2,1,0:T(8,128)S(1)} custom-call(f32[8,17,32,256]{3,2,1,0:T(8,128)} %all-to-all-done.third_ref.one_ref.two_ref, f32[8,17,32,256]{3,2,1,0:T(8,128)} %all-to-all-done.third_ref.one_ref.two_ref, f32[8,17,32,256]{3,2,1,0:T(8,128)} %all-to-all-done.third_ref.one_ref.two_ref), custom_call_target="tpu_custom_call" | custom-call | flops 805306368 | bytes 4194304 | tf_op jit(solution)/shard_map/pallas_call | solution.py:229
  73.5 3.9 %collective-permute-start.17 = (f32[64,256]{1,0:T(8,128)S(1)}, f32[64,256]{1,0:T(8,128)S(1)}, u32[]{:S(2)}, u32[]{:S(2)}) collective-permute-start(f32[64,256]{1,0:T(8,128)S(1)} %get-tuple-element.63), channel_id=1, source_target_pairs={{0,56},{8,0},{16,8},{24,16},{32,24},{40,32},{48,40},{56,48},{1,57}... | collective-permute-start | bytes 196616 | tf_op jit(solution)/shard_map/ppermute | solution.py:253
  77.4 1.6 %collective-permute-done.16 = f32[64,256]{1,0:T(8,128)S(1)} collective-permute-done((f32[64,256]{1,0:T(8,128)S(1)}, f32[64,256]{1,0:T(8,128)S(1)}, u32[]{:S(2)}, u32[]{:S(2)}) %collective-permute-start.16) | collective-permute-done | bytes 65568 | tf_op jit(solution)/shard_map/ppermute | solution.py:253
  79.2 2.8 %collective-permute-start.19 = (f32[128,256]{1,0:T(8,128)S(1)}, f32[128,256]{1,0:T(8,128)S(1)}, u32[]{:S(2)}, u32[]{:S(2)}) collective-permute-start(f32[128,256]{1,0:T(8,128)S(1)} %pad_maximum_fusion.9), channel_id=1, source_target_pairs={{0,56},{8,0},{16,8},{24,16},{32,24},{40,32},{48,40},{56,48},{1,57}... | collective-permute-start | bytes 393224 | tf_op jit(solution)/shard_map/ppermute | solution.py:253
  82.0 5.7 %all-to-all-start.1 = ((f32[8,64,256]{2,1,0:T(8,128)}), f32[8,64,256]{2,1,0:T(8,128)S(1)}, u32[]{:S(2)}, u32[]{:S(2)}) async-start(f32[8,64,256]{2,1,0:T(8,128)} %pad_maximum_fusion), calls=%async_computation.1 | async-start | bytes 1048576 | tf_op jit(solution)/shard_map/all_to_all | solution.py:285
  87.8 2.7 %collective-permute-start.21 = (f32[128,256]{1,0:T(8,128)S(1)}, f32[128,256]{1,0:T(8,128)S(1)}, u32[]{:S(2)}, u32[]{:S(2)}) collective-permute-start(f32[128,256]{1,0:T(8,128)S(1)} %get-tuple-element.67), channel_id=1, source_target_pairs={{0,56},{8,0},{16,8},{24,16},{32,24},{40,32},{48,40},{56,48},{1,57}... | collective-permute-start | bytes 393224 | tf_op jit(solution)/shard_map/ppermute | solution.py:253
  90.5 3.5 %collective-permute-done.20 = f32[128,256]{1,0:T(8,128)S(1)} collective-permute-done((f32[128,256]{1,0:T(8,128)S(1)}, f32[128,256]{1,0:T(8,128)S(1)}, u32[]{:S(2)}, u32[]{:S(2)}) %collective-permute-start.20) | collective-permute-done | bytes 131104 | tf_op jit(solution)/shard_map/ppermute | solution.py:253
  94.0 3.2 %all-to-all-done.1 = f32[8,64,256]{2,1,0:T(8,128)S(1)} async-done(((f32[8,64,256]{2,1,0:T(8,128)}), f32[8,64,256]{2,1,0:T(8,128)S(1)}, u32[]{:S(2)}, u32[]{:S(2)}) %all-to-all-start.1) | async-done | bytes 524320 | tf_op jit(solution)/shard_map/all_to_all | solution.py:285
  97.3 2.7 %collective-permute-start.23 = (f32[128,256]{1,0:T(8,128)S(1)}, f32[128,256]{1,0:T(8,128)S(1)}, u32[]{:S(2)}, u32[]{:S(2)}) collective-permute-start(f32[128,256]{1,0:T(8,128)S(1)} %get-tuple-element.72), channel_id=1, source_target_pairs={{0,56},{8,0},{16,8},{24,16},{32,24},{40,32},{48,40},{56,48},{1,57}... | collective-permute-start | bytes 393224 | tf_op jit(solution)/shard_map/ppermute | solution.py:253
  104.4 2.5 %collective-permute-start.25 = (f32[256,128]{1,0:T(8,128)S(1)}, f32[256,128]{1,0:T(8,128)S(1)}, u32[]{:S(2)}, u32[]{:S(2)}) collective-permute-start(f32[256,128]{1,0:T(8,128)S(1)} %fusion.2), channel_id=1, source_target_pairs={{0,128},{64,192},{128,0},{192,64},{1,129},{65,193},{129,1},{193,65... | collective-permute-start | bytes 393224 | tf_op jit(solution)/shard_map/ppermute | solution.py:253
  108.2 2.9 %collective-permute-done.25 = f32[256,128]{1,0:T(8,128)S(1)} collective-permute-done((f32[256,128]{1,0:T(8,128)S(1)}, f32[256,128]{1,0:T(8,128)S(1)}, u32[]{:S(2)}, u32[]{:S(2)}) %collective-permute-start.25) | collective-permute-done | bytes 131104 | tf_op jit(solution)/shard_map/ppermute | solution.py:253
  112.4 10.0 %all_to_all.25 = f32[8,32,128]{2,1,0:T(8,128)S(1)} all-to-all(f32[8,32,128]{2,1,0:T(8,128)S(1)} %bitcast.50), channel_id=1, replica_groups=mesh['gx'=4,'gy'=8,'vert'=8] {'vert'}, dimensions={0} | all-to-all | bytes 262144 | tf_op jit(solution)/shard_map/all_to_all | solution.py:285
  122.4 13.6 %all_to_all.26 = f32[8,32,128]{2,1,0:T(8,128)S(1)} all-to-all(f32[8,32,128]{2,1,0:T(8,128)S(1)} %broadcast_in_dim.4), channel_id=1, replica_groups=mesh['gx'=4,'gy'=8,'vert'=8] {'gy'}, dimensions={0} | all-to-all | bytes 262144 | tf_op jit(solution)/shard_map/all_to_all | solution.py:285
  136.1 10.0 %all_to_all.27 = f32[8,32,128]{2,1,0:T(8,128)S(1)} all-to-all(f32[8,32,128]{2,1,0:T(8,128)S(1)} %broadcast_in_dim.5), channel_id=1, replica_groups=mesh['gx'=4,'gy'=8,'vert'=8] {'vert'}, dimensions={0} | all-to-all | bytes 262144 | tf_op jit(solution)/shard_map/all_to_all | solution.py:285
  (69 shorter events, 11.9 us)
Async XLA Ops:
  0.0 102.7 %copy-start = (f32[1024,128]{1,0:T(8,128)S(1)}, f32[1024,128]{1,0:T(8,128)}, u32[]{:S(2)}) copy-start(f32[1024,128]{1,0:T(8,128)} %param.7) | copy-start | bytes 1572868
  9.9 12.9 %copy-start.1 = (f32[128,128]{1,0:T(8,128)S(1)}, f32[128,128]{1,0:T(8,128)}, u32[]{:S(2)}) copy-start(f32[128,128]{1,0:T(8,128)} %second_ref.2) | copy-start | bytes 196612
  9.9 12.9 %copy-start.2 = (f32[64,128]{1,0:T(8,128)S(1)}, f32[64,128]{1,0:T(8,128)}, u32[]{:S(2)}) copy-start(f32[64,128]{1,0:T(8,128)} %constant.22.clone.pick_ref) | copy-start | bytes 98308
  9.9 59.6 %all-to-all-start = ((f32[8,17,32,256]{3,2,1,0:T(8,128)}), f32[8,17,32,256]{3,2,1,0:T(8,128)}, u32[]{:S(2)}, u32[]{:S(2)}) async-start(f32[8,17,32,256]{3,2,1,0:T(8,128)} %get-tuple-element.60), calls=%async_computation | async-start | bytes 8912896 | tf_op jit(solution)/shard_map/all_to_all | solution.py:285
  18.7 10.4 %collective-permute-start = (f32[4,32,256]{2,1,0:T(8,128)S(1)}, f32[4,32,256]{2,1,0:T(8,128)S(1)}, u32[]{:S(2)}, u32[]{:S(2)}) collective-permute-start(f32[4,32,256]{2,1,0:T(8,128)S(1)} %get-tuple-element.42), channel_id=1, source_target_pairs={{0,8},{8,16},{16,24},{24,32},{32,40},{40,48},{48,56},{56,0},{1,9},... | collective-permute-start | bytes 393224 | tf_op jit(solution)/shard_map/ppermute | solution.py:253
  18.8 10.3 %collective-permute-start.1 = (f32[4,32,256]{2,1,0:T(8,128)S(1)}, f32[4,32,256]{2,1,0:T(8,128)S(1)}, u32[]{:S(2)}, u32[]{:S(2)}) collective-permute-start(f32[4,32,256]{2,1,0:T(8,128)S(1)} %get-tuple-element.43), channel_id=1, source_target_pairs={{0,56},{8,0},{16,8},{24,16},{32,24},{40,32},{48,40},{56,48},{1,57}... | collective-permute-start | bytes 393224 | tf_op jit(solution)/shard_map/ppermute | solution.py:253
  26.4 6.0 %collective-permute-start.8 = (f32[4,32,256]{2,1,0:T(8,128)S(1)}, f32[4,32,256]{2,1,0:T(8,128)S(1)}, u32[]{:S(2)}, u32[]{:S(2)}) collective-permute-start(f32[4,32,256]{2,1,0:T(8,128)S(1)} %get-tuple-element.52), channel_id=1, source_target_pairs={{0,8},{8,16},{16,24},{24,32},{32,40},{40,48},{48,56},{56,0},{1,9},... | collective-permute-start | bytes 393224 | tf_op jit(solution)/shard_map/ppermute | solution.py:253
  26.5 5.9 %collective-permute-start.9 = (f32[4,32,256]{2,1,0:T(8,128)S(1)}, f32[4,32,256]{2,1,0:T(8,128)S(1)}, u32[]{:S(2)}, u32[]{:S(2)}) collective-permute-start(f32[4,32,256]{2,1,0:T(8,128)S(1)} %get-tuple-element.53), channel_id=1, source_target_pairs={{0,56},{8,0},{16,8},{24,16},{32,24},{40,32},{48,40},{56,48},{1,57}... | collective-permute-start | bytes 393224 | tf_op jit(solution)/shard_map/ppermute | solution.py:253
  29.3 8.1 %collective-permute-start.2 = (f32[8,32,256]{2,1,0:T(8,128)S(1)}, f32[8,32,256]{2,1,0:T(8,128)S(1)}, u32[]{:S(2)}, u32[]{:S(2)}) collective-permute-start(f32[8,32,256]{2,1,0:T(8,128)S(1)} %get-tuple-element.44), channel_id=1, source_target_pairs={{0,8},{8,16},{16,24},{24,32},{32,40},{40,48},{48,56},{56,0},{1,9},... | collective-permute-start | bytes 786440 | tf_op jit(solution)/shard_map/ppermute | solution.py:253
  29.3 8.0 %collective-permute-start.3 = (f32[8,32,256]{2,1,0:T(8,128)S(1)}, f32[8,32,256]{2,1,0:T(8,128)S(1)}, u32[]{:S(2)}, u32[]{:S(2)}) collective-permute-start(f32[8,32,256]{2,1,0:T(8,128)S(1)} %get-tuple-element.45), channel_id=1, source_target_pairs={{0,56},{8,0},{16,8},{24,16},{32,24},{40,32},{48,40},{56,48},{1,57}... | collective-permute-start | bytes 786440 | tf_op jit(solution)/shard_map/ppermute | solution.py:253
  32.5 10.6 %collective-permute-start.10 = (f32[8,32,256]{2,1,0:T(8,128)S(1)}, f32[8,32,256]{2,1,0:T(8,128)S(1)}, u32[]{:S(2)}, u32[]{:S(2)}) collective-permute-start(f32[8,32,256]{2,1,0:T(8,128)S(1)} %get-tuple-element.54), channel_id=1, source_target_pairs={{0,8},{8,16},{16,24},{24,32},{32,40},{40,48},{48,56},{56,0},{1,9},... | collective-permute-start | bytes 786440 | tf_op jit(solution)/shard_map/ppermute | solution.py:253
  32.6 10.5 %collective-permute-start.11 = (f32[8,32,256]{2,1,0:T(8,128)S(1)}, f32[8,32,256]{2,1,0:T(8,128)S(1)}, u32[]{:S(2)}, u32[]{:S(2)}) collective-permute-start(f32[8,32,256]{2,1,0:T(8,128)S(1)} %get-tuple-element.55), channel_id=1, source_target_pairs={{0,56},{8,0},{16,8},{24,16},{32,24},{40,32},{48,40},{56,48},{1,57}... | collective-permute-start | bytes 786440 | tf_op jit(solution)/shard_map/ppermute | solution.py:253
  37.4 11.3 %collective-permute-start.4 = (f32[8,32,256]{2,1,0:T(8,128)S(1)}, f32[8,32,256]{2,1,0:T(8,128)S(1)}, u32[]{:S(2)}, u32[]{:S(2)}) collective-permute-start(f32[8,32,256]{2,1,0:T(8,128)S(1)} %get-tuple-element.46), channel_id=1, source_target_pairs={{0,8},{8,16},{16,24},{24,32},{32,40},{40,48},{48,56},{56,0},{1,9},... | collective-permute-start | bytes 786440 | tf_op jit(solution)/shard_map/ppermute | solution.py:253
  37.5 11.2 %collective-permute-start.5 = (f32[8,32,256]{2,1,0:T(8,128)S(1)}, f32[8,32,256]{2,1,0:T(8,128)S(1)}, u32[]{:S(2)}, u32[]{:S(2)}) collective-permute-start(f32[8,32,256]{2,1,0:T(8,128)S(1)} %get-tuple-element.47), channel_id=1, source_target_pairs={{0,56},{8,0},{16,8},{24,16},{32,24},{40,32},{48,40},{56,48},{1,57}... | collective-permute-start | bytes 786440 | tf_op jit(solution)/shard_map/ppermute | solution.py:253
  43.2 11.2 %collective-permute-start.12 = (f32[8,32,256]{2,1,0:T(8,128)S(1)}, f32[8,32,256]{2,1,0:T(8,128)S(1)}, u32[]{:S(2)}, u32[]{:S(2)}) collective-permute-start(f32[8,32,256]{2,1,0:T(8,128)S(1)} %get-tuple-element.56), channel_id=1, source_target_pairs={{0,8},{8,16},{16,24},{24,32},{32,40},{40,48},{48,56},{56,0},{1,9},... | collective-permute-start | bytes 786440 | tf_op jit(solution)/shard_map/ppermute | solution.py:253
  43.3 11.1 %collective-permute-start.13 = (f32[8,32,256]{2,1,0:T(8,128)S(1)}, f32[8,32,256]{2,1,0:T(8,128)S(1)}, u32[]{:S(2)}, u32[]{:S(2)}) collective-permute-start(f32[8,32,256]{2,1,0:T(8,128)S(1)} %get-tuple-element.57), channel_id=1, source_target_pairs={{0,56},{8,0},{16,8},{24,16},{32,24},{40,32},{48,40},{56,48},{1,57}... | collective-permute-start | bytes 786440 | tf_op jit(solution)/shard_map/ppermute | solution.py:253
  48.8 11.2 %collective-permute-start.6 = (f32[8,32,256]{2,1,0:T(8,128)S(1)}, f32[8,32,256]{2,1,0:T(8,128)S(1)}, u32[]{:S(2)}, u32[]{:S(2)}) collective-permute-start(f32[8,32,256]{2,1,0:T(8,128)S(1)} %get-tuple-element.48), channel_id=1, source_target_pairs={{0,8},{8,16},{16,24},{24,32},{32,40},{40,48},{48,56},{56,0},{1,9},... | collective-permute-start | bytes 786440 | tf_op jit(solution)/shard_map/ppermute | solution.py:253
  49.1 10.9 %collective-permute-start.7 = (f32[8,32,256]{2,1,0:T(8,128)S(1)}, f32[8,32,256]{2,1,0:T(8,128)S(1)}, u32[]{:S(2)}, u32[]{:S(2)}) collective-permute-start(f32[8,32,256]{2,1,0:T(8,128)S(1)} %get-tuple-element.49), channel_id=1, source_target_pairs={{0,56},{8,0},{16,8},{24,16},{32,24},{40,32},{48,40},{56,48},{1,57}... | collective-permute-start | bytes 786440 | tf_op jit(solution)/shard_map/ppermute | solution.py:253
  54.4 11.2 %collective-permute-start.14 = (f32[8,32,256]{2,1,0:T(8,128)S(1)}, f32[8,32,256]{2,1,0:T(8,128)S(1)}, u32[]{:S(2)}, u32[]{:S(2)}) collective-permute-start(f32[8,32,256]{2,1,0:T(8,128)S(1)} %get-tuple-element.58), channel_id=1, source_target_pairs={{0,8},{8,16},{16,24},{24,32},{32,40},{40,48},{48,56},{56,0},{1,9},... | collective-permute-start | bytes 786440 | tf_op jit(solution)/shard_map/ppermute | solution.py:253
  54.5 11.1 %collective-permute-start.15 = (f32[8,32,256]{2,1,0:T(8,128)S(1)}, f32[8,32,256]{2,1,0:T(8,128)S(1)}, u32[]{:S(2)}, u32[]{:S(2)}) collective-permute-start(f32[8,32,256]{2,1,0:T(8,128)S(1)} %get-tuple-element.59), channel_id=1, source_target_pairs={{0,56},{8,0},{16,8},{24,16},{32,24},{40,32},{48,40},{56,48},{1,57}... | collective-permute-start | bytes 786440 | tf_op jit(solution)/shard_map/ppermute | solution.py:253
  73.4 5.6 %collective-permute-start.16 = (f32[64,256]{1,0:T(8,128)S(1)}, f32[64,256]{1,0:T(8,128)S(1)}, u32[]{:S(2)}, u32[]{:S(2)}) collective-permute-start(f32[64,256]{1,0:T(8,128)S(1)} %get-tuple-element.62), channel_id=1, source_target_pairs={{0,8},{8,16},{16,24},{24,32},{32,40},{40,48},{48,56},{56,0},{1,9},... | collective-permute-start | bytes 196616 | tf_op jit(solution)/shard_map/ppermute | solution.py:253
  73.5 5.5 %collective-permute-start.17 = (f32[64,256]{1,0:T(8,128)S(1)}, f32[64,256]{1,0:T(8,128)S(1)}, u32[]{:S(2)}, u32[]{:S(2)}) collective-permute-start(f32[64,256]{1,0:T(8,128)S(1)} %get-tuple-element.63), channel_id=1, source_target_pairs={{0,56},{8,0},{16,8},{24,16},{32,24},{40,32},{48,40},{56,48},{1,57}... | collective-permute-start | bytes 196616 | tf_op jit(solution)/shard_map/ppermute | solution.py:253
  79.1 8.6 %collective-permute-start.18 = (f32[128,256]{1,0:T(8,128)S(1)}, f32[128,256]{1,0:T(8,128)S(1)}, u32[]{:S(2)}, u32[]{:S(2)}) collective-permute-start(f32[128,256]{1,0:T(8,128)S(1)} %pad_maximum_fusion.8), channel_id=1, source_target_pairs={{0,8},{8,16},{16,24},{24,32},{32,40},{40,48},{48,56},{56,0},{1,9},... | collective-permute-start | bytes 393224 | tf_op jit(solution)/shard_map/ppermute | solution.py:253
  79.2 8.5 %collective-permute-start.19 = (f32[128,256]{1,0:T(8,128)S(1)}, f32[128,256]{1,0:T(8,128)S(1)}, u32[]{:S(2)}, u32[]{:S(2)}) collective-permute-start(f32[128,256]{1,0:T(8,128)S(1)} %pad_maximum_fusion.9), channel_id=1, source_target_pairs={{0,56},{8,0},{16,8},{24,16},{32,24},{40,32},{48,40},{56,48},{1,57}... | collective-permute-start | bytes 393224 | tf_op jit(solution)/shard_map/ppermute | solution.py:253
  82.0 15.2 %all-to-all-start.1 = ((f32[8,64,256]{2,1,0:T(8,128)}), f32[8,64,256]{2,1,0:T(8,128)S(1)}, u32[]{:S(2)}, u32[]{:S(2)}) async-start(f32[8,64,256]{2,1,0:T(8,128)} %pad_maximum_fusion), calls=%async_computation.1 | async-start | bytes 1048576 | tf_op jit(solution)/shard_map/all_to_all | solution.py:285
  87.7 6.3 %collective-permute-start.20 = (f32[128,256]{1,0:T(8,128)S(1)}, f32[128,256]{1,0:T(8,128)S(1)}, u32[]{:S(2)}, u32[]{:S(2)}) collective-permute-start(f32[128,256]{1,0:T(8,128)S(1)} %get-tuple-element.66), channel_id=1, source_target_pairs={{0,8},{8,16},{16,24},{24,32},{32,40},{40,48},{48,56},{56,0},{1,9},... | collective-permute-start | bytes 393224 | tf_op jit(solution)/shard_map/ppermute | solution.py:253
  87.8 6.2 %collective-permute-start.21 = (f32[128,256]{1,0:T(8,128)S(1)}, f32[128,256]{1,0:T(8,128)S(1)}, u32[]{:S(2)}, u32[]{:S(2)}) collective-permute-start(f32[128,256]{1,0:T(8,128)S(1)} %get-tuple-element.67), channel_id=1, source_target_pairs={{0,56},{8,0},{16,8},{24,16},{32,24},{40,32},{48,40},{56,48},{1,57}... | collective-permute-start | bytes 393224 | tf_op jit(solution)/shard_map/ppermute | solution.py:253
  97.2 5.4 %collective-permute-start.22 = (f32[128,256]{1,0:T(8,128)S(1)}, f32[128,256]{1,0:T(8,128)S(1)}, u32[]{:S(2)}, u32[]{:S(2)}) collective-permute-start(f32[128,256]{1,0:T(8,128)S(1)} %get-tuple-element.71), channel_id=1, source_target_pairs={{0,8},{8,16},{16,24},{24,32},{32,40},{40,48},{48,56},{56,0},{1,9},... | collective-permute-start | bytes 393224 | tf_op jit(solution)/shard_map/ppermute | solution.py:253
  97.3 5.3 %collective-permute-start.23 = (f32[128,256]{1,0:T(8,128)S(1)}, f32[128,256]{1,0:T(8,128)S(1)}, u32[]{:S(2)}, u32[]{:S(2)}) collective-permute-start(f32[128,256]{1,0:T(8,128)S(1)} %get-tuple-element.72), channel_id=1, source_target_pairs={{0,56},{8,0},{16,8},{24,16},{32,24},{40,32},{48,40},{56,48},{1,57}... | collective-permute-start | bytes 393224 | tf_op jit(solution)/shard_map/ppermute | solution.py:253
  103.1 5.1 %collective-permute-start.24 = (f32[256,128]{1,0:T(8,128)S(1)}, f32[256,128]{1,0:T(8,128)S(1)}, u32[]{:S(2)}, u32[]{:S(2)}) collective-permute-start(f32[256,128]{1,0:T(8,128)S(1)} %fusion.2), channel_id=1, source_target_pairs={{0,64},{64,128},{128,192},{192,0},{1,65},{65,129},{129,193},{193,1... | collective-permute-start | bytes 393224 | tf_op jit(solution)/shard_map/ppermute | solution.py:253
  104.4 6.7 %collective-permute-start.25 = (f32[256,128]{1,0:T(8,128)S(1)}, f32[256,128]{1,0:T(8,128)S(1)}, u32[]{:S(2)}, u32[]{:S(2)}) collective-permute-start(f32[256,128]{1,0:T(8,128)S(1)} %fusion.2), channel_id=1, source_target_pairs={{0,128},{64,192},{128,0},{192,64},{1,129},{65,193},{129,1},{193,65... | collective-permute-start | bytes 393224 | tf_op jit(solution)/shard_map/ppermute | solution.py:253
  106.8 4.9 %collective-permute-start.26 = (f32[256,128]{1,0:T(8,128)S(1)}, f32[256,128]{1,0:T(8,128)S(1)}, u32[]{:S(2)}, u32[]{:S(2)}) collective-permute-start(f32[256,128]{1,0:T(8,128)S(1)} %fusion.2), channel_id=1, source_target_pairs={{0,192},{64,0},{128,64},{192,128},{1,193},{65,1},{129,65},{193,129... | collective-permute-start | bytes 393224 | tf_op jit(solution)/shard_map/ppermute | solution.py:253
  (1 other events, 10.4 us)

commit v7 on v6

--- a/solution.py
+++ b/solution.py
@@ -13,6 +13,7 @@
 NN = (((1,), (0,)), ((), ()))
 VMEM_LIMIT = 10 * 2**20
 STEP = 8
+AHEAD = 3
 SETS = 8
 
 
@@ -42,7 +43,7 @@
 
     @pl.when(now == 0)
     def _():
-        for i in range(steps):
+        for i in range(AHEAD):
             fetch(i).start()
         pick = pltpu.roll(pick_ref[...], lax.axis_index("gy") * roll, 1).astype(jnp.bfloat16)
         both_ref[...] = jnp.zeros_like(both_ref)
@@ -51,6 +52,10 @@
             both_ref[part * rows : (part + 1) * rows, :ny] = value
             if part == 0:
                 both_ref[:rows, ny:] = value
+
+    @pl.when(now + AHEAD < steps)
+    def _():
+        fetch(now + AHEAD).start()
 
     fetch(now).wait()
     both = both_ref[...]
@@ -115,7 +120,7 @@
 
     @pl.when(now == 0)
     def _():
-        for i in range(steps):
+        for i in range(AHEAD):
             fetch(i).start()
         for half in range(2):
             pack_ref[:, half * rank : (half + 1) * rank] = third_ref[half * per_half * STEP : (half + 1) * per_half * STEP, :]
@@ -135,6 +140,10 @@
     def _():
         send(now - 2).wait()
 
+    @pl.when(now + AHEAD < steps)
+    def _():
+        fetch(now + AHEAD).start()
+
     fetch(now).wait()
 
     def multiply(with_m):
@@ -207,43 +216,57 @@
     )(jnp.asarray(pick), second, third, field)
 
 
-def depth_kernel(third_ref, one_ref, two_ref, out_ref, both_ref):
+def depth_kernel(third_ref, part_ref, out_ref, both_ref, held_ref, sems):
     rank, nx = out_ref.shape[1:]
-
-    @pl.when(pl.program_id(0) == 0)
-    def _():
+    groups = held_ref.shape[0]
+    now = pl.program_id(0)
+
+    def fetch(g, half):
+        return pltpu.make_async_copy(part_ref.at[:, half * groups + g], held_ref.at[g, half], sems.at[g, half])
+
+    @pl.when(now == 0)
+    def _():
+        for g in range(min(AHEAD, groups)):
+            for half in range(2):
+                fetch(g, half).start()
         halves = [third_ref[:, 0, :, half * rank : (half + 1) * rank].reshape(-1, rank) for half in range(2)]
         high, low = split(jnp.concatenate(halves, 0).T)
         both_ref[:rank] = high
         both_ref[rank:] = low
 
-    for g in range(out_ref.shape[0]):
-        value = jnp.concatenate([ref[:, g].reshape(-1, nx) for ref in (one_ref, two_ref)], 0)
-        out_ref[g] = product(both_ref[:rank], both_ref[...], value)
+    @pl.when(now + AHEAD < groups)
+    def _():
+        for half in range(2):
+            fetch(now + AHEAD, half).start()
+
+    for half in range(2):
+        fetch(now, half).wait()
+    out_ref[0] = product(both_ref[:rank], both_ref[...], held_ref[now].reshape(-1, nx))
 
 
 def depth_product(gathered, part, rank, groups):
     n, count, planes, nx = gathered.shape
-    step = 2 if groups % 2 == 0 else 1
-    block = (n, step, planes, nx)
     return pl.pallas_call(
         depth_kernel,
-        grid=(groups // step,),
+        grid=(groups,),
         in_specs=[
             pl.BlockSpec((n, 1, planes, nx), lambda i: (0, count - 1, 0, 0)),
-            pl.BlockSpec(block, lambda i: (0, i, 0, 0)),
-            pl.BlockSpec(block, lambda i: (0, groups // step + i, 0, 0)),
-        ],
-        out_specs=pl.BlockSpec((step, rank, nx), lambda i: (i, 0, 0)),
+            pl.BlockSpec(memory_space=pl.ANY),
+        ],
+        out_specs=pl.BlockSpec((1, rank, nx), lambda i: (i, 0, 0)),
         out_shape=jax.ShapeDtypeStruct((groups, rank, nx), jnp.float32),
-        scratch_shapes=[pltpu.VMEM((2 * rank, 2 * n * planes), jnp.bfloat16)],
+        scratch_shapes=[
+            pltpu.VMEM((2 * rank, 2 * n * planes), jnp.bfloat16),
+            pltpu.VMEM((groups, 2, n, planes, nx), jnp.float32),
+            pltpu.SemaphoreType.DMA((groups, 2)),
+        ],
         compiler_params=pltpu.CompilerParams(vmem_limit_bytes=VMEM_LIMIT),
         cost_estimate=pl.CostEstimate(
             flops=12 * n * groups * planes * nx * rank,
             bytes_accessed=8 * n * groups * planes * nx,
             transcendentals=0,
         ),
-    )(gathered, part, part)
+    )(gathered, part)
 
 
 def shifts(moves, axis):

time: 147 us -> 148 us (level)
  no operation moved by 1% of the time
where the time goes in v7:
time: 148 us
  starting transfers between devices  54.2 us (37%)
  waiting for transfers between devices  35.4 us (24%)
  blocking collectives  33.7 us (23%)
  Pallas kernels  19.7 us (13%)
  local copies, waits for them, and re-layouts  1.72 us (1%)
  other arithmetic  1.61 us (1%)
    ppermute x27, starting transfers between devices, shifts(): lax.ppermute(value, axis, [(i, (i + by) % n) for i in range(n)])  40.7 us
    all_to_all x3, blocking collectives, trade(): return lax.all_to_all(value, axis, 0, 0)  33.7 us
    ppermute x27, waiting for transfers between devices, shifts(): lax.ppermute(value, axis, [(i, (i + by) % n) for i in range(n)])  29.2 us
    all_to_all x2, starting transfers between devices, trade(): return lax.all_to_all(value, axis, 0, 0)  13.5 us
    pallas_call x1, Pallas kernels, lead_product(): pl.pallas_call(functools.partial(lead_kernel, roll), grid=(steps,), in_sp...  9.87 us
    pallas_call x2, Pallas kernels, depth_product(): pl.pallas_call(depth_kernel, grid=(groups,), in_specs=[pl.BlockSpec((n, 1...  6.21 us
    all_to_all x2, waiting for transfers between devices, trade(): return lax.all_to_all(value, axis, 0, 0)  6.2 us
    pallas_call x1, Pallas kernels, mode_product(): pl.pallas_call(functools.partial(mode_kernel, roll, start // STEP), grid=...  3.59 us
  transfers between devices with their start and end apart: 29, of which 15 were waited for; matrix products, arithmetic and copies ran while one was open for 2% of the time, Pallas kernels for 3%

profile of v7, /device:TPU:1, one launch (start us, length us, event | category | flops | bytes accessed | tf_op | source)
XLA Modules:
  0.0 147.6 jit_solution(9401999672153290308)
XLA Ops:
  0.0 9.9 %shard_map.64 = (f32[8,17,32,256]{3,2,1,0:T(8,128)}, f32[64,32,256]{2,1,0:T(8,128)}) custom-call(f32[128,128]{1,0:T(8,128)} %constant.21.clone.pick_ref, f32[128,128]{1,0:T(8,128)} %second_ref.2, f32[64,128]{1,0:T(8,128)} %bitcast.51, f32[64,256,128]{2,1,0:T(8,128)} %bitcast.47), custom_call_target="tpu_custom_call" | custom-call | flops 1610612736 | bytes 16777216 | tf_op jit(solution)/shard_map/pallas_call | solution.py:184
  9.9 7.8 %all-to-all-start = ((f32[8,17,32,256]{3,2,1,0:T(8,128)}), f32[8,17,32,256]{3,2,1,0:T(8,128)}, u32[]{:S(2)}, u32[]{:S(2)}) async-start(f32[8,17,32,256]{3,2,1,0:T(8,128)} %get-tuple-element.60), calls=%async_computation | async-start | bytes 8912896 | tf_op jit(solution)/shard_map/all_to_all | solution.py:308
  18.8 3.9 %collective-permute-start.1 = (f32[4,32,256]{2,1,0:T(8,128)S(1)}, f32[4,32,256]{2,1,0:T(8,128)S(1)}, u32[]{:S(2)}, u32[]{:S(2)}) collective-permute-start(f32[4,32,256]{2,1,0:T(8,128)S(1)} %get-tuple-element.43), channel_id=1, source_target_pairs={{0,56},{8,0},{16,8},{24,16},{32,24},{40,32},{48,40},{56,48},{1,57}... | collective-permute-start | bytes 393224 | tf_op jit(solution)/shard_map/ppermute | solution.py:276
  22.8 3.6 %shard_map.65 = f32[64,32,256]{2,1,0:T(8,128)S(1)} custom-call(f32[64,128]{1,0:T(8,128)S(1)} %copy-done.2, f32[128,128]{1,0:T(8,128)S(1)} %copy-done.1, f32[64,256,128]{2,1,0:T(8,128)} %bitcast.48), custom_call_target="tpu_custom_call" | custom-call | flops 402653184 | bytes 6291456 | tf_op jit(solution)/shard_map/pallas_call | solution.py:72
  26.5 2.7 %collective-permute-start.9 = (f32[4,32,256]{2,1,0:T(8,128)S(1)}, f32[4,32,256]{2,1,0:T(8,128)S(1)}, u32[]{:S(2)}, u32[]{:S(2)}) collective-permute-start(f32[4,32,256]{2,1,0:T(8,128)S(1)} %get-tuple-element.53), channel_id=1, source_target_pairs={{0,56},{8,0},{16,8},{24,16},{32,24},{40,32},{48,40},{56,48},{1,57}... | collective-permute-start | bytes 393224 | tf_op jit(solution)/shard_map/ppermute | solution.py:276
  29.4 2.7 %collective-permute-start.3 = (f32[8,32,256]{2,1,0:T(8,128)S(1)}, f32[8,32,256]{2,1,0:T(8,128)S(1)}, u32[]{:S(2)}, u32[]{:S(2)}) collective-permute-start(f32[8,32,256]{2,1,0:T(8,128)S(1)} %get-tuple-element.45), channel_id=1, source_target_pairs={{0,56},{8,0},{16,8},{24,16},{32,24},{40,32},{48,40},{56,48},{1,57}... | collective-permute-start | bytes 786440 | tf_op jit(solution)/shard_map/ppermute | solution.py:276
  32.6 2.7 %collective-permute-start.11 = (f32[8,32,256]{2,1,0:T(8,128)S(1)}, f32[8,32,256]{2,1,0:T(8,128)S(1)}, u32[]{:S(2)}, u32[]{:S(2)}) collective-permute-start(f32[8,32,256]{2,1,0:T(8,128)S(1)} %get-tuple-element.55), channel_id=1, source_target_pairs={{0,56},{8,0},{16,8},{24,16},{32,24},{40,32},{48,40},{56,48},{1,57}... | collective-permute-start | bytes 786440 | tf_op jit(solution)/shard_map/ppermute | solution.py:276
  35.3 2.1 %collective-permute-done.2 = f32[8,32,256]{2,1,0:T(8,128)S(1)} collective-permute-done((f32[8,32,256]{2,1,0:T(8,128)S(1)}, f32[8,32,256]{2,1,0:T(8,128)S(1)}, u32[]{:S(2)}, u32[]{:S(2)}) %collective-permute-start.2) | collective-permute-done | bytes 262176 | tf_op jit(solution)/shard_map/ppermute | solution.py:276
  37.5 2.7 %collective-permute-start.5 = (f32[8,32,256]{2,1,0:T(8,128)S(1)}, f32[8,32,256]{2,1,0:T(8,128)S(1)}, u32[]{:S(2)}, u32[]{:S(2)}) collective-permute-start(f32[8,32,256]{2,1,0:T(8,128)S(1)} %get-tuple-element.47), channel_id=1, source_target_pairs={{0,56},{8,0},{16,8},{24,16},{32,24},{40,32},{48,40},{56,48},{1,57}... | collective-permute-start | bytes 786440 | tf_op jit(solution)/shard_map/ppermute | solution.py:276
  40.2 2.9 %collective-permute-done.10 = f32[8,32,256]{2,1,0:T(8,128)S(1)} collective-permute-done((f32[8,32,256]{2,1,0:T(8,128)S(1)}, f32[8,32,256]{2,1,0:T(8,128)S(1)}, u32[]{:S(2)}, u32[]{:S(2)}) %collective-permute-start.10) | collective-permute-done | bytes 262176 | tf_op jit(solution)/shard_map/ppermute | solution.py:276
  43.3 2.7 %collective-permute-start.13 = (f32[8,32,256]{2,1,0:T(8,128)S(1)}, f32[8,32,256]{2,1,0:T(8,128)S(1)}, u32[]{:S(2)}, u32[]{:S(2)}) collective-permute-start(f32[8,32,256]{2,1,0:T(8,128)S(1)} %get-tuple-element.57), channel_id=1, source_target_pairs={{0,56},{8,0},{16,8},{24,16},{32,24},{40,32},{48,40},{56,48},{1,57}... | collective-permute-start | bytes 786440 | tf_op jit(solution)/shard_map/ppermute | solution.py:276
  45.9 2.8 %collective-permute-done.4 = f32[8,32,256]{2,1,0:T(8,128)S(1)} collective-permute-done((f32[8,32,256]{2,1,0:T(8,128)S(1)}, f32[8,32,256]{2,1,0:T(8,128)S(1)}, u32[]{:S(2)}, u32[]{:S(2)}) %collective-permute-start.4) | collective-permute-done | bytes 262176 | tf_op jit(solution)/shard_map/ppermute | solution.py:276
  49.1 2.7 %collective-permute-start.7 = (f32[8,32,256]{2,1,0:T(8,128)S(1)}, f32[8,32,256]{2,1,0:T(8,128)S(1)}, u32[]{:S(2)}, u32[]{:S(2)}) collective-permute-start(f32[8,32,256]{2,1,0:T(8,128)S(1)} %get-tuple-element.49), channel_id=1, source_target_pairs={{0,56},{8,0},{16,8},{24,16},{32,24},{40,32},{48,40},{56,48},{1,57}... | collective-permute-start | bytes 786440 | tf_op jit(solution)/shard_map/ppermute | solution.py:276
  51.7 2.6 %collective-permute-done.12 = f32[8,32,256]{2,1,0:T(8,128)S(1)} collective-permute-done((f32[8,32,256]{2,1,0:T(8,128)S(1)}, f32[8,32,256]{2,1,0:T(8,128)S(1)}, u32[]{:S(2)}, u32[]{:S(2)}) %collective-permute-start.12) | collective-permute-done | bytes 262176 | tf_op jit(solution)/shard_map/ppermute | solution.py:276
  54.5 2.7 %collective-permute-start.15 = (f32[8,32,256]{2,1,0:T(8,128)S(1)}, f32[8,32,256]{2,1,0:T(8,128)S(1)}, u32[]{:S(2)}, u32[]{:S(2)}) collective-permute-start(f32[8,32,256]{2,1,0:T(8,128)S(1)} %get-tuple-element.59), channel_id=1, source_target_pairs={{0,56},{8,0},{16,8},{24,16},{32,24},{40,32},{48,40},{56,48},{1,57}... | collective-permute-start | bytes 786440 | tf_op jit(solution)/shard_map/ppermute | solution.py:276
  57.2 2.8 %collective-permute-done.6 = f32[8,32,256]{2,1,0:T(8,128)S(1)} collective-permute-done((f32[8,32,256]{2,1,0:T(8,128)S(1)}, f32[8,32,256]{2,1,0:T(8,128)S(1)}, u32[]{:S(2)}, u32[]{:S(2)}) %collective-permute-start.6) | collective-permute-done | bytes 262176 | tf_op jit(solution)/shard_map/ppermute | solution.py:276
  60.0 5.6 %collective-permute-done.14 = f32[8,32,256]{2,1,0:T(8,128)S(1)} collective-permute-done((f32[8,32,256]{2,1,0:T(8,128)S(1)}, f32[8,32,256]{2,1,0:T(8,128)S(1)}, u32[]{:S(2)}, u32[]{:S(2)}) %collective-permute-start.14) | collective-permute-done | bytes 262176 | tf_op jit(solution)/shard_map/ppermute | solution.py:276
  66.5 3.0 %all-to-all-done.third_ref.part_ref = f32[8,17,32,256]{3,2,1,0:T(8,128)} async-done(((f32[8,17,32,256]{3,2,1,0:T(8,128)}), f32[8,17,32,256]{3,2,1,0:T(8,128)}, u32[]{:S(2)}, u32[]{:S(2)}) %all-to-all-start) | async-done | bytes 4456480 | tf_op jit(solution)/shard_map/all_to_all | solution.py:308
  69.5 4.8 %shard_map.66 = f32[8,128,256]{2,1,0:T(8,128)S(1)} custom-call(f32[8,17,32,256]{3,2,1,0:T(8,128)} %all-to-all-done.third_ref.part_ref, f32[8,17,32,256]{3,2,1,0:T(8,128)} %all-to-all-done.third_ref.part_ref), custom_call_target="tpu_custom_call" | custom-call | flops 805306368 | bytes 4194304 | tf_op jit(solution)/shard_map/pallas_call | solution.py:249
  74.4 3.9 %collective-permute-start.17 = (f32[64,256]{1,0:T(8,128)S(1)}, f32[64,256]{1,0:T(8,128)S(1)}, u32[]{:S(2)}, u32[]{:S(2)}) collective-permute-start(f32[64,256]{1,0:T(8,128)S(1)} %get-tuple-element.63), channel_id=1, source_target_pairs={{0,56},{8,0},{16,8},{24,16},{32,24},{40,32},{48,40},{56,48},{1,57}... | collective-permute-start | bytes 196616 | tf_op jit(solution)/shard_map/ppermute | solution.py:276
  78.3 1.6 %collective-permute-done.16 = f32[64,256]{1,0:T(8,128)S(1)} collective-permute-done((f32[64,256]{1,0:T(8,128)S(1)}, f32[64,256]{1,0:T(8,128)S(1)}, u32[]{:S(2)}, u32[]{:S(2)}) %collective-permute-start.16) | collective-permute-done | bytes 65568 | tf_op jit(solution)/shard_map/ppermute | solution.py:276
  80.0 2.8 %collective-permute-start.19 = (f32[128,256]{1,0:T(8,128)S(1)}, f32[128,256]{1,0:T(8,128)S(1)}, u32[]{:S(2)}, u32[]{:S(2)}) collective-permute-start(f32[128,256]{1,0:T(8,128)S(1)} %pad_maximum_fusion.9), channel_id=1, source_target_pairs={{0,56},{8,0},{16,8},{24,16},{32,24},{40,32},{48,40},{56,48},{1,57}... | collective-permute-start | bytes 393224 | tf_op jit(solution)/shard_map/ppermute | solution.py:276
  82.9 5.7 %all-to-all-start.1 = ((f32[8,64,256]{2,1,0:T(8,128)}), f32[8,64,256]{2,1,0:T(8,128)S(1)}, u32[]{:S(2)}, u32[]{:S(2)}) async-start(f32[8,64,256]{2,1,0:T(8,128)} %pad_maximum_fusion), calls=%async_computation.1 | async-start | bytes 1048576 | tf_op jit(solution)/shard_map/all_to_all | solution.py:308
  88.7 2.7 %collective-permute-start.21 = (f32[128,256]{1,0:T(8,128)S(1)}, f32[128,256]{1,0:T(8,128)S(1)}, u32[]{:S(2)}, u32[]{:S(2)}) collective-permute-start(f32[128,256]{1,0:T(8,128)S(1)} %get-tuple-element.67), channel_id=1, source_target_pairs={{0,56},{8,0},{16,8},{24,16},{32,24},{40,32},{48,40},{56,48},{1,57}... | collective-permute-start | bytes 393224 | tf_op jit(solution)/shard_map/ppermute | solution.py:276
  91.4 3.5 %collective-permute-done.20 = f32[128,256]{1,0:T(8,128)S(1)} collective-permute-done((f32[128,256]{1,0:T(8,128)S(1)}, f32[128,256]{1,0:T(8,128)S(1)}, u32[]{:S(2)}, u32[]{:S(2)}) %collective-permute-start.20) | collective-permute-done | bytes 131104 | tf_op jit(solution)/shard_map/ppermute | solution.py:276
  94.9 3.2 %all-to-all-done.1 = f32[8,64,256]{2,1,0:T(8,128)S(1)} async-done(((f32[8,64,256]{2,1,0:T(8,128)}), f32[8,64,256]{2,1,0:T(8,128)S(1)}, u32[]{:S(2)}, u32[]{:S(2)}) %all-to-all-start.1) | async-done | bytes 524320 | tf_op jit(solution)/shard_map/all_to_all | solution.py:308
  98.2 2.7 %collective-permute-start.23 = (f32[128,256]{1,0:T(8,128)S(1)}, f32[128,256]{1,0:T(8,128)S(1)}, u32[]{:S(2)}, u32[]{:S(2)}) collective-permute-start(f32[128,256]{1,0:T(8,128)S(1)} %get-tuple-element.72), channel_id=1, source_target_pairs={{0,56},{8,0},{16,8},{24,16},{32,24},{40,32},{48,40},{56,48},{1,57}... | collective-permute-start | bytes 393224 | tf_op jit(solution)/shard_map/ppermute | solution.py:276
  105.3 2.4 %collective-permute-start.25 = (f32[256,128]{1,0:T(8,128)S(1)}, f32[256,128]{1,0:T(8,128)S(1)}, u32[]{:S(2)}, u32[]{:S(2)}) collective-permute-start(f32[256,128]{1,0:T(8,128)S(1)} %fusion.2), channel_id=1, source_target_pairs={{0,128},{64,192},{128,0},{192,64},{1,129},{65,193},{129,1},{193,65... | collective-permute-start | bytes 393224 | tf_op jit(solution)/shard_map/ppermute | solution.py:276
  109.1 2.9 %collective-permute-done.25 = f32[256,128]{1,0:T(8,128)S(1)} collective-permute-done((f32[256,128]{1,0:T(8,128)S(1)}, f32[256,128]{1,0:T(8,128)S(1)}, u32[]{:S(2)}, u32[]{:S(2)}) %collective-permute-start.25) | collective-permute-done | bytes 131104 | tf_op jit(solution)/shard_map/ppermute | solution.py:276
  113.2 10.0 %all_to_all.25 = f32[8,32,128]{2,1,0:T(8,128)S(1)} all-to-all(f32[8,32,128]{2,1,0:T(8,128)S(1)} %bitcast.49), channel_id=1, replica_groups=mesh['gx'=4,'gy'=8,'vert'=8] {'vert'}, dimensions={0} | all-to-all | bytes 262144 | tf_op jit(solution)/shard_map/all_to_all | solution.py:308
  123.3 13.6 %all_to_all.26 = f32[8,32,128]{2,1,0:T(8,128)S(1)} all-to-all(f32[8,32,128]{2,1,0:T(8,128)S(1)} %broadcast_in_dim.4), channel_id=1, replica_groups=mesh['gx'=4,'gy'=8,'vert'=8] {'gy'}, dimensions={0} | all-to-all | bytes 262144 | tf_op jit(solution)/shard_map/all_to_all | solution.py:308
  136.9 10.0 %all_to_all.27 = f32[8,32,128]{2,1,0:T(8,128)S(1)} all-to-all(f32[8,32,128]{2,1,0:T(8,128)S(1)} %broadcast_in_dim.5), channel_id=1, replica_groups=mesh['gx'=4,'gy'=8,'vert'=8] {'vert'}, dimensions={0} | all-to-all | bytes 262144 | tf_op jit(solution)/shard_map/all_to_all | solution.py:308
  (69 shorter events, 11.9 us)
Async XLA Ops:
  0.0 103.6 %copy-start = (f32[1024,128]{1,0:T(8,128)S(1)}, f32[1024,128]{1,0:T(8,128)}, u32[]{:S(2)}) copy-start(f32[1024,128]{1,0:T(8,128)} %param.7) | copy-start | bytes 1572868
  9.9 12.9 %copy-start.1 = (f32[128,128]{1,0:T(8,128)S(1)}, f32[128,128]{1,0:T(8,128)}, u32[]{:S(2)}) copy-start(f32[128,128]{1,0:T(8,128)} %second_ref.2) | copy-start | bytes 196612
  9.9 12.9 %copy-start.2 = (f32[64,128]{1,0:T(8,128)S(1)}, f32[64,128]{1,0:T(8,128)}, u32[]{:S(2)}) copy-start(f32[64,128]{1,0:T(8,128)} %constant.22.clone.pick_ref) | copy-start | bytes 98308
  9.9 59.6 %all-to-all-start = ((f32[8,17,32,256]{3,2,1,0:T(8,128)}), f32[8,17,32,256]{3,2,1,0:T(8,128)}, u32[]{:S(2)}, u32[]{:S(2)}) async-start(f32[8,17,32,256]{3,2,1,0:T(8,128)} %get-tuple-element.60), calls=%async_computation | async-start | bytes 8912896 | tf_op jit(solution)/shard_map/all_to_all | solution.py:308
  18.7 10.4 %collective-permute-start = (f32[4,32,256]{2,1,0:T(8,128)S(1)}, f32[4,32,256]{2,1,0:T(8,128)S(1)}, u32[]{:S(2)}, u32[]{:S(2)}) collective-permute-start(f32[4,32,256]{2,1,0:T(8,128)S(1)} %get-tuple-element.42), channel_id=1, source_target_pairs={{0,8},{8,16},{16,24},{24,32},{32,40},{40,48},{48,56},{56,0},{1,9},... | collective-permute-start | bytes 393224 | tf_op jit(solution)/shard_map/ppermute | solution.py:276
  18.8 10.3 %collective-permute-start.1 = (f32[4,32,256]{2,1,0:T(8,128)S(1)}, f32[4,32,256]{2,1,0:T(8,128)S(1)}, u32[]{:S(2)}, u32[]{:S(2)}) collective-permute-start(f32[4,32,256]{2,1,0:T(8,128)S(1)} %get-tuple-element.43), channel_id=1, source_target_pairs={{0,56},{8,0},{16,8},{24,16},{32,24},{40,32},{48,40},{56,48},{1,57}... | collective-permute-start | bytes 393224 | tf_op jit(solution)/shard_map/ppermute | solution.py:276
  26.4 6.0 %collective-permute-start.8 = (f32[4,32,256]{2,1,0:T(8,128)S(1)}, f32[4,32,256]{2,1,0:T(8,128)S(1)}, u32[]{:S(2)}, u32[]{:S(2)}) collective-permute-start(f32[4,32,256]{2,1,0:T(8,128)S(1)} %get-tuple-element.52), channel_id=1, source_target_pairs={{0,8},{8,16},{16,24},{24,32},{32,40},{40,48},{48,56},{56,0},{1,9},... | collective-permute-start | bytes 393224 | tf_op jit(solution)/shard_map/ppermute | solution.py:276
  26.5 6.0 %collective-permute-start.9 = (f32[4,32,256]{2,1,0:T(8,128)S(1)}, f32[4,32,256]{2,1,0:T(8,128)S(1)}, u32[]{:S(2)}, u32[]{:S(2)}) collective-permute-start(f32[4,32,256]{2,1,0:T(8,128)S(1)} %get-tuple-element.53), channel_id=1, source_target_pairs={{0,56},{8,0},{16,8},{24,16},{32,24},{40,32},{48,40},{56,48},{1,57}... | collective-permute-start | bytes 393224 | tf_op jit(solution)/shard_map/ppermute | solution.py:276
  29.3 8.1 %collective-permute-start.2 = (f32[8,32,256]{2,1,0:T(8,128)S(1)}, f32[8,32,256]{2,1,0:T(8,128)S(1)}, u32[]{:S(2)}, u32[]{:S(2)}) collective-permute-start(f32[8,32,256]{2,1,0:T(8,128)S(1)} %get-tuple-element.44), channel_id=1, source_target_pairs={{0,8},{8,16},{16,24},{24,32},{32,40},{40,48},{48,56},{56,0},{1,9},... | collective-permute-start | bytes 786440 | tf_op jit(solution)/shard_map/ppermute | solution.py:276
  29.4 8.0 %collective-permute-start.3 = (f32[8,32,256]{2,1,0:T(8,128)S(1)}, f32[8,32,256]{2,1,0:T(8,128)S(1)}, u32[]{:S(2)}, u32[]{:S(2)}) collective-permute-start(f32[8,32,256]{2,1,0:T(8,128)S(1)} %get-tuple-element.45), channel_id=1, source_target_pairs={{0,56},{8,0},{16,8},{24,16},{32,24},{40,32},{48,40},{56,48},{1,57}... | collective-permute-start | bytes 786440 | tf_op jit(solution)/shard_map/ppermute | solution.py:276
  32.5 10.6 %collective-permute-start.10 = (f32[8,32,256]{2,1,0:T(8,128)S(1)}, f32[8,32,256]{2,1,0:T(8,128)S(1)}, u32[]{:S(2)}, u32[]{:S(2)}) collective-permute-start(f32[8,32,256]{2,1,0:T(8,128)S(1)} %get-tuple-element.54), channel_id=1, source_target_pairs={{0,8},{8,16},{16,24},{24,32},{32,40},{40,48},{48,56},{56,0},{1,9},... | collective-permute-start | bytes 786440 | tf_op jit(solution)/shard_map/ppermute | solution.py:276
  32.6 10.5 %collective-permute-start.11 = (f32[8,32,256]{2,1,0:T(8,128)S(1)}, f32[8,32,256]{2,1,0:T(8,128)S(1)}, u32[]{:S(2)}, u32[]{:S(2)}) collective-permute-start(f32[8,32,256]{2,1,0:T(8,128)S(1)} %get-tuple-element.55), channel_id=1, source_target_pairs={{0,56},{8,0},{16,8},{24,16},{32,24},{40,32},{48,40},{56,48},{1,57}... | collective-permute-start | bytes 786440 | tf_op jit(solution)/shard_map/ppermute | solution.py:276
  37.5 11.3 %collective-permute-start.4 = (f32[8,32,256]{2,1,0:T(8,128)S(1)}, f32[8,32,256]{2,1,0:T(8,128)S(1)}, u32[]{:S(2)}, u32[]{:S(2)}) collective-permute-start(f32[8,32,256]{2,1,0:T(8,128)S(1)} %get-tuple-element.46), channel_id=1, source_target_pairs={{0,8},{8,16},{16,24},{24,32},{32,40},{40,48},{48,56},{56,0},{1,9},... | collective-permute-start | bytes 786440 | tf_op jit(solution)/shard_map/ppermute | solution.py:276
  37.5 11.2 %collective-permute-start.5 = (f32[8,32,256]{2,1,0:T(8,128)S(1)}, f32[8,32,256]{2,1,0:T(8,128)S(1)}, u32[]{:S(2)}, u32[]{:S(2)}) collective-permute-start(f32[8,32,256]{2,1,0:T(8,128)S(1)} %get-tuple-element.47), channel_id=1, source_target_pairs={{0,56},{8,0},{16,8},{24,16},{32,24},{40,32},{48,40},{56,48},{1,57}... | collective-permute-start | bytes 786440 | tf_op jit(solution)/shard_map/ppermute | solution.py:276
  43.2 11.2 %collective-permute-start.12 = (f32[8,32,256]{2,1,0:T(8,128)S(1)}, f32[8,32,256]{2,1,0:T(8,128)S(1)}, u32[]{:S(2)}, u32[]{:S(2)}) collective-permute-start(f32[8,32,256]{2,1,0:T(8,128)S(1)} %get-tuple-element.56), channel_id=1, source_target_pairs={{0,8},{8,16},{16,24},{24,32},{32,40},{40,48},{48,56},{56,0},{1,9},... | collective-permute-start | bytes 786440 | tf_op jit(solution)/shard_map/ppermute | solution.py:276
  43.3 11.1 %collective-permute-start.13 = (f32[8,32,256]{2,1,0:T(8,128)S(1)}, f32[8,32,256]{2,1,0:T(8,128)S(1)}, u32[]{:S(2)}, u32[]{:S(2)}) collective-permute-start(f32[8,32,256]{2,1,0:T(8,128)S(1)} %get-tuple-element.57), channel_id=1, source_target_pairs={{0,56},{8,0},{16,8},{24,16},{32,24},{40,32},{48,40},{56,48},{1,57}... | collective-permute-start | bytes 786440 | tf_op jit(solution)/shard_map/ppermute | solution.py:276
  48.8 11.2 %collective-permute-start.6 = (f32[8,32,256]{2,1,0:T(8,128)S(1)}, f32[8,32,256]{2,1,0:T(8,128)S(1)}, u32[]{:S(2)}, u32[]{:S(2)}) collective-permute-start(f32[8,32,256]{2,1,0:T(8,128)S(1)} %get-tuple-element.48), channel_id=1, source_target_pairs={{0,8},{8,16},{16,24},{24,32},{32,40},{40,48},{48,56},{56,0},{1,9},... | collective-permute-start | bytes 786440 | tf_op jit(solution)/shard_map/ppermute | solution.py:276
  49.1 10.9 %collective-permute-start.7 = (f32[8,32,256]{2,1,0:T(8,128)S(1)}, f32[8,32,256]{2,1,0:T(8,128)S(1)}, u32[]{:S(2)}, u32[]{:S(2)}) collective-permute-start(f32[8,32,256]{2,1,0:T(8,128)S(1)} %get-tuple-element.49), channel_id=1, source_target_pairs={{0,56},{8,0},{16,8},{24,16},{32,24},{40,32},{48,40},{56,48},{1,57}... | collective-permute-start | bytes 786440 | tf_op jit(solution)/shard_map/ppermute | solution.py:276
  54.4 11.2 %collective-permute-start.14 = (f32[8,32,256]{2,1,0:T(8,128)S(1)}, f32[8,32,256]{2,1,0:T(8,128)S(1)}, u32[]{:S(2)}, u32[]{:S(2)}) collective-permute-start(f32[8,32,256]{2,1,0:T(8,128)S(1)} %get-tuple-element.58), channel_id=1, source_target_pairs={{0,8},{8,16},{16,24},{24,32},{32,40},{40,48},{48,56},{56,0},{1,9},... | collective-permute-start | bytes 786440 | tf_op jit(solution)/shard_map/ppermute | solution.py:276
  54.5 11.1 %collective-permute-start.15 = (f32[8,32,256]{2,1,0:T(8,128)S(1)}, f32[8,32,256]{2,1,0:T(8,128)S(1)}, u32[]{:S(2)}, u32[]{:S(2)}) collective-permute-start(f32[8,32,256]{2,1,0:T(8,128)S(1)} %get-tuple-element.59), channel_id=1, source_target_pairs={{0,56},{8,0},{16,8},{24,16},{32,24},{40,32},{48,40},{56,48},{1,57}... | collective-permute-start | bytes 786440 | tf_op jit(solution)/shard_map/ppermute | solution.py:276
  74.3 5.6 %collective-permute-start.16 = (f32[64,256]{1,0:T(8,128)S(1)}, f32[64,256]{1,0:T(8,128)S(1)}, u32[]{:S(2)}, u32[]{:S(2)}) collective-permute-start(f32[64,256]{1,0:T(8,128)S(1)} %get-tuple-element.62), channel_id=1, source_target_pairs={{0,8},{8,16},{16,24},{24,32},{32,40},{40,48},{48,56},{56,0},{1,9},... | collective-permute-start | bytes 196616 | tf_op jit(solution)/shard_map/ppermute | solution.py:276
  74.4 5.5 %collective-permute-start.17 = (f32[64,256]{1,0:T(8,128)S(1)}, f32[64,256]{1,0:T(8,128)S(1)}, u32[]{:S(2)}, u32[]{:S(2)}) collective-permute-start(f32[64,256]{1,0:T(8,128)S(1)} %get-tuple-element.63), channel_id=1, source_target_pairs={{0,56},{8,0},{16,8},{24,16},{32,24},{40,32},{48,40},{56,48},{1,57}... | collective-permute-start | bytes 196616 | tf_op jit(solution)/shard_map/ppermute | solution.py:276
  79.9 8.6 %collective-permute-start.18 = (f32[128,256]{1,0:T(8,128)S(1)}, f32[128,256]{1,0:T(8,128)S(1)}, u32[]{:S(2)}, u32[]{:S(2)}) collective-permute-start(f32[128,256]{1,0:T(8,128)S(1)} %pad_maximum_fusion.8), channel_id=1, source_target_pairs={{0,8},{8,16},{16,24},{24,32},{32,40},{40,48},{48,56},{56,0},{1,9},... | collective-permute-start | bytes 393224 | tf_op jit(solution)/shard_map/ppermute | solution.py:276
  80.0 8.5 %collective-permute-start.19 = (f32[128,256]{1,0:T(8,128)S(1)}, f32[128,256]{1,0:T(8,128)S(1)}, u32[]{:S(2)}, u32[]{:S(2)}) collective-permute-start(f32[128,256]{1,0:T(8,128)S(1)} %pad_maximum_fusion.9), channel_id=1, source_target_pairs={{0,56},{8,0},{16,8},{24,16},{32,24},{40,32},{48,40},{56,48},{1,57}... | collective-permute-start | bytes 393224 | tf_op jit(solution)/shard_map/ppermute | solution.py:276
  82.9 15.2 %all-to-all-start.1 = ((f32[8,64,256]{2,1,0:T(8,128)}), f32[8,64,256]{2,1,0:T(8,128)S(1)}, u32[]{:S(2)}, u32[]{:S(2)}) async-start(f32[8,64,256]{2,1,0:T(8,128)} %pad_maximum_fusion), calls=%async_computation.1 | async-start | bytes 1048576 | tf_op jit(solution)/shard_map/all_to_all | solution.py:308
  88.6 6.3 %collective-permute-start.20 = (f32[128,256]{1,0:T(8,128)S(1)}, f32[128,256]{1,0:T(8,128)S(1)}, u32[]{:S(2)}, u32[]{:S(2)}) collective-permute-start(f32[128,256]{1,0:T(8,128)S(1)} %get-tuple-element.66), channel_id=1, source_target_pairs={{0,8},{8,16},{16,24},{24,32},{32,40},{40,48},{48,56},{56,0},{1,9},... | collective-permute-start | bytes 393224 | tf_op jit(solution)/shard_map/ppermute | solution.py:276
  88.7 6.2 %collective-permute-start.21 = (f32[128,256]{1,0:T(8,128)S(1)}, f32[128,256]{1,0:T(8,128)S(1)}, u32[]{:S(2)}, u32[]{:S(2)}) collective-permute-start(f32[128,256]{1,0:T(8,128)S(1)} %get-tuple-element.67), channel_id=1, source_target_pairs={{0,56},{8,0},{16,8},{24,16},{32,24},{40,32},{48,40},{56,48},{1,57}... | collective-permute-start | bytes 393224 | tf_op jit(solution)/shard_map/ppermute | solution.py:276
  98.1 5.4 %collective-permute-start.22 = (f32[128,256]{1,0:T(8,128)S(1)}, f32[128,256]{1,0:T(8,128)S(1)}, u32[]{:S(2)}, u32[]{:S(2)}) collective-permute-start(f32[128,256]{1,0:T(8,128)S(1)} %get-tuple-element.71), channel_id=1, source_target_pairs={{0,8},{8,16},{16,24},{24,32},{32,40},{40,48},{48,56},{56,0},{1,9},... | collective-permute-start | bytes 393224 | tf_op jit(solution)/shard_map/ppermute | solution.py:276
  98.2 5.3 %collective-permute-start.23 = (f32[128,256]{1,0:T(8,128)S(1)}, f32[128,256]{1,0:T(8,128)S(1)}, u32[]{:S(2)}, u32[]{:S(2)}) collective-permute-start(f32[128,256]{1,0:T(8,128)S(1)} %get-tuple-element.72), channel_id=1, source_target_pairs={{0,56},{8,0},{16,8},{24,16},{32,24},{40,32},{48,40},{56,48},{1,57}... | collective-permute-start | bytes 393224 | tf_op jit(solution)/shard_map/ppermute | solution.py:276
  104.0 5.1 %collective-permute-start.24 = (f32[256,128]{1,0:T(8,128)S(1)}, f32[256,128]{1,0:T(8,128)S(1)}, u32[]{:S(2)}, u32[]{:S(2)}) collective-permute-start(f32[256,128]{1,0:T(8,128)S(1)} %fusion.2), channel_id=1, source_target_pairs={{0,64},{64,128},{128,192},{192,0},{1,65},{65,129},{129,193},{193,1... | collective-permute-start | bytes 393224 | tf_op jit(solution)/shard_map/ppermute | solution.py:276
  105.3 6.7 %collective-permute-start.25 = (f32[256,128]{1,0:T(8,128)S(1)}, f32[256,128]{1,0:T(8,128)S(1)}, u32[]{:S(2)}, u32[]{:S(2)}) collective-permute-start(f32[256,128]{1,0:T(8,128)S(1)} %fusion.2), channel_id=1, source_target_pairs={{0,128},{64,192},{128,0},{192,64},{1,129},{65,193},{129,1},{193,65... | collective-permute-start | bytes 393224 | tf_op jit(solution)/shard_map/ppermute | solution.py:276
  107.7 4.9 %collective-permute-start.26 = (f32[256,128]{1,0:T(8,128)S(1)}, f32[256,128]{1,0:T(8,128)S(1)}, u32[]{:S(2)}, u32[]{:S(2)}) collective-permute-start(f32[256,128]{1,0:T(8,128)S(1)} %fusion.2), channel_id=1, source_target_pairs={{0,192},{64,0},{128,64},{192,128},{1,193},{65,1},{129,65},{193,129... | collective-permute-start | bytes 393224 | tf_op jit(solution)/shard_map/ppermute | solution.py:276
  (1 other events, 10.4 us)

commit v8 on v6

--- a/solution.py
+++ b/solution.py
@@ -12,7 +12,7 @@
 NT = (((1,), (1,)), ((), ()))
 NN = (((1,), (0,)), ((), ()))
 VMEM_LIMIT = 10 * 2**20
-STEP = 8
+STEP = 16
 SETS = 8
 
 

time: 147 us -> 147 us (level)
  no operation moved by 1% of the time
where the time goes in v8:
time: 147 us; the launch traced here: 146 us
  starting transfers between devices  54.1 us (37%)
  waiting for transfers between devices  35.7 us (24%)
  blocking collectives  33.7 us (23%)
  Pallas kernels  17.9 us (12%)
  local copies, waits for them, and re-layouts  1.72 us (1%)
  other arithmetic  1.61 us (1%)
    ppermute x27, starting transfers between devices, shifts(): lax.ppermute(value, axis, [(i, (i + by) % n) for i in range(n)])  40.5 us
    all_to_all x3, blocking collectives, trade(): return lax.all_to_all(value, axis, 0, 0)  33.7 us
    ppermute x27, waiting for transfers between devices, shifts(): lax.ppermute(value, axis, [(i, (i + by) % n) for i in range(n)])  29.5 us
    all_to_all x2, starting transfers between devices, trade(): return lax.all_to_all(value, axis, 0, 0)  13.5 us
    pallas_call x1, Pallas kernels, lead_product(): pl.pallas_call(functools.partial(lead_kernel, roll), grid=(steps,), in_sp...  9.14 us
    all_to_all x2, waiting for transfers between devices, trade(): return lax.all_to_all(value, axis, 0, 0)  6.18 us
    pallas_call x2, Pallas kernels, depth_product(): pl.pallas_call(depth_kernel, grid=(groups // step,), in_specs=[pl.BlockSp...  5.2 us
    pallas_call x1, Pallas kernels, mode_product(): pl.pallas_call(functools.partial(mode_kernel, roll, start // STEP), grid=...  3.61 us
  transfers between devices with their start and end apart: 29, of which 15 were waited for; matrix products, arithmetic and copies ran while one was open for 2% of the time, Pallas kernels for 3%

profile of v8, /device:TPU:1, one launch (start us, length us, event | category | flops | bytes accessed | tf_op | source)
XLA Modules:
  0.0 146.0 jit_solution(3308734394078954107)
XLA Ops:
  0.0 9.1 %shard_map.64 = (f32[8,17,32,256]{3,2,1,0:T(8,128)}, f32[64,32,256]{2,1,0:T(8,128)}) custom-call(f32[128,128]{1,0:T(8,128)} %constant.21.clone.pick_ref, f32[128,128]{1,0:T(8,128)} %second_ref.2, f32[64,128]{1,0:T(8,128)} %bitcast.52, f32[64,256,128]{2,1,0:T(8,128)} %bitcast.48), custom_call_target="tpu_custom_call" | custom-call | flops 1610612736 | bytes 16777216 | tf_op jit(solution)/shard_map/pallas_call | solution.py:175
  9.2 7.8 %all-to-all-start = ((f32[8,17,32,256]{3,2,1,0:T(8,128)}), f32[8,17,32,256]{3,2,1,0:T(8,128)}, u32[]{:S(2)}, u32[]{:S(2)}) async-start(f32[8,17,32,256]{3,2,1,0:T(8,128)} %get-tuple-element.60), calls=%async_computation | async-start | bytes 8912896 | tf_op jit(solution)/shard_map/all_to_all | solution.py:285
  18.1 3.9 %collective-permute-start.1 = (f32[4,32,256]{2,1,0:T(8,128)S(1)}, f32[4,32,256]{2,1,0:T(8,128)S(1)}, u32[]{:S(2)}, u32[]{:S(2)}) collective-permute-start(f32[4,32,256]{2,1,0:T(8,128)S(1)} %get-tuple-element.43), channel_id=1, source_target_pairs={{0,56},{8,0},{16,8},{24,16},{32,24},{40,32},{48,40},{56,48},{1,57}... | collective-permute-start | bytes 393224 | tf_op jit(solution)/shard_map/ppermute | solution.py:253
  22.0 3.6 %shard_map.65 = f32[64,32,256]{2,1,0:T(8,128)S(1)} custom-call(f32[64,128]{1,0:T(8,128)S(1)} %copy-done.2, f32[128,128]{1,0:T(8,128)S(1)} %copy-done.1, f32[64,256,128]{2,1,0:T(8,128)} %bitcast.49), custom_call_target="tpu_custom_call" | custom-call | flops 402653184 | bytes 6291456 | tf_op jit(solution)/shard_map/pallas_call | solution.py:67
  25.8 2.7 %collective-permute-start.9 = (f32[4,32,256]{2,1,0:T(8,128)S(1)}, f32[4,32,256]{2,1,0:T(8,128)S(1)}, u32[]{:S(2)}, u32[]{:S(2)}) collective-permute-start(f32[4,32,256]{2,1,0:T(8,128)S(1)} %get-tuple-element.53), channel_id=1, source_target_pairs={{0,56},{8,0},{16,8},{24,16},{32,24},{40,32},{48,40},{56,48},{1,57}... | collective-permute-start | bytes 393224 | tf_op jit(solution)/shard_map/ppermute | solution.py:253
  28.7 2.7 %collective-permute-start.3 = (f32[8,32,256]{2,1,0:T(8,128)S(1)}, f32[8,32,256]{2,1,0:T(8,128)S(1)}, u32[]{:S(2)}, u32[]{:S(2)}) collective-permute-start(f32[8,32,256]{2,1,0:T(8,128)S(1)} %get-tuple-element.45), channel_id=1, source_target_pairs={{0,56},{8,0},{16,8},{24,16},{32,24},{40,32},{48,40},{56,48},{1,57}... | collective-permute-start | bytes 786440 | tf_op jit(solution)/shard_map/ppermute | solution.py:253
  31.9 2.7 %collective-permute-start.11 = (f32[8,32,256]{2,1,0:T(8,128)S(1)}, f32[8,32,256]{2,1,0:T(8,128)S(1)}, u32[]{:S(2)}, u32[]{:S(2)}) collective-permute-start(f32[8,32,256]{2,1,0:T(8,128)S(1)} %get-tuple-element.55), channel_id=1, source_target_pairs={{0,56},{8,0},{16,8},{24,16},{32,24},{40,32},{48,40},{56,48},{1,57}... | collective-permute-start | bytes 786440 | tf_op jit(solution)/shard_map/ppermute | solution.py:253
  34.6 2.1 %collective-permute-done.2 = f32[8,32,256]{2,1,0:T(8,128)S(1)} collective-permute-done((f32[8,32,256]{2,1,0:T(8,128)S(1)}, f32[8,32,256]{2,1,0:T(8,128)S(1)}, u32[]{:S(2)}, u32[]{:S(2)}) %collective-permute-start.2) | collective-permute-done | bytes 262176 | tf_op jit(solution)/shard_map/ppermute | solution.py:253
  36.8 2.7 %collective-permute-start.5 = (f32[8,32,256]{2,1,0:T(8,128)S(1)}, f32[8,32,256]{2,1,0:T(8,128)S(1)}, u32[]{:S(2)}, u32[]{:S(2)}) collective-permute-start(f32[8,32,256]{2,1,0:T(8,128)S(1)} %get-tuple-element.47), channel_id=1, source_target_pairs={{0,56},{8,0},{16,8},{24,16},{32,24},{40,32},{48,40},{56,48},{1,57}... | collective-permute-start | bytes 786440 | tf_op jit(solution)/shard_map/ppermute | solution.py:253
  39.5 2.9 %collective-permute-done.10 = f32[8,32,256]{2,1,0:T(8,128)S(1)} collective-permute-done((f32[8,32,256]{2,1,0:T(8,128)S(1)}, f32[8,32,256]{2,1,0:T(8,128)S(1)}, u32[]{:S(2)}, u32[]{:S(2)}) %collective-permute-start.10) | collective-permute-done | bytes 262176 | tf_op jit(solution)/shard_map/ppermute | solution.py:253
  42.6 2.7 %collective-permute-start.13 = (f32[8,32,256]{2,1,0:T(8,128)S(1)}, f32[8,32,256]{2,1,0:T(8,128)S(1)}, u32[]{:S(2)}, u32[]{:S(2)}) collective-permute-start(f32[8,32,256]{2,1,0:T(8,128)S(1)} %get-tuple-element.57), channel_id=1, source_target_pairs={{0,56},{8,0},{16,8},{24,16},{32,24},{40,32},{48,40},{56,48},{1,57}... | collective-permute-start | bytes 786440 | tf_op jit(solution)/shard_map/ppermute | solution.py:253
  45.2 2.8 %collective-permute-done.4 = f32[8,32,256]{2,1,0:T(8,128)S(1)} collective-permute-done((f32[8,32,256]{2,1,0:T(8,128)S(1)}, f32[8,32,256]{2,1,0:T(8,128)S(1)}, u32[]{:S(2)}, u32[]{:S(2)}) %collective-permute-start.4) | collective-permute-done | bytes 262176 | tf_op jit(solution)/shard_map/ppermute | solution.py:253
  48.2 2.7 %collective-permute-start.7 = (f32[8,32,256]{2,1,0:T(8,128)S(1)}, f32[8,32,256]{2,1,0:T(8,128)S(1)}, u32[]{:S(2)}, u32[]{:S(2)}) collective-permute-start(f32[8,32,256]{2,1,0:T(8,128)S(1)} %get-tuple-element.49), channel_id=1, source_target_pairs={{0,56},{8,0},{16,8},{24,16},{32,24},{40,32},{48,40},{56,48},{1,57}... | collective-permute-start | bytes 786440 | tf_op jit(solution)/shard_map/ppermute | solution.py:253
  50.8 2.8 %collective-permute-done.12 = f32[8,32,256]{2,1,0:T(8,128)S(1)} collective-permute-done((f32[8,32,256]{2,1,0:T(8,128)S(1)}, f32[8,32,256]{2,1,0:T(8,128)S(1)}, u32[]{:S(2)}, u32[]{:S(2)}) %collective-permute-start.12) | collective-permute-done | bytes 262176 | tf_op jit(solution)/shard_map/ppermute | solution.py:253
  53.8 2.7 %collective-permute-start.15 = (f32[8,32,256]{2,1,0:T(8,128)S(1)}, f32[8,32,256]{2,1,0:T(8,128)S(1)}, u32[]{:S(2)}, u32[]{:S(2)}) collective-permute-start(f32[8,32,256]{2,1,0:T(8,128)S(1)} %get-tuple-element.59), channel_id=1, source_target_pairs={{0,56},{8,0},{16,8},{24,16},{32,24},{40,32},{48,40},{56,48},{1,57}... | collective-permute-start | bytes 786440 | tf_op jit(solution)/shard_map/ppermute | solution.py:253
  56.5 2.8 %collective-permute-done.6 = f32[8,32,256]{2,1,0:T(8,128)S(1)} collective-permute-done((f32[8,32,256]{2,1,0:T(8,128)S(1)}, f32[8,32,256]{2,1,0:T(8,128)S(1)}, u32[]{:S(2)}, u32[]{:S(2)}) %collective-permute-start.6) | collective-permute-done | bytes 262176 | tf_op jit(solution)/shard_map/ppermute | solution.py:253
  59.3 5.6 %collective-permute-done.14 = f32[8,32,256]{2,1,0:T(8,128)S(1)} collective-permute-done((f32[8,32,256]{2,1,0:T(8,128)S(1)}, f32[8,32,256]{2,1,0:T(8,128)S(1)}, u32[]{:S(2)}, u32[]{:S(2)}) %collective-permute-start.14) | collective-permute-done | bytes 262176 | tf_op jit(solution)/shard_map/ppermute | solution.py:253
  65.8 3.0 %all-to-all-done.third_ref.one_ref.two_ref = f32[8,17,32,256]{3,2,1,0:T(8,128)} async-done(((f32[8,17,32,256]{3,2,1,0:T(8,128)}), f32[8,17,32,256]{3,2,1,0:T(8,128)}, u32[]{:S(2)}, u32[]{:S(2)}) %all-to-all-start) | async-done | bytes 4456480 | tf_op jit(solution)/shard_map/all_to_all | solution.py:285
  68.8 3.9 %shard_map.66 = f32[8,128,256]{2,1,0:T(8,128)S(1)} custom-call(f32[8,17,32,256]{3,2,1,0:T(8,128)} %all-to-all-done.third_ref.one_ref.two_ref, f32[8,17,32,256]{3,2,1,0:T(8,128)} %all-to-all-done.third_ref.one_ref.two_ref, f32[8,17,32,256]{3,2,1,0:T(8,128)} %all-to-all-done.third_ref.one_ref.two_ref), custom_call_target="tpu_custom_call" | custom-call | flops 805306368 | bytes 4194304 | tf_op jit(solution)/shard_map/pallas_call | solution.py:229
  72.8 3.9 %collective-permute-start.17 = (f32[64,256]{1,0:T(8,128)S(1)}, f32[64,256]{1,0:T(8,128)S(1)}, u32[]{:S(2)}, u32[]{:S(2)}) collective-permute-start(f32[64,256]{1,0:T(8,128)S(1)} %get-tuple-element.63), channel_id=1, source_target_pairs={{0,56},{8,0},{16,8},{24,16},{32,24},{40,32},{48,40},{56,48},{1,57}... | collective-permute-start | bytes 196616 | tf_op jit(solution)/shard_map/ppermute | solution.py:253
  76.7 1.6 %collective-permute-done.16 = f32[64,256]{1,0:T(8,128)S(1)} collective-permute-done((f32[64,256]{1,0:T(8,128)S(1)}, f32[64,256]{1,0:T(8,128)S(1)}, u32[]{:S(2)}, u32[]{:S(2)}) %collective-permute-start.16) | collective-permute-done | bytes 65568 | tf_op jit(solution)/shard_map/ppermute | solution.py:253
  78.4 2.8 %collective-permute-start.19 = (f32[128,256]{1,0:T(8,128)S(1)}, f32[128,256]{1,0:T(8,128)S(1)}, u32[]{:S(2)}, u32[]{:S(2)}) collective-permute-start(f32[128,256]{1,0:T(8,128)S(1)} %pad_maximum_fusion.9), channel_id=1, source_target_pairs={{0,56},{8,0},{16,8},{24,16},{32,24},{40,32},{48,40},{56,48},{1,57}... | collective-permute-start | bytes 393224 | tf_op jit(solution)/shard_map/ppermute | solution.py:253
  81.3 5.7 %all-to-all-start.1 = ((f32[8,64,256]{2,1,0:T(8,128)}), f32[8,64,256]{2,1,0:T(8,128)S(1)}, u32[]{:S(2)}, u32[]{:S(2)}) async-start(f32[8,64,256]{2,1,0:T(8,128)} %pad_maximum_fusion), calls=%async_computation.1 | async-start | bytes 1048576 | tf_op jit(solution)/shard_map/all_to_all | solution.py:285
  87.1 2.7 %collective-permute-start.21 = (f32[128,256]{1,0:T(8,128)S(1)}, f32[128,256]{1,0:T(8,128)S(1)}, u32[]{:S(2)}, u32[]{:S(2)}) collective-permute-start(f32[128,256]{1,0:T(8,128)S(1)} %get-tuple-element.67), channel_id=1, source_target_pairs={{0,56},{8,0},{16,8},{24,16},{32,24},{40,32},{48,40},{56,48},{1,57}... | collective-permute-start | bytes 393224 | tf_op jit(solution)/shard_map/ppermute | solution.py:253
  89.8 3.5 %collective-permute-done.20 = f32[128,256]{1,0:T(8,128)S(1)} collective-permute-done((f32[128,256]{1,0:T(8,128)S(1)}, f32[128,256]{1,0:T(8,128)S(1)}, u32[]{:S(2)}, u32[]{:S(2)}) %collective-permute-start.20) | collective-permute-done | bytes 131104 | tf_op jit(solution)/shard_map/ppermute | solution.py:253
  93.3 3.2 %all-to-all-done.1 = f32[8,64,256]{2,1,0:T(8,128)S(1)} async-done(((f32[8,64,256]{2,1,0:T(8,128)}), f32[8,64,256]{2,1,0:T(8,128)S(1)}, u32[]{:S(2)}, u32[]{:S(2)}) %all-to-all-start.1) | async-done | bytes 524320 | tf_op jit(solution)/shard_map/all_to_all | solution.py:285
  96.6 2.7 %collective-permute-start.23 = (f32[128,256]{1,0:T(8,128)S(1)}, f32[128,256]{1,0:T(8,128)S(1)}, u32[]{:S(2)}, u32[]{:S(2)}) collective-permute-start(f32[128,256]{1,0:T(8,128)S(1)} %get-tuple-element.72), channel_id=1, source_target_pairs={{0,56},{8,0},{16,8},{24,16},{32,24},{40,32},{48,40},{56,48},{1,57}... | collective-permute-start | bytes 393224 | tf_op jit(solution)/shard_map/ppermute | solution.py:253
  103.7 2.4 %collective-permute-start.25 = (f32[256,128]{1,0:T(8,128)S(1)}, f32[256,128]{1,0:T(8,128)S(1)}, u32[]{:S(2)}, u32[]{:S(2)}) collective-permute-start(f32[256,128]{1,0:T(8,128)S(1)} %fusion.2), channel_id=1, source_target_pairs={{0,128},{64,192},{128,0},{192,64},{1,129},{65,193},{129,1},{193,65... | collective-permute-start | bytes 393224 | tf_op jit(solution)/shard_map/ppermute | solution.py:253
  107.5 2.9 %collective-permute-done.25 = f32[256,128]{1,0:T(8,128)S(1)} collective-permute-done((f32[256,128]{1,0:T(8,128)S(1)}, f32[256,128]{1,0:T(8,128)S(1)}, u32[]{:S(2)}, u32[]{:S(2)}) %collective-permute-start.25) | collective-permute-done | bytes 131104 | tf_op jit(solution)/shard_map/ppermute | solution.py:253
  111.6 10.0 %all_to_all.25 = f32[8,32,128]{2,1,0:T(8,128)S(1)} all-to-all(f32[8,32,128]{2,1,0:T(8,128)S(1)} %bitcast.50), channel_id=1, replica_groups=mesh['gx'=4,'gy'=8,'vert'=8] {'vert'}, dimensions={0} | all-to-all | bytes 262144 | tf_op jit(solution)/shard_map/all_to_all | solution.py:285
  121.7 13.6 %all_to_all.26 = f32[8,32,128]{2,1,0:T(8,128)S(1)} all-to-all(f32[8,32,128]{2,1,0:T(8,128)S(1)} %broadcast_in_dim.4), channel_id=1, replica_groups=mesh['gx'=4,'gy'=8,'vert'=8] {'gy'}, dimensions={0} | all-to-all | bytes 262144 | tf_op jit(solution)/shard_map/all_to_all | solution.py:285
  135.3 10.0 %all_to_all.27 = f32[8,32,128]{2,1,0:T(8,128)S(1)} all-to-all(f32[8,32,128]{2,1,0:T(8,128)S(1)} %broadcast_in_dim.5), channel_id=1, replica_groups=mesh['gx'=4,'gy'=8,'vert'=8] {'vert'}, dimensions={0} | all-to-all | bytes 262144 | tf_op jit(solution)/shard_map/all_to_all | solution.py:285
  (69 shorter events, 11.7 us)
Async XLA Ops:
  0.0 102.0 %copy-start = (f32[1024,128]{1,0:T(8,128)S(1)}, f32[1024,128]{1,0:T(8,128)}, u32[]{:S(2)}) copy-start(f32[1024,128]{1,0:T(8,128)} %param.7) | copy-start | bytes 1572868
  9.2 12.9 %copy-start.1 = (f32[128,128]{1,0:T(8,128)S(1)}, f32[128,128]{1,0:T(8,128)}, u32[]{:S(2)}) copy-start(f32[128,128]{1,0:T(8,128)} %second_ref.2) | copy-start | bytes 196612
  9.2 12.9 %copy-start.2 = (f32[64,128]{1,0:T(8,128)S(1)}, f32[64,128]{1,0:T(8,128)}, u32[]{:S(2)}) copy-start(f32[64,128]{1,0:T(8,128)} %constant.22.clone.pick_ref) | copy-start | bytes 98308
  9.2 59.6 %all-to-all-start = ((f32[8,17,32,256]{3,2,1,0:T(8,128)}), f32[8,17,32,256]{3,2,1,0:T(8,128)}, u32[]{:S(2)}, u32[]{:S(2)}) async-start(f32[8,17,32,256]{3,2,1,0:T(8,128)} %get-tuple-element.60), calls=%async_computation | async-start | bytes 8912896 | tf_op jit(solution)/shard_map/all_to_all | solution.py:285
  18.0 10.4 %collective-permute-start = (f32[4,32,256]{2,1,0:T(8,128)S(1)}, f32[4,32,256]{2,1,0:T(8,128)S(1)}, u32[]{:S(2)}, u32[]{:S(2)}) collective-permute-start(f32[4,32,256]{2,1,0:T(8,128)S(1)} %get-tuple-element.42), channel_id=1, source_target_pairs={{0,8},{8,16},{16,24},{24,32},{32,40},{40,48},{48,56},{56,0},{1,9},... | collective-permute-start | bytes 393224 | tf_op jit(solution)/shard_map/ppermute | solution.py:253
  18.1 10.3 %collective-permute-start.1 = (f32[4,32,256]{2,1,0:T(8,128)S(1)}, f32[4,32,256]{2,1,0:T(8,128)S(1)}, u32[]{:S(2)}, u32[]{:S(2)}) collective-permute-start(f32[4,32,256]{2,1,0:T(8,128)S(1)} %get-tuple-element.43), channel_id=1, source_target_pairs={{0,56},{8,0},{16,8},{24,16},{32,24},{40,32},{48,40},{56,48},{1,57}... | collective-permute-start | bytes 393224 | tf_op jit(solution)/shard_map/ppermute | solution.py:253
  25.7 6.0 %collective-permute-start.8 = (f32[4,32,256]{2,1,0:T(8,128)S(1)}, f32[4,32,256]{2,1,0:T(8,128)S(1)}, u32[]{:S(2)}, u32[]{:S(2)}) collective-permute-start(f32[4,32,256]{2,1,0:T(8,128)S(1)} %get-tuple-element.52), channel_id=1, source_target_pairs={{0,8},{8,16},{16,24},{24,32},{32,40},{40,48},{48,56},{56,0},{1,9},... | collective-permute-start | bytes 393224 | tf_op jit(solution)/shard_map/ppermute | solution.py:253
  25.8 5.9 %collective-permute-start.9 = (f32[4,32,256]{2,1,0:T(8,128)S(1)}, f32[4,32,256]{2,1,0:T(8,128)S(1)}, u32[]{:S(2)}, u32[]{:S(2)}) collective-permute-start(f32[4,32,256]{2,1,0:T(8,128)S(1)} %get-tuple-element.53), channel_id=1, source_target_pairs={{0,56},{8,0},{16,8},{24,16},{32,24},{40,32},{48,40},{56,48},{1,57}... | collective-permute-start | bytes 393224 | tf_op jit(solution)/shard_map/ppermute | solution.py:253
  28.6 8.1 %collective-permute-start.2 = (f32[8,32,256]{2,1,0:T(8,128)S(1)}, f32[8,32,256]{2,1,0:T(8,128)S(1)}, u32[]{:S(2)}, u32[]{:S(2)}) collective-permute-start(f32[8,32,256]{2,1,0:T(8,128)S(1)} %get-tuple-element.44), channel_id=1, source_target_pairs={{0,8},{8,16},{16,24},{24,32},{32,40},{40,48},{48,56},{56,0},{1,9},... | collective-permute-start | bytes 786440 | tf_op jit(solution)/shard_map/ppermute | solution.py:253
  28.7 8.0 %collective-permute-start.3 = (f32[8,32,256]{2,1,0:T(8,128)S(1)}, f32[8,32,256]{2,1,0:T(8,128)S(1)}, u32[]{:S(2)}, u32[]{:S(2)}) collective-permute-start(f32[8,32,256]{2,1,0:T(8,128)S(1)} %get-tuple-element.45), channel_id=1, source_target_pairs={{0,56},{8,0},{16,8},{24,16},{32,24},{40,32},{48,40},{56,48},{1,57}... | collective-permute-start | bytes 786440 | tf_op jit(solution)/shard_map/ppermute | solution.py:253
  31.8 10.6 %collective-permute-start.10 = (f32[8,32,256]{2,1,0:T(8,128)S(1)}, f32[8,32,256]{2,1,0:T(8,128)S(1)}, u32[]{:S(2)}, u32[]{:S(2)}) collective-permute-start(f32[8,32,256]{2,1,0:T(8,128)S(1)} %get-tuple-element.54), channel_id=1, source_target_pairs={{0,8},{8,16},{16,24},{24,32},{32,40},{40,48},{48,56},{56,0},{1,9},... | collective-permute-start | bytes 786440 | tf_op jit(solution)/shard_map/ppermute | solution.py:253
  31.9 10.5 %collective-permute-start.11 = (f32[8,32,256]{2,1,0:T(8,128)S(1)}, f32[8,32,256]{2,1,0:T(8,128)S(1)}, u32[]{:S(2)}, u32[]{:S(2)}) collective-permute-start(f32[8,32,256]{2,1,0:T(8,128)S(1)} %get-tuple-element.55), channel_id=1, source_target_pairs={{0,56},{8,0},{16,8},{24,16},{32,24},{40,32},{48,40},{56,48},{1,57}... | collective-permute-start | bytes 786440 | tf_op jit(solution)/shard_map/ppermute | solution.py:253
  36.7 11.3 %collective-permute-start.4 = (f32[8,32,256]{2,1,0:T(8,128)S(1)}, f32[8,32,256]{2,1,0:T(8,128)S(1)}, u32[]{:S(2)}, u32[]{:S(2)}) collective-permute-start(f32[8,32,256]{2,1,0:T(8,128)S(1)} %get-tuple-element.46), channel_id=1, source_target_pairs={{0,8},{8,16},{16,24},{24,32},{32,40},{40,48},{48,56},{56,0},{1,9},... | collective-permute-start | bytes 786440 | tf_op jit(solution)/shard_map/ppermute | solution.py:253
  36.8 11.2 %collective-permute-start.5 = (f32[8,32,256]{2,1,0:T(8,128)S(1)}, f32[8,32,256]{2,1,0:T(8,128)S(1)}, u32[]{:S(2)}, u32[]{:S(2)}) collective-permute-start(f32[8,32,256]{2,1,0:T(8,128)S(1)} %get-tuple-element.47), channel_id=1, source_target_pairs={{0,56},{8,0},{16,8},{24,16},{32,24},{40,32},{48,40},{56,48},{1,57}... | collective-permute-start | bytes 786440 | tf_op jit(solution)/shard_map/ppermute | solution.py:253
  42.5 11.2 %collective-permute-start.12 = (f32[8,32,256]{2,1,0:T(8,128)S(1)}, f32[8,32,256]{2,1,0:T(8,128)S(1)}, u32[]{:S(2)}, u32[]{:S(2)}) collective-permute-start(f32[8,32,256]{2,1,0:T(8,128)S(1)} %get-tuple-element.56), channel_id=1, source_target_pairs={{0,8},{8,16},{16,24},{24,32},{32,40},{40,48},{48,56},{56,0},{1,9},... | collective-permute-start | bytes 786440 | tf_op jit(solution)/shard_map/ppermute | solution.py:253
  42.6 11.1 %collective-permute-start.13 = (f32[8,32,256]{2,1,0:T(8,128)S(1)}, f32[8,32,256]{2,1,0:T(8,128)S(1)}, u32[]{:S(2)}, u32[]{:S(2)}) collective-permute-start(f32[8,32,256]{2,1,0:T(8,128)S(1)} %get-tuple-element.57), channel_id=1, source_target_pairs={{0,56},{8,0},{16,8},{24,16},{32,24},{40,32},{48,40},{56,48},{1,57}... | collective-permute-start | bytes 786440 | tf_op jit(solution)/shard_map/ppermute | solution.py:253
  48.1 11.2 %collective-permute-start.6 = (f32[8,32,256]{2,1,0:T(8,128)S(1)}, f32[8,32,256]{2,1,0:T(8,128)S(1)}, u32[]{:S(2)}, u32[]{:S(2)}) collective-permute-start(f32[8,32,256]{2,1,0:T(8,128)S(1)} %get-tuple-element.48), channel_id=1, source_target_pairs={{0,8},{8,16},{16,24},{24,32},{32,40},{40,48},{48,56},{56,0},{1,9},... | collective-permute-start | bytes 786440 | tf_op jit(solution)/shard_map/ppermute | solution.py:253
  48.2 11.1 %collective-permute-start.7 = (f32[8,32,256]{2,1,0:T(8,128)S(1)}, f32[8,32,256]{2,1,0:T(8,128)S(1)}, u32[]{:S(2)}, u32[]{:S(2)}) collective-permute-start(f32[8,32,256]{2,1,0:T(8,128)S(1)} %get-tuple-element.49), channel_id=1, source_target_pairs={{0,56},{8,0},{16,8},{24,16},{32,24},{40,32},{48,40},{56,48},{1,57}... | collective-permute-start | bytes 786440 | tf_op jit(solution)/shard_map/ppermute | solution.py:253
  53.7 11.2 %collective-permute-start.14 = (f32[8,32,256]{2,1,0:T(8,128)S(1)}, f32[8,32,256]{2,1,0:T(8,128)S(1)}, u32[]{:S(2)}, u32[]{:S(2)}) collective-permute-start(f32[8,32,256]{2,1,0:T(8,128)S(1)} %get-tuple-element.58), channel_id=1, source_target_pairs={{0,8},{8,16},{16,24},{24,32},{32,40},{40,48},{48,56},{56,0},{1,9},... | collective-permute-start | bytes 786440 | tf_op jit(solution)/shard_map/ppermute | solution.py:253
  53.8 11.1 %collective-permute-start.15 = (f32[8,32,256]{2,1,0:T(8,128)S(1)}, f32[8,32,256]{2,1,0:T(8,128)S(1)}, u32[]{:S(2)}, u32[]{:S(2)}) collective-permute-start(f32[8,32,256]{2,1,0:T(8,128)S(1)} %get-tuple-element.59), channel_id=1, source_target_pairs={{0,56},{8,0},{16,8},{24,16},{32,24},{40,32},{48,40},{56,48},{1,57}... | collective-permute-start | bytes 786440 | tf_op jit(solution)/shard_map/ppermute | solution.py:253
  72.7 5.6 %collective-permute-start.16 = (f32[64,256]{1,0:T(8,128)S(1)}, f32[64,256]{1,0:T(8,128)S(1)}, u32[]{:S(2)}, u32[]{:S(2)}) collective-permute-start(f32[64,256]{1,0:T(8,128)S(1)} %get-tuple-element.62), channel_id=1, source_target_pairs={{0,8},{8,16},{16,24},{24,32},{32,40},{40,48},{48,56},{56,0},{1,9},... | collective-permute-start | bytes 196616 | tf_op jit(solution)/shard_map/ppermute | solution.py:253
  72.8 5.5 %collective-permute-start.17 = (f32[64,256]{1,0:T(8,128)S(1)}, f32[64,256]{1,0:T(8,128)S(1)}, u32[]{:S(2)}, u32[]{:S(2)}) collective-permute-start(f32[64,256]{1,0:T(8,128)S(1)} %get-tuple-element.63), channel_id=1, source_target_pairs={{0,56},{8,0},{16,8},{24,16},{32,24},{40,32},{48,40},{56,48},{1,57}... | collective-permute-start | bytes 196616 | tf_op jit(solution)/shard_map/ppermute | solution.py:253
  78.3 8.6 %collective-permute-start.18 = (f32[128,256]{1,0:T(8,128)S(1)}, f32[128,256]{1,0:T(8,128)S(1)}, u32[]{:S(2)}, u32[]{:S(2)}) collective-permute-start(f32[128,256]{1,0:T(8,128)S(1)} %pad_maximum_fusion.8), channel_id=1, source_target_pairs={{0,8},{8,16},{16,24},{24,32},{32,40},{40,48},{48,56},{56,0},{1,9},... | collective-permute-start | bytes 393224 | tf_op jit(solution)/shard_map/ppermute | solution.py:253
  78.4 8.5 %collective-permute-start.19 = (f32[128,256]{1,0:T(8,128)S(1)}, f32[128,256]{1,0:T(8,128)S(1)}, u32[]{:S(2)}, u32[]{:S(2)}) collective-permute-start(f32[128,256]{1,0:T(8,128)S(1)} %pad_maximum_fusion.9), channel_id=1, source_target_pairs={{0,56},{8,0},{16,8},{24,16},{32,24},{40,32},{48,40},{56,48},{1,57}... | collective-permute-start | bytes 393224 | tf_op jit(solution)/shard_map/ppermute | solution.py:253
  81.3 15.2 %all-to-all-start.1 = ((f32[8,64,256]{2,1,0:T(8,128)}), f32[8,64,256]{2,1,0:T(8,128)S(1)}, u32[]{:S(2)}, u32[]{:S(2)}) async-start(f32[8,64,256]{2,1,0:T(8,128)} %pad_maximum_fusion), calls=%async_computation.1 | async-start | bytes 1048576 | tf_op jit(solution)/shard_map/all_to_all | solution.py:285
  87.0 6.3 %collective-permute-start.20 = (f32[128,256]{1,0:T(8,128)S(1)}, f32[128,256]{1,0:T(8,128)S(1)}, u32[]{:S(2)}, u32[]{:S(2)}) collective-permute-start(f32[128,256]{1,0:T(8,128)S(1)} %get-tuple-element.66), channel_id=1, source_target_pairs={{0,8},{8,16},{16,24},{24,32},{32,40},{40,48},{48,56},{56,0},{1,9},... | collective-permute-start | bytes 393224 | tf_op jit(solution)/shard_map/ppermute | solution.py:253
  87.1 6.2 %collective-permute-start.21 = (f32[128,256]{1,0:T(8,128)S(1)}, f32[128,256]{1,0:T(8,128)S(1)}, u32[]{:S(2)}, u32[]{:S(2)}) collective-permute-start(f32[128,256]{1,0:T(8,128)S(1)} %get-tuple-element.67), channel_id=1, source_target_pairs={{0,56},{8,0},{16,8},{24,16},{32,24},{40,32},{48,40},{56,48},{1,57}... | collective-permute-start | bytes 393224 | tf_op jit(solution)/shard_map/ppermute | solution.py:253
  96.5 5.4 %collective-permute-start.22 = (f32[128,256]{1,0:T(8,128)S(1)}, f32[128,256]{1,0:T(8,128)S(1)}, u32[]{:S(2)}, u32[]{:S(2)}) collective-permute-start(f32[128,256]{1,0:T(8,128)S(1)} %get-tuple-element.71), channel_id=1, source_target_pairs={{0,8},{8,16},{16,24},{24,32},{32,40},{40,48},{48,56},{56,0},{1,9},... | collective-permute-start | bytes 393224 | tf_op jit(solution)/shard_map/ppermute | solution.py:253
  96.6 5.3 %collective-permute-start.23 = (f32[128,256]{1,0:T(8,128)S(1)}, f32[128,256]{1,0:T(8,128)S(1)}, u32[]{:S(2)}, u32[]{:S(2)}) collective-permute-start(f32[128,256]{1,0:T(8,128)S(1)} %get-tuple-element.72), channel_id=1, source_target_pairs={{0,56},{8,0},{16,8},{24,16},{32,24},{40,32},{48,40},{56,48},{1,57}... | collective-permute-start | bytes 393224 | tf_op jit(solution)/shard_map/ppermute | solution.py:253
  102.4 5.1 %collective-permute-start.24 = (f32[256,128]{1,0:T(8,128)S(1)}, f32[256,128]{1,0:T(8,128)S(1)}, u32[]{:S(2)}, u32[]{:S(2)}) collective-permute-start(f32[256,128]{1,0:T(8,128)S(1)} %fusion.2), channel_id=1, source_target_pairs={{0,64},{64,128},{128,192},{192,0},{1,65},{65,129},{129,193},{193,1... | collective-permute-start | bytes 393224 | tf_op jit(solution)/shard_map/ppermute | solution.py:253
  103.7 6.7 %collective-permute-start.25 = (f32[256,128]{1,0:T(8,128)S(1)}, f32[256,128]{1,0:T(8,128)S(1)}, u32[]{:S(2)}, u32[]{:S(2)}) collective-permute-start(f32[256,128]{1,0:T(8,128)S(1)} %fusion.2), channel_id=1, source_target_pairs={{0,128},{64,192},{128,0},{192,64},{1,129},{65,193},{129,1},{193,65... | collective-permute-start | bytes 393224 | tf_op jit(solution)/shard_map/ppermute | solution.py:253
  106.1 4.9 %collective-permute-start.26 = (f32[256,128]{1,0:T(8,128)S(1)}, f32[256,128]{1,0:T(8,128)S(1)}, u32[]{:S(2)}, u32[]{:S(2)}) collective-permute-start(f32[256,128]{1,0:T(8,128)S(1)} %fusion.2), channel_id=1, source_target_pairs={{0,192},{64,0},{128,64},{192,128},{1,193},{65,1},{129,65},{193,129... | collective-permute-start | bytes 393224 | tf_op jit(solution)/shard_map/ppermute | solution.py:253
  (1 other events, 10.4 us)

commit v9 on v8

--- a/solution.py
+++ b/solution.py
@@ -11,7 +11,7 @@
 HIGHEST = lax.Precision.HIGHEST
 NT = (((1,), (1,)), ((), ()))
 NN = (((1,), (0,)), ((), ()))
-VMEM_LIMIT = 10 * 2**20
+VMEM_LIMIT = 14 * 2**20
 STEP = 16
 SETS = 8
 
@@ -224,7 +224,7 @@
 
 def depth_product(gathered, part, rank, groups):
     n, count, planes, nx = gathered.shape
-    step = 2 if groups % 2 == 0 else 1
+    step = 4 if groups % 4 == 0 else 1
     block = (n, step, planes, nx)
     return pl.pallas_call(
         depth_kernel,

time: 147 us -> 146 us (level)
  no operation moved by 1% of the time
where the time goes in v9:
time: 146 us; the launch traced here: 145 us
  starting transfers between devices  54.1 us (37%)
  waiting for transfers between devices  35.7 us (24%)
  blocking collectives  33.7 us (23%)
  Pallas kernels  17 us (12%)
  local copies, waits for them, and re-layouts  1.72 us (1%)
  other arithmetic  1.61 us (1%)
    ppermute x27, starting transfers between devices, shifts(): lax.ppermute(value, axis, [(i, (i + by) % n) for i in range(n)])  40.5 us
    all_to_all x3, blocking collectives, trade(): return lax.all_to_all(value, axis, 0, 0)  33.7 us
    ppermute x27, waiting for transfers between devices, shifts(): lax.ppermute(value, axis, [(i, (i + by) % n) for i in range(n)])  29.5 us
    all_to_all x2, starting transfers between devices, trade(): return lax.all_to_all(value, axis, 0, 0)  13.5 us
    pallas_call x1, Pallas kernels, lead_product(): pl.pallas_call(functools.partial(lead_kernel, roll), grid=(steps,), in_sp...  9.14 us
    all_to_all x2, waiting for transfers between devices, trade(): return lax.all_to_all(value, axis, 0, 0)  6.18 us
    pallas_call x2, Pallas kernels, depth_product(): pl.pallas_call(depth_kernel, grid=(groups // step,), in_specs=[pl.BlockSp...  4.23 us
    pallas_call x1, Pallas kernels, mode_product(): pl.pallas_call(functools.partial(mode_kernel, roll, start // STEP), grid=...  3.61 us
  transfers between devices with their start and end apart: 29, of which 15 were waited for; matrix products, arithmetic and copies ran while one was open for 2% of the time, Pallas kernels for 3%

profile of v9, /device:TPU:1, one launch (start us, length us, event | category | flops | bytes accessed | tf_op | source)
XLA Modules:
  0.0 145.1 jit_solution(4040632739635584307)
XLA Ops:
  0.0 9.1 %shard_map.64 = (f32[8,17,32,256]{3,2,1,0:T(8,128)}, f32[64,32,256]{2,1,0:T(8,128)}) custom-call(f32[128,128]{1,0:T(8,128)} %constant.21.clone.pick_ref, f32[128,128]{1,0:T(8,128)} %second_ref.2, f32[64,128]{1,0:T(8,128)} %bitcast.52, f32[64,256,128]{2,1,0:T(8,128)} %bitcast.48), custom_call_target="tpu_custom_call" | custom-call | flops 1610612736 | bytes 16777216 | tf_op jit(solution)/shard_map/pallas_call | solution.py:175
  9.2 7.8 %all-to-all-start = ((f32[8,17,32,256]{3,2,1,0:T(8,128)}), f32[8,17,32,256]{3,2,1,0:T(8,128)}, u32[]{:S(2)}, u32[]{:S(2)}) async-start(f32[8,17,32,256]{3,2,1,0:T(8,128)} %get-tuple-element.60), calls=%async_computation | async-start | bytes 8912896 | tf_op jit(solution)/shard_map/all_to_all | solution.py:285
  18.1 3.9 %collective-permute-start.1 = (f32[4,32,256]{2,1,0:T(8,128)S(1)}, f32[4,32,256]{2,1,0:T(8,128)S(1)}, u32[]{:S(2)}, u32[]{:S(2)}) collective-permute-start(f32[4,32,256]{2,1,0:T(8,128)S(1)} %get-tuple-element.43), channel_id=1, source_target_pairs={{0,56},{8,0},{16,8},{24,16},{32,24},{40,32},{48,40},{56,48},{1,57}... | collective-permute-start | bytes 393224 | tf_op jit(solution)/shard_map/ppermute | solution.py:253
  22.0 3.6 %shard_map.65 = f32[64,32,256]{2,1,0:T(8,128)S(1)} custom-call(f32[64,128]{1,0:T(8,128)S(1)} %copy-done.2, f32[128,128]{1,0:T(8,128)S(1)} %copy-done.1, f32[64,256,128]{2,1,0:T(8,128)} %bitcast.49), custom_call_target="tpu_custom_call" | custom-call | flops 402653184 | bytes 6291456 | tf_op jit(solution)/shard_map/pallas_call | solution.py:67
  25.8 2.7 %collective-permute-start.9 = (f32[4,32,256]{2,1,0:T(8,128)S(1)}, f32[4,32,256]{2,1,0:T(8,128)S(1)}, u32[]{:S(2)}, u32[]{:S(2)}) collective-permute-start(f32[4,32,256]{2,1,0:T(8,128)S(1)} %get-tuple-element.53), channel_id=1, source_target_pairs={{0,56},{8,0},{16,8},{24,16},{32,24},{40,32},{48,40},{56,48},{1,57}... | collective-permute-start | bytes 393224 | tf_op jit(solution)/shard_map/ppermute | solution.py:253
  28.7 2.7 %collective-permute-start.3 = (f32[8,32,256]{2,1,0:T(8,128)S(1)}, f32[8,32,256]{2,1,0:T(8,128)S(1)}, u32[]{:S(2)}, u32[]{:S(2)}) collective-permute-start(f32[8,32,256]{2,1,0:T(8,128)S(1)} %get-tuple-element.45), channel_id=1, source_target_pairs={{0,56},{8,0},{16,8},{24,16},{32,24},{40,32},{48,40},{56,48},{1,57}... | collective-permute-start | bytes 786440 | tf_op jit(solution)/shard_map/ppermute | solution.py:253
  31.9 2.7 %collective-permute-start.11 = (f32[8,32,256]{2,1,0:T(8,128)S(1)}, f32[8,32,256]{2,1,0:T(8,128)S(1)}, u32[]{:S(2)}, u32[]{:S(2)}) collective-permute-start(f32[8,32,256]{2,1,0:T(8,128)S(1)} %get-tuple-element.55), channel_id=1, source_target_pairs={{0,56},{8,0},{16,8},{24,16},{32,24},{40,32},{48,40},{56,48},{1,57}... | collective-permute-start | bytes 786440 | tf_op jit(solution)/shard_map/ppermute | solution.py:253
  34.6 2.1 %collective-permute-done.2 = f32[8,32,256]{2,1,0:T(8,128)S(1)} collective-permute-done((f32[8,32,256]{2,1,0:T(8,128)S(1)}, f32[8,32,256]{2,1,0:T(8,128)S(1)}, u32[]{:S(2)}, u32[]{:S(2)}) %collective-permute-start.2) | collective-permute-done | bytes 262176 | tf_op jit(solution)/shard_map/ppermute | solution.py:253
  36.8 2.7 %collective-permute-start.5 = (f32[8,32,256]{2,1,0:T(8,128)S(1)}, f32[8,32,256]{2,1,0:T(8,128)S(1)}, u32[]{:S(2)}, u32[]{:S(2)}) collective-permute-start(f32[8,32,256]{2,1,0:T(8,128)S(1)} %get-tuple-element.47), channel_id=1, source_target_pairs={{0,56},{8,0},{16,8},{24,16},{32,24},{40,32},{48,40},{56,48},{1,57}... | collective-permute-start | bytes 786440 | tf_op jit(solution)/shard_map/ppermute | solution.py:253
  39.5 2.9 %collective-permute-done.10 = f32[8,32,256]{2,1,0:T(8,128)S(1)} collective-permute-done((f32[8,32,256]{2,1,0:T(8,128)S(1)}, f32[8,32,256]{2,1,0:T(8,128)S(1)}, u32[]{:S(2)}, u32[]{:S(2)}) %collective-permute-start.10) | collective-permute-done | bytes 262176 | tf_op jit(solution)/shard_map/ppermute | solution.py:253
  42.6 2.7 %collective-permute-start.13 = (f32[8,32,256]{2,1,0:T(8,128)S(1)}, f32[8,32,256]{2,1,0:T(8,128)S(1)}, u32[]{:S(2)}, u32[]{:S(2)}) collective-permute-start(f32[8,32,256]{2,1,0:T(8,128)S(1)} %get-tuple-element.57), channel_id=1, source_target_pairs={{0,56},{8,0},{16,8},{24,16},{32,24},{40,32},{48,40},{56,48},{1,57}... | collective-permute-start | bytes 786440 | tf_op jit(solution)/shard_map/ppermute | solution.py:253
  45.2 2.8 %collective-permute-done.4 = f32[8,32,256]{2,1,0:T(8,128)S(1)} collective-permute-done((f32[8,32,256]{2,1,0:T(8,128)S(1)}, f32[8,32,256]{2,1,0:T(8,128)S(1)}, u32[]{:S(2)}, u32[]{:S(2)}) %collective-permute-start.4) | collective-permute-done | bytes 262176 | tf_op jit(solution)/shard_map/ppermute | solution.py:253
  48.2 2.7 %collective-permute-start.7 = (f32[8,32,256]{2,1,0:T(8,128)S(1)}, f32[8,32,256]{2,1,0:T(8,128)S(1)}, u32[]{:S(2)}, u32[]{:S(2)}) collective-permute-start(f32[8,32,256]{2,1,0:T(8,128)S(1)} %get-tuple-element.49), channel_id=1, source_target_pairs={{0,56},{8,0},{16,8},{24,16},{32,24},{40,32},{48,40},{56,48},{1,57}... | collective-permute-start | bytes 786440 | tf_op jit(solution)/shard_map/ppermute | solution.py:253
  50.8 2.8 %collective-permute-done.12 = f32[8,32,256]{2,1,0:T(8,128)S(1)} collective-permute-done((f32[8,32,256]{2,1,0:T(8,128)S(1)}, f32[8,32,256]{2,1,0:T(8,128)S(1)}, u32[]{:S(2)}, u32[]{:S(2)}) %collective-permute-start.12) | collective-permute-done | bytes 262176 | tf_op jit(solution)/shard_map/ppermute | solution.py:253
  53.8 2.7 %collective-permute-start.15 = (f32[8,32,256]{2,1,0:T(8,128)S(1)}, f32[8,32,256]{2,1,0:T(8,128)S(1)}, u32[]{:S(2)}, u32[]{:S(2)}) collective-permute-start(f32[8,32,256]{2,1,0:T(8,128)S(1)} %get-tuple-element.59), channel_id=1, source_target_pairs={{0,56},{8,0},{16,8},{24,16},{32,24},{40,32},{48,40},{56,48},{1,57}... | collective-permute-start | bytes 786440 | tf_op jit(solution)/shard_map/ppermute | solution.py:253
  56.5 2.8 %collective-permute-done.6 = f32[8,32,256]{2,1,0:T(8,128)S(1)} collective-permute-done((f32[8,32,256]{2,1,0:T(8,128)S(1)}, f32[8,32,256]{2,1,0:T(8,128)S(1)}, u32[]{:S(2)}, u32[]{:S(2)}) %collective-permute-start.6) | collective-permute-done | bytes 262176 | tf_op jit(solution)/shard_map/ppermute | solution.py:253
  59.3 5.6 %collective-permute-done.14 = f32[8,32,256]{2,1,0:T(8,128)S(1)} collective-permute-done((f32[8,32,256]{2,1,0:T(8,128)S(1)}, f32[8,32,256]{2,1,0:T(8,128)S(1)}, u32[]{:S(2)}, u32[]{:S(2)}) %collective-permute-start.14) | collective-permute-done | bytes 262176 | tf_op jit(solution)/shard_map/ppermute | solution.py:253
  65.8 3.0 %all-to-all-done.third_ref.one_ref.two_ref = f32[8,17,32,256]{3,2,1,0:T(8,128)} async-done(((f32[8,17,32,256]{3,2,1,0:T(8,128)}), f32[8,17,32,256]{3,2,1,0:T(8,128)}, u32[]{:S(2)}, u32[]{:S(2)}) %all-to-all-start) | async-done | bytes 4456480 | tf_op jit(solution)/shard_map/all_to_all | solution.py:285
  68.8 2.9 %shard_map.66 = f32[8,128,256]{2,1,0:T(8,128)S(1)} custom-call(f32[8,17,32,256]{3,2,1,0:T(8,128)} %all-to-all-done.third_ref.one_ref.two_ref, f32[8,17,32,256]{3,2,1,0:T(8,128)} %all-to-all-done.third_ref.one_ref.two_ref, f32[8,17,32,256]{3,2,1,0:T(8,128)} %all-to-all-done.third_ref.one_ref.two_ref), custom_call_target="tpu_custom_call" | custom-call | flops 805306368 | bytes 4194304 | tf_op jit(solution)/shard_map/pallas_call | solution.py:229
  71.8 3.9 %collective-permute-start.17 = (f32[64,256]{1,0:T(8,128)S(1)}, f32[64,256]{1,0:T(8,128)S(1)}, u32[]{:S(2)}, u32[]{:S(2)}) collective-permute-start(f32[64,256]{1,0:T(8,128)S(1)} %get-tuple-element.63), channel_id=1, source_target_pairs={{0,56},{8,0},{16,8},{24,16},{32,24},{40,32},{48,40},{56,48},{1,57}... | collective-permute-start | bytes 196616 | tf_op jit(solution)/shard_map/ppermute | solution.py:253
  75.7 1.6 %collective-permute-done.16 = f32[64,256]{1,0:T(8,128)S(1)} collective-permute-done((f32[64,256]{1,0:T(8,128)S(1)}, f32[64,256]{1,0:T(8,128)S(1)}, u32[]{:S(2)}, u32[]{:S(2)}) %collective-permute-start.16) | collective-permute-done | bytes 65568 | tf_op jit(solution)/shard_map/ppermute | solution.py:253
  77.5 2.8 %collective-permute-start.19 = (f32[128,256]{1,0:T(8,128)S(1)}, f32[128,256]{1,0:T(8,128)S(1)}, u32[]{:S(2)}, u32[]{:S(2)}) collective-permute-start(f32[128,256]{1,0:T(8,128)S(1)} %pad_maximum_fusion.9), channel_id=1, source_target_pairs={{0,56},{8,0},{16,8},{24,16},{32,24},{40,32},{48,40},{56,48},{1,57}... | collective-permute-start | bytes 393224 | tf_op jit(solution)/shard_map/ppermute | solution.py:253
  80.3 5.7 %all-to-all-start.1 = ((f32[8,64,256]{2,1,0:T(8,128)}), f32[8,64,256]{2,1,0:T(8,128)S(1)}, u32[]{:S(2)}, u32[]{:S(2)}) async-start(f32[8,64,256]{2,1,0:T(8,128)} %pad_maximum_fusion), calls=%async_computation.1 | async-start | bytes 1048576 | tf_op jit(solution)/shard_map/all_to_all | solution.py:285
  86.1 2.7 %collective-permute-start.21 = (f32[128,256]{1,0:T(8,128)S(1)}, f32[128,256]{1,0:T(8,128)S(1)}, u32[]{:S(2)}, u32[]{:S(2)}) collective-permute-start(f32[128,256]{1,0:T(8,128)S(1)} %get-tuple-element.67), channel_id=1, source_target_pairs={{0,56},{8,0},{16,8},{24,16},{32,24},{40,32},{48,40},{56,48},{1,57}... | collective-permute-start | bytes 393224 | tf_op jit(solution)/shard_map/ppermute | solution.py:253
  88.8 3.5 %collective-permute-done.20 = f32[128,256]{1,0:T(8,128)S(1)} collective-permute-done((f32[128,256]{1,0:T(8,128)S(1)}, f32[128,256]{1,0:T(8,128)S(1)}, u32[]{:S(2)}, u32[]{:S(2)}) %collective-permute-start.20) | collective-permute-done | bytes 131104 | tf_op jit(solution)/shard_map/ppermute | solution.py:253
  92.3 3.2 %all-to-all-done.1 = f32[8,64,256]{2,1,0:T(8,128)S(1)} async-done(((f32[8,64,256]{2,1,0:T(8,128)}), f32[8,64,256]{2,1,0:T(8,128)S(1)}, u32[]{:S(2)}, u32[]{:S(2)}) %all-to-all-start.1) | async-done | bytes 524320 | tf_op jit(solution)/shard_map/all_to_all | solution.py:285
  95.6 2.7 %collective-permute-start.23 = (f32[128,256]{1,0:T(8,128)S(1)}, f32[128,256]{1,0:T(8,128)S(1)}, u32[]{:S(2)}, u32[]{:S(2)}) collective-permute-start(f32[128,256]{1,0:T(8,128)S(1)} %get-tuple-element.72), channel_id=1, source_target_pairs={{0,56},{8,0},{16,8},{24,16},{32,24},{40,32},{48,40},{56,48},{1,57}... | collective-permute-start | bytes 393224 | tf_op jit(solution)/shard_map/ppermute | solution.py:253
  102.7 2.5 %collective-permute-start.25 = (f32[256,128]{1,0:T(8,128)S(1)}, f32[256,128]{1,0:T(8,128)S(1)}, u32[]{:S(2)}, u32[]{:S(2)}) collective-permute-start(f32[256,128]{1,0:T(8,128)S(1)} %fusion.2), channel_id=1, source_target_pairs={{0,128},{64,192},{128,0},{192,64},{1,129},{65,193},{129,1},{193,65... | collective-permute-start | bytes 393224 | tf_op jit(solution)/shard_map/ppermute | solution.py:253
  106.5 2.9 %collective-permute-done.25 = f32[256,128]{1,0:T(8,128)S(1)} collective-permute-done((f32[256,128]{1,0:T(8,128)S(1)}, f32[256,128]{1,0:T(8,128)S(1)}, u32[]{:S(2)}, u32[]{:S(2)}) %collective-permute-start.25) | collective-permute-done | bytes 131104 | tf_op jit(solution)/shard_map/ppermute | solution.py:253
  110.7 10.0 %all_to_all.25 = f32[8,32,128]{2,1,0:T(8,128)S(1)} all-to-all(f32[8,32,128]{2,1,0:T(8,128)S(1)} %bitcast.50), channel_id=1, replica_groups=mesh['gx'=4,'gy'=8,'vert'=8] {'vert'}, dimensions={0} | all-to-all | bytes 262144 | tf_op jit(solution)/shard_map/all_to_all | solution.py:285
  120.7 13.6 %all_to_all.26 = f32[8,32,128]{2,1,0:T(8,128)S(1)} all-to-all(f32[8,32,128]{2,1,0:T(8,128)S(1)} %broadcast_in_dim.4), channel_id=1, replica_groups=mesh['gx'=4,'gy'=8,'vert'=8] {'gy'}, dimensions={0} | all-to-all | bytes 262144 | tf_op jit(solution)/shard_map/all_to_all | solution.py:285
  134.4 10.0 %all_to_all.27 = f32[8,32,128]{2,1,0:T(8,128)S(1)} all-to-all(f32[8,32,128]{2,1,0:T(8,128)S(1)} %broadcast_in_dim.5), channel_id=1, replica_groups=mesh['gx'=4,'gy'=8,'vert'=8] {'vert'}, dimensions={0} | all-to-all | bytes 262144 | tf_op jit(solution)/shard_map/all_to_all | solution.py:285
  (69 shorter events, 11.7 us)
Async XLA Ops:
  0.0 101.0 %copy-start = (f32[1024,128]{1,0:T(8,128)S(1)}, f32[1024,128]{1,0:T(8,128)}, u32[]{:S(2)}) copy-start(f32[1024,128]{1,0:T(8,128)} %param.7) | copy-start | bytes 1572868
  9.2 12.9 %copy-start.1 = (f32[128,128]{1,0:T(8,128)S(1)}, f32[128,128]{1,0:T(8,128)}, u32[]{:S(2)}) copy-start(f32[128,128]{1,0:T(8,128)} %second_ref.2) | copy-start | bytes 196612
  9.2 12.9 %copy-start.2 = (f32[64,128]{1,0:T(8,128)S(1)}, f32[64,128]{1,0:T(8,128)}, u32[]{:S(2)}) copy-start(f32[64,128]{1,0:T(8,128)} %constant.22.clone.pick_ref) | copy-start | bytes 98308
  9.2 59.6 %all-to-all-start = ((f32[8,17,32,256]{3,2,1,0:T(8,128)}), f32[8,17,32,256]{3,2,1,0:T(8,128)}, u32[]{:S(2)}, u32[]{:S(2)}) async-start(f32[8,17,32,256]{3,2,1,0:T(8,128)} %get-tuple-element.60), calls=%async_computation | async-start | bytes 8912896 | tf_op jit(solution)/shard_map/all_to_all | solution.py:285
  18.0 10.4 %collective-permute-start = (f32[4,32,256]{2,1,0:T(8,128)S(1)}, f32[4,32,256]{2,1,0:T(8,128)S(1)}, u32[]{:S(2)}, u32[]{:S(2)}) collective-permute-start(f32[4,32,256]{2,1,0:T(8,128)S(1)} %get-tuple-element.42), channel_id=1, source_target_pairs={{0,8},{8,16},{16,24},{24,32},{32,40},{40,48},{48,56},{56,0},{1,9},... | collective-permute-start | bytes 393224 | tf_op jit(solution)/shard_map/ppermute | solution.py:253
  18.1 10.3 %collective-permute-start.1 = (f32[4,32,256]{2,1,0:T(8,128)S(1)}, f32[4,32,256]{2,1,0:T(8,128)S(1)}, u32[]{:S(2)}, u32[]{:S(2)}) collective-permute-start(f32[4,32,256]{2,1,0:T(8,128)S(1)} %get-tuple-element.43), channel_id=1, source_target_pairs={{0,56},{8,0},{16,8},{24,16},{32,24},{40,32},{48,40},{56,48},{1,57}... | collective-permute-start | bytes 393224 | tf_op jit(solution)/shard_map/ppermute | solution.py:253
  25.7 6.0 %collective-permute-start.8 = (f32[4,32,256]{2,1,0:T(8,128)S(1)}, f32[4,32,256]{2,1,0:T(8,128)S(1)}, u32[]{:S(2)}, u32[]{:S(2)}) collective-permute-start(f32[4,32,256]{2,1,0:T(8,128)S(1)} %get-tuple-element.52), channel_id=1, source_target_pairs={{0,8},{8,16},{16,24},{24,32},{32,40},{40,48},{48,56},{56,0},{1,9},... | collective-permute-start | bytes 393224 | tf_op jit(solution)/shard_map/ppermute | solution.py:253
  25.8 5.9 %collective-permute-start.9 = (f32[4,32,256]{2,1,0:T(8,128)S(1)}, f32[4,32,256]{2,1,0:T(8,128)S(1)}, u32[]{:S(2)}, u32[]{:S(2)}) collective-permute-start(f32[4,32,256]{2,1,0:T(8,128)S(1)} %get-tuple-element.53), channel_id=1, source_target_pairs={{0,56},{8,0},{16,8},{24,16},{32,24},{40,32},{48,40},{56,48},{1,57}... | collective-permute-start | bytes 393224 | tf_op jit(solution)/shard_map/ppermute | solution.py:253
  28.6 8.1 %collective-permute-start.2 = (f32[8,32,256]{2,1,0:T(8,128)S(1)}, f32[8,32,256]{2,1,0:T(8,128)S(1)}, u32[]{:S(2)}, u32[]{:S(2)}) collective-permute-start(f32[8,32,256]{2,1,0:T(8,128)S(1)} %get-tuple-element.44), channel_id=1, source_target_pairs={{0,8},{8,16},{16,24},{24,32},{32,40},{40,48},{48,56},{56,0},{1,9},... | collective-permute-start | bytes 786440 | tf_op jit(solution)/shard_map/ppermute | solution.py:253
  28.7 8.0 %collective-permute-start.3 = (f32[8,32,256]{2,1,0:T(8,128)S(1)}, f32[8,32,256]{2,1,0:T(8,128)S(1)}, u32[]{:S(2)}, u32[]{:S(2)}) collective-permute-start(f32[8,32,256]{2,1,0:T(8,128)S(1)} %get-tuple-element.45), channel_id=1, source_target_pairs={{0,56},{8,0},{16,8},{24,16},{32,24},{40,32},{48,40},{56,48},{1,57}... | collective-permute-start | bytes 786440 | tf_op jit(solution)/shard_map/ppermute | solution.py:253
  31.8 10.6 %collective-permute-start.10 = (f32[8,32,256]{2,1,0:T(8,128)S(1)}, f32[8,32,256]{2,1,0:T(8,128)S(1)}, u32[]{:S(2)}, u32[]{:S(2)}) collective-permute-start(f32[8,32,256]{2,1,0:T(8,128)S(1)} %get-tuple-element.54), channel_id=1, source_target_pairs={{0,8},{8,16},{16,24},{24,32},{32,40},{40,48},{48,56},{56,0},{1,9},... | collective-permute-start | bytes 786440 | tf_op jit(solution)/shard_map/ppermute | solution.py:253
  31.9 10.5 %collective-permute-start.11 = (f32[8,32,256]{2,1,0:T(8,128)S(1)}, f32[8,32,256]{2,1,0:T(8,128)S(1)}, u32[]{:S(2)}, u32[]{:S(2)}) collective-permute-start(f32[8,32,256]{2,1,0:T(8,128)S(1)} %get-tuple-element.55), channel_id=1, source_target_pairs={{0,56},{8,0},{16,8},{24,16},{32,24},{40,32},{48,40},{56,48},{1,57}... | collective-permute-start | bytes 786440 | tf_op jit(solution)/shard_map/ppermute | solution.py:253
  36.7 11.3 %collective-permute-start.4 = (f32[8,32,256]{2,1,0:T(8,128)S(1)}, f32[8,32,256]{2,1,0:T(8,128)S(1)}, u32[]{:S(2)}, u32[]{:S(2)}) collective-permute-start(f32[8,32,256]{2,1,0:T(8,128)S(1)} %get-tuple-element.46), channel_id=1, source_target_pairs={{0,8},{8,16},{16,24},{24,32},{32,40},{40,48},{48,56},{56,0},{1,9},... | collective-permute-start | bytes 786440 | tf_op jit(solution)/shard_map/ppermute | solution.py:253
  36.8 11.2 %collective-permute-start.5 = (f32[8,32,256]{2,1,0:T(8,128)S(1)}, f32[8,32,256]{2,1,0:T(8,128)S(1)}, u32[]{:S(2)}, u32[]{:S(2)}) collective-permute-start(f32[8,32,256]{2,1,0:T(8,128)S(1)} %get-tuple-element.47), channel_id=1, source_target_pairs={{0,56},{8,0},{16,8},{24,16},{32,24},{40,32},{48,40},{56,48},{1,57}... | collective-permute-start | bytes 786440 | tf_op jit(solution)/shard_map/ppermute | solution.py:253
  42.5 11.2 %collective-permute-start.12 = (f32[8,32,256]{2,1,0:T(8,128)S(1)}, f32[8,32,256]{2,1,0:T(8,128)S(1)}, u32[]{:S(2)}, u32[]{:S(2)}) collective-permute-start(f32[8,32,256]{2,1,0:T(8,128)S(1)} %get-tuple-element.56), channel_id=1, source_target_pairs={{0,8},{8,16},{16,24},{24,32},{32,40},{40,48},{48,56},{56,0},{1,9},... | collective-permute-start | bytes 786440 | tf_op jit(solution)/shard_map/ppermute | solution.py:253
  42.6 11.1 %collective-permute-start.13 = (f32[8,32,256]{2,1,0:T(8,128)S(1)}, f32[8,32,256]{2,1,0:T(8,128)S(1)}, u32[]{:S(2)}, u32[]{:S(2)}) collective-permute-start(f32[8,32,256]{2,1,0:T(8,128)S(1)} %get-tuple-element.57), channel_id=1, source_target_pairs={{0,56},{8,0},{16,8},{24,16},{32,24},{40,32},{48,40},{56,48},{1,57}... | collective-permute-start | bytes 786440 | tf_op jit(solution)/shard_map/ppermute | solution.py:253
  48.1 11.2 %collective-permute-start.6 = (f32[8,32,256]{2,1,0:T(8,128)S(1)}, f32[8,32,256]{2,1,0:T(8,128)S(1)}, u32[]{:S(2)}, u32[]{:S(2)}) collective-permute-start(f32[8,32,256]{2,1,0:T(8,128)S(1)} %get-tuple-element.48), channel_id=1, source_target_pairs={{0,8},{8,16},{16,24},{24,32},{32,40},{40,48},{48,56},{56,0},{1,9},... | collective-permute-start | bytes 786440 | tf_op jit(solution)/shard_map/ppermute | solution.py:253
  48.2 11.1 %collective-permute-start.7 = (f32[8,32,256]{2,1,0:T(8,128)S(1)}, f32[8,32,256]{2,1,0:T(8,128)S(1)}, u32[]{:S(2)}, u32[]{:S(2)}) collective-permute-start(f32[8,32,256]{2,1,0:T(8,128)S(1)} %get-tuple-element.49), channel_id=1, source_target_pairs={{0,56},{8,0},{16,8},{24,16},{32,24},{40,32},{48,40},{56,48},{1,57}... | collective-permute-start | bytes 786440 | tf_op jit(solution)/shard_map/ppermute | solution.py:253
  53.7 11.2 %collective-permute-start.14 = (f32[8,32,256]{2,1,0:T(8,128)S(1)}, f32[8,32,256]{2,1,0:T(8,128)S(1)}, u32[]{:S(2)}, u32[]{:S(2)}) collective-permute-start(f32[8,32,256]{2,1,0:T(8,128)S(1)} %get-tuple-element.58), channel_id=1, source_target_pairs={{0,8},{8,16},{16,24},{24,32},{32,40},{40,48},{48,56},{56,0},{1,9},... | collective-permute-start | bytes 786440 | tf_op jit(solution)/shard_map/ppermute | solution.py:253
  53.8 11.1 %collective-permute-start.15 = (f32[8,32,256]{2,1,0:T(8,128)S(1)}, f32[8,32,256]{2,1,0:T(8,128)S(1)}, u32[]{:S(2)}, u32[]{:S(2)}) collective-permute-start(f32[8,32,256]{2,1,0:T(8,128)S(1)} %get-tuple-element.59), channel_id=1, source_target_pairs={{0,56},{8,0},{16,8},{24,16},{32,24},{40,32},{48,40},{56,48},{1,57}... | collective-permute-start | bytes 786440 | tf_op jit(solution)/shard_map/ppermute | solution.py:253
  71.7 5.6 %collective-permute-start.16 = (f32[64,256]{1,0:T(8,128)S(1)}, f32[64,256]{1,0:T(8,128)S(1)}, u32[]{:S(2)}, u32[]{:S(2)}) collective-permute-start(f32[64,256]{1,0:T(8,128)S(1)} %get-tuple-element.62), channel_id=1, source_target_pairs={{0,8},{8,16},{16,24},{24,32},{32,40},{40,48},{48,56},{56,0},{1,9},... | collective-permute-start | bytes 196616 | tf_op jit(solution)/shard_map/ppermute | solution.py:253
  71.8 5.5 %collective-permute-start.17 = (f32[64,256]{1,0:T(8,128)S(1)}, f32[64,256]{1,0:T(8,128)S(1)}, u32[]{:S(2)}, u32[]{:S(2)}) collective-permute-start(f32[64,256]{1,0:T(8,128)S(1)} %get-tuple-element.63), channel_id=1, source_target_pairs={{0,56},{8,0},{16,8},{24,16},{32,24},{40,32},{48,40},{56,48},{1,57}... | collective-permute-start | bytes 196616 | tf_op jit(solution)/shard_map/ppermute | solution.py:253
  77.4 8.6 %collective-permute-start.18 = (f32[128,256]{1,0:T(8,128)S(1)}, f32[128,256]{1,0:T(8,128)S(1)}, u32[]{:S(2)}, u32[]{:S(2)}) collective-permute-start(f32[128,256]{1,0:T(8,128)S(1)} %pad_maximum_fusion.8), channel_id=1, source_target_pairs={{0,8},{8,16},{16,24},{24,32},{32,40},{40,48},{48,56},{56,0},{1,9},... | collective-permute-start | bytes 393224 | tf_op jit(solution)/shard_map/ppermute | solution.py:253
  77.5 8.5 %collective-permute-start.19 = (f32[128,256]{1,0:T(8,128)S(1)}, f32[128,256]{1,0:T(8,128)S(1)}, u32[]{:S(2)}, u32[]{:S(2)}) collective-permute-start(f32[128,256]{1,0:T(8,128)S(1)} %pad_maximum_fusion.9), channel_id=1, source_target_pairs={{0,56},{8,0},{16,8},{24,16},{32,24},{40,32},{48,40},{56,48},{1,57}... | collective-permute-start | bytes 393224 | tf_op jit(solution)/shard_map/ppermute | solution.py:253
  80.3 15.2 %all-to-all-start.1 = ((f32[8,64,256]{2,1,0:T(8,128)}), f32[8,64,256]{2,1,0:T(8,128)S(1)}, u32[]{:S(2)}, u32[]{:S(2)}) async-start(f32[8,64,256]{2,1,0:T(8,128)} %pad_maximum_fusion), calls=%async_computation.1 | async-start | bytes 1048576 | tf_op jit(solution)/shard_map/all_to_all | solution.py:285
  86.0 6.3 %collective-permute-start.20 = (f32[128,256]{1,0:T(8,128)S(1)}, f32[128,256]{1,0:T(8,128)S(1)}, u32[]{:S(2)}, u32[]{:S(2)}) collective-permute-start(f32[128,256]{1,0:T(8,128)S(1)} %get-tuple-element.66), channel_id=1, source_target_pairs={{0,8},{8,16},{16,24},{24,32},{32,40},{40,48},{48,56},{56,0},{1,9},... | collective-permute-start | bytes 393224 | tf_op jit(solution)/shard_map/ppermute | solution.py:253
  86.1 6.2 %collective-permute-start.21 = (f32[128,256]{1,0:T(8,128)S(1)}, f32[128,256]{1,0:T(8,128)S(1)}, u32[]{:S(2)}, u32[]{:S(2)}) collective-permute-start(f32[128,256]{1,0:T(8,128)S(1)} %get-tuple-element.67), channel_id=1, source_target_pairs={{0,56},{8,0},{16,8},{24,16},{32,24},{40,32},{48,40},{56,48},{1,57}... | collective-permute-start | bytes 393224 | tf_op jit(solution)/shard_map/ppermute | solution.py:253
  95.5 5.4 %collective-permute-start.22 = (f32[128,256]{1,0:T(8,128)S(1)}, f32[128,256]{1,0:T(8,128)S(1)}, u32[]{:S(2)}, u32[]{:S(2)}) collective-permute-start(f32[128,256]{1,0:T(8,128)S(1)} %get-tuple-element.71), channel_id=1, source_target_pairs={{0,8},{8,16},{16,24},{24,32},{32,40},{40,48},{48,56},{56,0},{1,9},... | collective-permute-start | bytes 393224 | tf_op jit(solution)/shard_map/ppermute | solution.py:253
  95.6 5.3 %collective-permute-start.23 = (f32[128,256]{1,0:T(8,128)S(1)}, f32[128,256]{1,0:T(8,128)S(1)}, u32[]{:S(2)}, u32[]{:S(2)}) collective-permute-start(f32[128,256]{1,0:T(8,128)S(1)} %get-tuple-element.72), channel_id=1, source_target_pairs={{0,56},{8,0},{16,8},{24,16},{32,24},{40,32},{48,40},{56,48},{1,57}... | collective-permute-start | bytes 393224 | tf_op jit(solution)/shard_map/ppermute | solution.py:253
  101.4 5.1 %collective-permute-start.24 = (f32[256,128]{1,0:T(8,128)S(1)}, f32[256,128]{1,0:T(8,128)S(1)}, u32[]{:S(2)}, u32[]{:S(2)}) collective-permute-start(f32[256,128]{1,0:T(8,128)S(1)} %fusion.2), channel_id=1, source_target_pairs={{0,64},{64,128},{128,192},{192,0},{1,65},{65,129},{129,193},{193,1... | collective-permute-start | bytes 393224 | tf_op jit(solution)/shard_map/ppermute | solution.py:253
  102.7 6.7 %collective-permute-start.25 = (f32[256,128]{1,0:T(8,128)S(1)}, f32[256,128]{1,0:T(8,128)S(1)}, u32[]{:S(2)}, u32[]{:S(2)}) collective-permute-start(f32[256,128]{1,0:T(8,128)S(1)} %fusion.2), channel_id=1, source_target_pairs={{0,128},{64,192},{128,0},{192,64},{1,129},{65,193},{129,1},{193,65... | collective-permute-start | bytes 393224 | tf_op jit(solution)/shard_map/ppermute | solution.py:253
  105.1 4.9 %collective-permute-start.26 = (f32[256,128]{1,0:T(8,128)S(1)}, f32[256,128]{1,0:T(8,128)S(1)}, u32[]{:S(2)}, u32[]{:S(2)}) collective-permute-start(f32[256,128]{1,0:T(8,128)S(1)} %fusion.2), channel_id=1, source_target_pairs={{0,192},{64,0},{128,64},{192,128},{1,193},{65,1},{129,65},{193,129... | collective-permute-start | bytes 393224 | tf_op jit(solution)/shard_map/ppermute | solution.py:253
  (1 other events, 10.4 us)
